TPU v7x, 128 devices: a whole 4x4x4 slice. The times are simulated.
128 devices in a mesh: fsdp: 16 (over x, y), emb: 8 (over z, core).
Axes of the slice: x: 4, y: 4, z: 4, core: 2. Of those that a mesh axis runs over, the one named last changes fastest.
Arguments:
- pooled: bfloat16 [16384, 49152], P(('fsdp', 'emb')), may hold values from -6 to 6
- projection: bfloat16 [256, 96], replicated, may hold values from -0.375 to 0.375
- out_weight: bfloat16 [24576, 128], P('fsdp'), may hold values from -0.0390625 to 0.0390625
- cotangent: bfloat16 [16384, 128], P(('fsdp', 'emb')), may hold values from -6 to 6
- segments: int32 [16384, 256], P(None, ('fsdp', 'emb')), may hold values from 0 to 1023, as said below
Outputs:
- weight_grad: float32 [24576, 128], P(('fsdp', 'emb'))
- proj_grad: float32 [256, 96], replicated
- row_grad: float32 [131072, 192], P(('fsdp', 'emb'))
Inputs may be any that keep to these rules, and one draw needn't show every extreme that they name: `segments`: all features of one owner share that owner's count of distinct rows; every value of the owner lies below it, and the owner's largest value is that count minus one. Counts lie between 256 and 1024, and some owner's count is 1024.
All inputs are finite; a program needn't handle non-finite values.
Results may differ from a plain program's by a relative error of at most 0.008.
Values may be sent and summed in bfloat16 or wider, within the bound.
A program may use at most 192 MiB of HBM per device.

v0:
```python
import jax
import jax.numpy as jnp
from jax import lax
from jax.sharding import PartitionSpec as P

F = 256
E = 192
K = 96
UNIQUE_CAP = 1024


def on_device(pooled, projection, out_weight, cotangent, segments):
    scale = E ** (-0.5)
    batch = pooled.shape[0]
    feats = pooled.reshape(batch, F, E)
    mixed = jnp.einsum("bfe,fk->bke", feats, projection, preferred_element_type=jnp.float32).astype(
        jnp.bfloat16
    )
    gram = (
        jnp.einsum("bfe,bke->bfk", feats, mixed, preferred_element_type=jnp.float32) * scale
    ).astype(jnp.bfloat16)
    gram_flat = gram.reshape(batch, F * K)
    columns = gram_flat
    preact = jnp.dot(
        columns,
        lax.all_gather(out_weight, "fsdp", axis=0, tiled=True),
        preferred_element_type=jnp.float32,
    )
    sig = jax.nn.sigmoid(preact)
    slope = (cotangent.astype(jnp.float32) * sig * (1.0 + preact * (1.0 - sig))).astype(
        jnp.bfloat16
    )
    gram_grad = lax.dot_general(
        slope,
        lax.all_gather(out_weight, "fsdp", axis=0, tiled=True),
        (((1,), (1,)), ((), ())),
        preferred_element_type=jnp.float32,
    )
    gram_grad = gram_grad.astype(jnp.bfloat16).reshape(batch, F, K)
    mixed_grad = (
        jnp.einsum("bfk,bfe->bke", gram_grad, feats, preferred_element_type=jnp.float32) * scale
    ).astype(jnp.bfloat16)
    proj_term = jnp.einsum("bfe,bke->fk", feats, mixed_grad, preferred_element_type=jnp.float32)
    proj_grad = lax.psum(proj_term, ("fsdp", "emb"))
    feat_grad = jnp.einsum(
        "bfk,bke->bfe", gram_grad, mixed, preferred_element_type=jnp.float32
    ) * scale + jnp.einsum(
        "fk,bke->bfe", projection, mixed_grad, preferred_element_type=jnp.float32
    )
    feat_grad = feat_grad.astype(jnp.bfloat16).reshape(batch, F * E)
    columns = gram_flat
    weight_grad = lax.psum_scatter(
        lax.dot_general(
            columns, slope, (((0,), (0,)), ((), ())), preferred_element_type=jnp.float32
        ),
        ("fsdp", "emb"),
        scatter_dimension=0,
        tiled=True,
    )
    received = lax.all_to_all(feat_grad, ("fsdp", "emb"), split_axis=1, concat_axis=0, tiled=True)
    positions = received.reshape(-1, E)
    flat_seg = segments.reshape(-1)
    count_pos = positions.shape[0]
    pos_block = count_pos // 4
    seg_blocks = flat_seg.reshape(4, pos_block)
    data_blocks = positions.reshape(4, pos_block, E)
    tile_rows = UNIQUE_CAP // 4
    tile_limit = 4

    def one_tile(tile_index, totals):
        row_index = tile_index * tile_rows + jnp.arange(tile_rows, dtype=jnp.int32)

        def add_block(running, inputs):
            seg_piece, data_piece = inputs
            onehot = (row_index[:, None] == seg_piece[None, :]).astype(jnp.bfloat16)
            return (running + jnp.dot(onehot, data_piece, preferred_element_type=jnp.float32), None)

        tile_sum, _ = lax.scan(
            add_block, jnp.zeros((tile_rows, E), jnp.float32), (seg_blocks, data_blocks)
        )
        return lax.dynamic_update_slice_in_dim(totals, tile_sum, tile_index * tile_rows, 0)

    row_grad = lax.fori_loop(0, tile_limit, one_tile, jnp.zeros((UNIQUE_CAP, E), jnp.float32))
    return (weight_grad, proj_grad, row_grad)


def solution(mesh):
    placed = (
        P(("fsdp", "emb"), None),
        P(),
        P("fsdp", None),
        P(("fsdp", "emb"), None),
        P(None, ("fsdp", "emb")),
    )
    return jax.shard_map(
        on_device,
        mesh=mesh,
        in_specs=placed,
        out_specs=(P(("fsdp", "emb"), None), P(), P(("fsdp", "emb"), None)),
        check_vma=False,
    )
```

profile of v0, /device:TPU:0, one launch (start us, length us, event | category | flops | bytes accessed | tf_op | source)
XLA Modules:
  0.0 744.3 jit_solution(6117422545976532023)
XLA Ops:
  7.9 15.9 %copy.37 = bf16[128,49152]{0,1:T(8,128)(2,1)} copy(bf16[128,49152]{1,0:T(8,128)(2,1)} %param.9) | data formatting | bytes 25165824 | tf_op args[0]
  23.8 17.5 %copy.38 = bf16[128,256,192]{1,0,2:T(8,128)(2,1)} copy(bf16[128,256,192]{0,2,1:T(8,128)(2,1)} %bitcast.47) | data formatting | bytes 25165824 | tf_op jit(solution)/shard_map/reshape | solution.py:15
  41.3 18.1 %copy.40 = bf16[128,256,192]{1,2,0:T(8,128)(2,1)} copy(bf16[128,256,192]{0,2,1:T(8,128)(2,1)} %bitcast.48) | data formatting | bytes 25165824 | tf_op jit(solution)/shard_map/reshape | solution.py:15
  59.4 10.8 %convert_bitcast_fusion = bf16[128,96,192]{0,1,2:T(8,128)(2,1)} fusion(bf16[128,256,192]{1,0,2:T(8,128)(2,1)} %copy.38, bf16[256,96]{0,1:T(8,128)(2,1)S(1)} %copy-done), kind=kOutput, calls=%fused_computation.20 | convolution fusion | flops 1210318848 | bytes 17350656 | tf_op jit(solution)/shard_map/bfe,fk->bke/dot_general | solution.py:16
  70.2 8.4 %copy.50 = bf16[128,96,192]{1,2,0:T(8,128)(2,1)} copy(bf16[128,96,192]{0,1,2:T(8,128)(2,1)} %convert_bitcast_fusion) | data formatting | bytes 9437184 | tf_op jit(solution)/shard_map/convert_element_type | solution.py:16
  78.7 11.8 %fusion.15 = bf16[128,256,96]{1,2,0:T(8,128)(2,1)} fusion(bf16[128,96,192]{1,2,0:T(8,128)(2,1)} %copy.50, bf16[128,256,192]{1,2,0:T(8,128)(2,1)} %copy.40), kind=kOutput, calls=%fused_computation.17 | convolution fusion | flops 1214251008 | bytes 23592960 | tf_op jit(solution)/shard_map/bfe,bke->bfk/dot_general | solution.py:20
  90.4 9.6 %copy.41 = bf16[128,256,96]{0,2,1:T(8,128)(2,1)} copy(bf16[128,256,96]{1,2,0:T(8,128)(2,1)} %fusion.15) | data formatting | bytes 12582912 | tf_op jit(solution)/shard_map/convert_element_type | solution.py:21
  100.0 6.6 fusion.31
  111.1 8.7 %copy.42 = bf16[128,24576]{0,1:T(8,128)(2,1)} copy(bf16[128,24576]{1,0:T(8,128)(2,1)} %convolution_convert_fusion) | data formatting | bytes 12582912 | tf_op jit(solution)/shard_map/convert_element_type | solution.py:39
  119.8 9.7 %copy.43 = bf16[128,256,96]{1,2,0:T(8,128)(2,1)} copy(bf16[128,256,96]{0,2,1:T(8,128)(2,1)} %bitcast.52) | data formatting | bytes 12582912 | tf_op jit(solution)/shard_map/reshape | solution.py:39
  129.5 16.9 %fusion.32 = f32[128,96,192]{2,1,0:T(8,128)} fusion(bf16[128,256,96]{1,2,0:T(8,128)(2,1)} %copy.43, bf16[128,256,192]{1,2,0:T(8,128)(2,1)} %copy.40), kind=kOutput, calls=%fused_computation.34 | convolution fusion | flops 1207959552 | bytes 28311552 | tf_op jit(solution)/shard_map/bfk,bfe->bke/dot_general | solution.py:41
  146.4 11.7 %copy.45 = f32[128,96,192]{0,2,1:T(8,128)} copy(f32[128,96,192]{2,1,0:T(8,128)} %fusion.32) | data formatting | bytes 18874368 | tf_op jit(solution)/shard_map/bfk,bfe->bke/dot_general | solution.py:41
  158.1 7.3 multiply_convert_fusion.1
  165.4 9.3 %copy.51 = bf16[128,96,192]{1,2,0:T(8,128)(2,1)} copy(bf16[128,96,192]{0,2,1:T(8,128)(2,1)} %multiply_convert_fusion.1) | data formatting | bytes 9437184 | tf_op jit(solution)/shard_map/convert_element_type | solution.py:42
  174.7 14.7 %fusion.24 = f32[128,192,256]{2,1,0:T(8,128)} fusion(bf16[128,96,192]{1,2,0:T(8,128)(2,1)} %copy.51, bf16[256,96]{0,1:T(8,128)(2,1)S(1)} %copy-done), kind=kOutput, calls=%fused_computation.26 | convolution fusion | flops 1207959552 | bytes 29933568 | tf_op jit(solution)/shard_map/fk,bke->bfe/dot_general | solution.py:47
  189.4 16.3 %fusion.14 = bf16[128,256,192]{1,2,0:T(8,128)(2,1)} fusion(f32[128,192,256]{2,1,0:T(8,128)} %fusion.24, bf16[128,96,192]{1,2,0:T(8,128)(2,1)} %copy.50, bf16[128,256,96]{1,2,0:T(8,128)(2,1)S(1)} %bitcast.46), kind=kOutput, calls=%fused_computation.14 | convolution fusion | flops 1226833920 | bytes 48758784 | tf_op jit(solution)/shard_map/bfk,bke->bfe/dot_general | solution.py:45
  205.7 18.1 %copy.52 = bf16[128,256,192]{0,2,1:T(8,128)(2,1)} copy(bf16[128,256,192]{1,2,0:T(8,128)(2,1)} %fusion.14) | data formatting | bytes 25165824 | tf_op jit(solution)/shard_map/convert_element_type | solution.py:50
  223.8 12.1 %all-to-all-start = ((bf16[128,128,384]{0,2,1:T(8,128)(2,1)}), bf16[128,128,384]{0,2,1:T(8,128)(2,1)}, u32[]{:S(2)}, u32[]{:S(2)}) async-start(bf16[128,128,384]{0,2,1:T(8,128)(2,1)} %bitcast.51), calls=%async_computation.1 | async-start | bytes 25165824 | tf_op jit(solution)/shard_map/all_to_all | solution.py:60
  236.0 5.2 copy.48
  241.1 11.0 %reshape_reshape.6 = s32[4,8192]{1,0:T(4,128)S(1)} reshape(s32[16384,2]{1,0:T(8,128)} %copy.48) | data formatting | bytes 262144 | tf_op jit(solution)/shard_map/reshape;reshape | solution.py:65
  252.1 9.9 %fusion.18 = f32[256,96]{0,1:T(8,128)} fusion(bf16[128,256,192]{1,0,2:T(8,128)(2,1)} %copy.38, bf16[128,96,192]{0,2,1:T(8,128)(2,1)} %multiply_convert_fusion.1), kind=kOutput, calls=%fused_computation.21 | convolution fusion | flops 1207959552 | bytes 17399808 | tf_op jit(solution)/shard_map/bfe,bke->fk/dot_general | solution.py:43
  262.2 9.2 %fusion.21 = f32[24576,128]{1,0:T(8,128)} fusion(bf16[128,24576]{0,1:T(8,128)(2,1)} %bitcast.50, f32[128,128]{1,0:T(8,128)S(1)} %fusion.31, bf16[128,128]{1,0:T(8,128)(2,1)S(1)} %copy-done.5), kind=kOutput, calls=%fused_computation.23 | convolution fusion | flops 805470208 | bytes 18972672 | tf_op jit(solution)/shard_map/dot_general | solution.py:53
  271.4 130.8 %all-to-all-done = bf16[128,128,384]{0,2,1:T(8,128)(2,1)} async-done(((bf16[128,128,384]{0,2,1:T(8,128)(2,1)}), bf16[128,128,384]{0,2,1:T(8,128)(2,1)}, u32[]{:S(2)}, u32[]{:S(2)}) %all-to-all-start) | async-done | bytes 12582944 | tf_op jit(solution)/shard_map/all_to_all | solution.py:60
  402.2 16.6 %copy.53 = bf16[128,128,384]{2,1,0:T(8,128)(2,1)} copy(bf16[128,128,384]{1,2,0:T(8,128)(2,1)} %bitcast.10) | data formatting | bytes 25165824 | tf_op jit(solution)/shard_map/all_to_all | solution.py:60
  418.9 24.4 %reshape_reshape.7 = bf16[4,8192,192]{2,1,0:T(8,128)(2,1)} reshape(bf16[128,128,384]{2,1,0:T(8,128)(2,1)} %copy.53) | data formatting | bytes 25165824 | tf_op jit(solution)/shard_map/reshape;reshape | solution.py:66
  443.4 73.5 %while.37 = (s32[]{:T(128)}, f32[1024,192]{0,1:T(8,128)S(1)}, s32[4,8192]{1,0:T(4,128)S(1)}, bf16[4,8192,192]{2,1,0:T(8,128)(2,1)}, s32[]{:T(128)}, /*index=5*/s...) while((s32[]{:T(128)}, f32[1024,192]{0,1:T(8,128)S(1)}, s32[4,8192]{1,0:T(4,128)S(1)}, ...), condition=%wide.region_5.6_spmd, body=%wide.region_2.5_spmd.sunk | while | flops 807502080 | bytes 5081418 | solution.py:83
  443.4 18.3 %while.38 = (s32[]{:T(128)}, f32[256,192]{0,1:T(8,128)S(1)}, s32[4,8192]{1,0:T(4,128)S(1)}, bf16[4,8192,192]{2,1,0:T(8,128)(2,1)}, s32[]{:T(128)}, /*index=5*/s32[]{:T(128)}, s32[]{:T(128)}) while((s32[]{:T(128)}, f32[256,192]{0,1:T(8,128)S(1)}, s32[4,8192]{1,0:T(4,128)S(1)}, bf16[4,8192,192]{2,1,0:T(8,128)(2,1)}, s32[]{:T(128)}, ...), condition=%wide.region_4.4_spmd.clone, body=%wide.region_3.3_spmd.clone.sunk | while | flops 807502080 | bytes 4687979 | solution.py:78
  448.0 4.5 fusion.51
  461.8 18.3 %while.38 = (s32[]{:T(128)}, f32[256,192]{0,1:T(8,128)S(1)}, s32[4,8192]{1,0:T(4,128)S(1)}, bf16[4,8192,192]{2,1,0:T(8,128)(2,1)}, s32[]{:T(128)}, /*index=5*/s32[]{:T(128)}, s32[]{:T(128)}) while((s32[]{:T(128)}, f32[256,192]{0,1:T(8,128)S(1)}, s32[4,8192]{1,0:T(4,128)S(1)}, bf16[4,8192,192]{2,1,0:T(8,128)(2,1)}, s32[]{:T(128)}, ...), condition=%wide.region_4.4_spmd.clone, body=%wide.region_3.3_spmd.clone.sunk | while | flops 807502080 | bytes 4687979 | solution.py:78
  480.2 18.3 %while.38 = (s32[]{:T(128)}, f32[256,192]{0,1:T(8,128)S(1)}, s32[4,8192]{1,0:T(4,128)S(1)}, bf16[4,8192,192]{2,1,0:T(8,128)(2,1)}, s32[]{:T(128)}, /*index=5*/s32[]{:T(128)}, s32[]{:T(128)}) while((s32[]{:T(128)}, f32[256,192]{0,1:T(8,128)S(1)}, s32[4,8192]{1,0:T(4,128)S(1)}, bf16[4,8192,192]{2,1,0:T(8,128)(2,1)}, s32[]{:T(128)}, ...), condition=%wide.region_4.4_spmd.clone, body=%wide.region_3.3_spmd.clone.sunk | while | flops 807502080 | bytes 4687979 | solution.py:78
  498.6 18.3 %while.38 = (s32[]{:T(128)}, f32[256,192]{0,1:T(8,128)S(1)}, s32[4,8192]{1,0:T(4,128)S(1)}, bf16[4,8192,192]{2,1,0:T(8,128)(2,1)}, s32[]{:T(128)}, /*index=5*/s32[]{:T(128)}, s32[]{:T(128)}) while((s32[]{:T(128)}, f32[256,192]{0,1:T(8,128)S(1)}, s32[4,8192]{1,0:T(4,128)S(1)}, bf16[4,8192,192]{2,1,0:T(8,128)(2,1)}, s32[]{:T(128)}, ...), condition=%wide.region_4.4_spmd.clone, body=%wide.region_3.3_spmd.clone.sunk | while | flops 807502080 | bytes 4687979 | solution.py:78
  517.0 219.0 %reduce-scatter.2.cloned.1.call-done = f32[192,128]{1,0:T(8,128)} async-done(((f32[24576,128]{1,0:T(8,128)}), f32[192,128]{1,0:T(8,128)}) %reduce-scatter.2.cloned.1.call-update) | async-done | bytes 98320 | tf_op jit(solution)/shard_map/reduce_scatter | solution.py:52
  (83 shorter events, 75.3 us)
Async XLA Ops:
  7.2 52.3 %copy-start = (bf16[256,96]{0,1:T(8,128)(2,1)S(1)}, bf16[256,96]{0,1:T(8,128)(2,1)}, u32[]{:S(2)}) copy-start(bf16[256,96]{0,1:T(8,128)(2,1)} %param.10) | copy-start | bytes 147460
  7.2 92.9 %all-gather.2.cloned.1.call-start = ((), (), s32[]{:S(2)}) async-start(), calls=%async_computation.2 | async-start | bytes 6684672 | tf_op jit(solution)/shard_map/all_gather | solution.py:26
  100.0 6.6 copy-start.2
  100.0 6.6 copy-start.5
  165.4 24.0 %slice-start = ((s8[6291456]{0:T(1024)(128)(4,1)}), s8[2097152]{0:T(1024)(128)(4,1)S(1)}, s32[]{:S(2)}) async-start(s8[6291456]{0:T(1024)(128)(4,1)} %bitcast.45), calls=%async_computation.5 | async-start | bytes 4194304
  174.7 14.7 %slice-start.1 = ((s8[6291456]{0:T(1024)(128)(4,1)}), s8[4194304]{0:T(1024)(128)(4,1)S(1)}, s32[]{:S(2)}) async-start(s8[6291456]{0:T(1024)(128)(4,1)} %bitcast.45), calls=%async_computation.6 | async-start | bytes 8388608
  223.8 12.1 %copy-start.4 = (s32[16384,2]{0,1:T(2,128)S(1)}, s32[16384,2]{0,1:T(2,128)}, u32[]{:S(2)}) copy-start(s32[16384,2]{0,1:T(2,128)} %param.13) | copy-start | bytes 393220
  223.8 178.4 %all-to-all-start = ((bf16[128,128,384]{0,2,1:T(8,128)(2,1)}), bf16[128,128,384]{0,2,1:T(8,128)(2,1)}, u32[]{:S(2)}, u32[]{:S(2)}) async-start(bf16[128,128,384]{0,2,1:T(8,128)(2,1)} %bitcast.51), calls=%async_computation.1 | async-start | bytes 25165824 | tf_op jit(solution)/shard_map/all_to_all | solution.py:60
  235.9 281.0 %all-reduce.2.cloned.1.call-start = ((), (), s32[]{:S(2)}) async-start(), calls=%async_computation.4 | async-start | bytes 196608 | tf_op jit(solution)/shard_map/psum | solution.py:44
  262.0 474.0 %reduce-scatter.2.cloned.1.call-start = ((), (), s32[]{:S(2)}) async-start(), calls=%async_computation.3 | async-start | bytes 12681216 | tf_op jit(solution)/shard_map/reduce_scatter | solution.py:52
  516.9 220.6 %copy-start.3 = (f32[1024,192]{0,1:T(8,128)}, f32[1024,192]{0,1:T(8,128)S(1)}, u32[]{:S(2)}) copy-start(f32[1024,192]{0,1:T(8,128)S(1)} %get-tuple-element.271) | copy-start | bytes 2359300
  516.9 220.6 %copy-start.1 = (bf16[256,96]{0,1:T(8,128)(2,1)S(1)}, bf16[256,96]{0,1:T(8,128)(2,1)}, u32[]{:S(2)}) copy-start(bf16[256,96]{0,1:T(8,128)(2,1)} %param.10) | copy-start | bytes 147460
Sparse Core Ops, SparseCore 0:
  10.2 63.6 all-gather.1
  262.1 247.5 all-reduce.1
  516.0 219.8 reduce-scatter.1
where the time goes:
time: 757 us; the launch traced here: 744 us
  waiting for transfers between devices  351 us (46%)
  local copies, waits for them, and re-layouts  187 us (25%)
  matrix products  173 us (23%)
  between operations  14.1 us (2%)
  starting transfers between devices  12.4 us (2%)
    reduce_scatter x1, waiting for transfers between devices, on_device(): lax.psum_scatter(lax.dot_general(columns, slope, (((0,), (0,)), ((), ()))...  219 us
    all_to_all x1, waiting for transfers between devices, on_device(): lax.all_to_all(feat_grad, ('fsdp', 'emb'), split_axis=1, concat_axis=0, t...  131 us
    dot_general x16, matrix products, add_block(): jnp.dot(onehot, data_piece, preferred_element_type=jnp.float32)  72.1 us
    reshape x2, local copies, waits for them, and re-layouts, on_device(): feats = pooled.reshape(batch, F, E)  35.6 us
    another operation x1, local copies, waits for them, and re-layouts, on_device(): data_blocks = positions.reshape(4, pos_block, E)  24.4 us
    unnamed x19, local copies, waits for them, and re-layouts  22.6 us
    convert_element_type x1, local copies, waits for them, and re-layouts, on_device(): feat_grad = feat_grad.astype(jnp.bfloat16).reshape(batch, F * E)  18.1 us
    dot_general x1, matrix products, on_device(): jnp.einsum('bfk,bfe->bke', gram_grad, feats, preferred_element_type=jnp.f...  16.9 us
  transfers between devices with their start and end apart: 4, of which 2 were waited for; matrix products, arithmetic and copies ran while one was open for 32% of the time, Pallas kernels for 0%

commit v1 on v0

v1 whole, which is shorter than its diff:
```python
import functools

import jax
import jax.numpy as jnp
from jax import lax
from jax.experimental import pallas as pl
from jax.experimental.pallas import tpu as pltpu
from jax.sharding import PartitionSpec as P

F = 256
E = 192
K = 96
H = 128
UNIQUE_CAP = 1024
PAIRS = F // 2
ROWS = 16
SCALE = E ** (-0.5)
BF = jnp.bfloat16
F32 = jnp.float32
VMEM_LIMIT = 60 * 1024 * 1024
NT = (((1,), (1,)), ((), ()))
TN = (((0,), (0,)), ((), ()))


def interleave(even, odd):
    width = even.shape[-1]
    both = jnp.concatenate([even.reshape(16, 8, width), odd.reshape(16, 8, width)], axis=1)
    return both.reshape(F, width)


def lower_half(rows):
    return lax.broadcasted_iota(jnp.int32, (rows, 128), 1) < 64


def front_kernel(x_ref, projt_ref, xs_ref, mixed_ref, gram_ref, wide, turned):
    def spread(step, carry):
        for inner in range(8):
            tile = step * 8 + inner
            wide[pl.ds(pl.multiple_of(tile * ROWS, ROWS), ROWS), :] = x_ref[
                :, pl.ds(pl.multiple_of(tile * 128, 128), 128)
            ].astype(F32)
        return carry

    lax.fori_loop(0, F * E // 1024, spread, 0)
    low = lower_half(PAIRS)

    def sample(b):
        a0 = wide[pl.ds(b, PAIRS, stride=3 * ROWS), :]
        a1 = wide[pl.ds(b + ROWS, PAIRS, stride=3 * ROWS), :]
        a2 = wide[pl.ds(b + 2 * ROWS, PAIRS, stride=3 * ROWS), :]
        r1 = pltpu.roll(a1, 64, 1)
        r2 = pltpu.roll(a2, 64, 1)
        even = jnp.concatenate([a0, jnp.where(low, a1, 0.0)], axis=1)
        odd = jnp.concatenate([jnp.where(low, r1, r2), jnp.where(low, r2, 0.0)], axis=1)
        xb = interleave(even, odd).astype(BF)
        xs_ref[b] = xb
        mixed = jnp.dot(projt_ref[...], xb, preferred_element_type=F32).astype(BF)
        mixed_ref[b] = mixed
        gram = lax.dot_general(mixed, xb, NT, preferred_element_type=F32) * SCALE
        turned[0, pl.ds(b, K, stride=ROWS), :] = gram[:, :128]
        turned[1, pl.ds(b, K, stride=ROWS), :] = gram[:, 128:]

    def samples(step, carry):
        for inner in range(4):
            sample(step * 4 + inner)
        return carry

    lax.fori_loop(0, ROWS // 4, samples, 0)
    for half in range(2):
        gram_ref[:, :, half * 128 : half * 128 + 128] = (
            turned[half].reshape(K, ROWS, 128).astype(BF)
        )


def front(x, projt):
    batch = x.shape[0]
    return pl.pallas_call(
        front_kernel,
        grid=(batch // ROWS,),
        in_specs=[
            pl.BlockSpec((ROWS, F * E), lambda i: (i, 0)),
            pl.BlockSpec((K, F), lambda i: (0, 0)),
        ],
        out_specs=[
            pl.BlockSpec((ROWS, F, 256), lambda i: (i, 0, 0)),
            pl.BlockSpec((ROWS, K, 256), lambda i: (i, 0, 0)),
            pl.BlockSpec((K, ROWS, F), lambda i: (0, i, 0)),
        ],
        out_shape=[
            jax.ShapeDtypeStruct((batch, F, 256), BF),
            jax.ShapeDtypeStruct((batch, K, 256), BF),
            jax.ShapeDtypeStruct((K, batch, F), BF),
        ],
        scratch_shapes=[
            pltpu.VMEM((F * E // 128 * ROWS, 128), F32),
            pltpu.VMEM((2, K * ROWS, 128), F32),
        ],
        compiler_params=pltpu.CompilerParams(vmem_limit_bytes=VMEM_LIMIT),
        cost_estimate=pl.CostEstimate(
            flops=4 * batch * F * E * K, bytes_accessed=42_000_000, transcendentals=0
        ),
        name="front",
    )(x, projt)


def middle_kernel(gram_ref, w_ref, cot_ref, wgrad_ref, gg_ref, turned):
    batch = gram_ref.shape[1]

    def weight(k):
        return w_ref[:, k].reshape(F, H)

    def product(step, total):
        for inner in range(8):
            k = step * 8 + inner
            total = total + jnp.dot(gram_ref[k], weight(k), preferred_element_type=F32)
        return total

    preact = lax.fori_loop(0, K // 8, product, jnp.zeros((batch, H), F32))
    sig = jax.nn.sigmoid(preact)
    slope = (cot_ref[...].astype(F32) * sig * (1.0 + preact * (1.0 - sig))).astype(BF)

    def gradients(step, carry):
        for inner in range(4):
            k = step * 4 + inner
            wgrad = lax.dot_general(gram_ref[k], slope, TN, preferred_element_type=F32)
            for block in range(16):
                for parity in range(2):
                    at = block * 16 + parity * 8
                    wgrad_ref[pl.ds(block * 8 * 2 * K + parity * K + k, 8, stride=2 * K), :] = wgrad[
                        at : at + 8
                    ]
            gg = lax.dot_general(slope, weight(k), NT, preferred_element_type=F32)
            turned[0, pl.ds(k, batch, stride=K), :] = gg[:, :128]
            turned[1, pl.ds(k, batch, stride=K), :] = gg[:, 128:]
        return carry

    lax.fori_loop(0, K // 4, gradients, 0)

    def pack(b, carry):
        at = pl.ds(pl.multiple_of(b * K, K), K)
        gg_ref[b] = jnp.concatenate([turned[0, at, :], turned[1, at, :]], axis=1).astype(BF)
        return carry

    lax.fori_loop(0, batch, pack, 0)


def middle(gram, w, cot):
    batch = gram.shape[1]
    whole = pl.BlockSpec(memory_space=pltpu.VMEM)
    return pl.pallas_call(
        middle_kernel,
        in_specs=[whole] * 3,
        out_specs=[whole] * 2,
        out_shape=[
            jax.ShapeDtypeStruct((F * K, H), F32),
            jax.ShapeDtypeStruct((batch, K, F), BF),
        ],
        scratch_shapes=[pltpu.VMEM((2, batch * K, 128), F32)],
        compiler_params=pltpu.CompilerParams(vmem_limit_bytes=VMEM_LIMIT),
        cost_estimate=pl.CostEstimate(
            flops=6 * batch * F * K * H, bytes_accessed=33_000_000, transcendentals=batch * H
        ),
        name="middle",
    )(gram, w, cot)


def back_kernel(xs_ref, mixed_ref, gg_ref, projt_ref, fg_ref, pg_ref, wide):
    low = lower_half(PAIRS)

    @pl.when(pl.program_id(0) == 0)
    def _():
        pg_ref[...] = jnp.zeros_like(pg_ref)

    def sample(b):
        xb = xs_ref[b]
        gg = gg_ref[b]
        mg = jnp.dot(gg, xb, preferred_element_type=F32).astype(BF)
        pg = lax.dot_general(mg, xb, NT, preferred_element_type=F32)
        left = jnp.concatenate([gg, projt_ref[...]], axis=0)
        right = jnp.concatenate([mixed_ref[b], mg], axis=0)
        fg = lax.dot_general(left, right, TN, preferred_element_type=F32) * SCALE
        fg = fg.reshape(16, 2, 8, 256)
        even = fg[:, 0].reshape(PAIRS, 256)
        odd = fg[:, 1].reshape(PAIRS, 256)
        r0 = pltpu.roll(odd[:, :128], 64, 1)
        r1 = pltpu.roll(odd[:, 128:], 64, 1)
        wide[pl.ds(b, PAIRS, stride=3 * ROWS), :] = even[:, :128]
        wide[pl.ds(b + ROWS, PAIRS, stride=3 * ROWS), :] = jnp.where(low, even[:, 128:], r0)
        wide[pl.ds(b + 2 * ROWS, PAIRS, stride=3 * ROWS), :] = jnp.where(low, r0, r1)
        return pg

    def samples(step, total):
        for inner in range(4):
            total = total + sample(step * 4 + inner)
        return total

    pg_ref[...] += lax.fori_loop(0, ROWS // 4, samples, jnp.zeros((K, F), F32)) * SCALE

    def pack(p, carry):
        for tile in range(3):
            at = pl.ds(pl.multiple_of(p * 3 * ROWS + tile * ROWS, ROWS), ROWS)
            fg_ref[p, :, tile * 128 : tile * 128 + 128] = wide[at, :].astype(BF)
        return carry

    lax.fori_loop(0, PAIRS, pack, 0, unroll=4)


def back(xs, mixed, gg, projt):
    batch = xs.shape[0]
    return pl.pallas_call(
        back_kernel,
        grid=(batch // ROWS,),
        in_specs=[
            pl.BlockSpec((ROWS, F, 256), lambda i: (i, 0, 0)),
            pl.BlockSpec((ROWS, K, 256), lambda i: (i, 0, 0)),
            pl.BlockSpec((ROWS, K, F), lambda i: (i, 0, 0)),
            pl.BlockSpec((K, F), lambda i: (0, 0)),
        ],
        out_specs=[
            pl.BlockSpec((PAIRS, ROWS, 2 * E), lambda i: (0, i, 0)),
            pl.BlockSpec((K, F), lambda i: (0, 0)),
        ],
        out_shape=[
            jax.ShapeDtypeStruct((PAIRS, batch, 2 * E), BF),
            jax.ShapeDtypeStruct((K, F), F32),
        ],
        scratch_shapes=[pltpu.VMEM((F * E // 128 * ROWS, 128), F32)],
        compiler_params=pltpu.CompilerParams(vmem_limit_bytes=VMEM_LIMIT),
        cost_estimate=pl.CostEstimate(
            flops=8 * batch * F * E * K, bytes_accessed=42_000_000, transcendentals=0
        ),
        name="back",
    )(xs, mixed, gg, projt)


CHUNK = 2048
SLOT_BLOCK = 256


def rows_kernel(data_ref, seg_ref, out_ref, even, odd):
    step = pl.program_id(0)

    @pl.when(step == 0)
    def _():
        even[...] = jnp.zeros_like(even)
        odd[...] = jnp.zeros_like(odd)

    slot = lax.broadcasted_iota(jnp.int32, (SLOT_BLOCK, CHUNK), 0)
    for block in range(UNIQUE_CAP // SLOT_BLOCK):
        at = pl.ds(block * SLOT_BLOCK, SLOT_BLOCK)
        for parity, total in ((0, even), (1, odd)):
            seg = seg_ref[parity : parity + 1, :] - block * SLOT_BLOCK
            hot = jnp.where(slot == seg, 1.0, 0.0).astype(BF)
            total[at, :] += jnp.dot(
                hot, data_ref[:, parity * 128 : parity * 128 + 256], preferred_element_type=F32
            )

    @pl.when(step == pl.num_programs(0) - 1)
    def _():
        low = lower_half(UNIQUE_CAP)
        r0 = pltpu.roll(odd[:, :128], 64, 1)
        r1 = pltpu.roll(odd[:, 128:], 64, 1)
        out_ref[:, :128] = even[:, :128] + jnp.where(low, r0, r1)
        out_ref[:, 128:] = (even[:, 128:] + r1)[:, :64]


def row_sums(data, seg):
    count = data.shape[0]
    return pl.pallas_call(
        rows_kernel,
        grid=(count // CHUNK,),
        in_specs=[
            pl.BlockSpec((CHUNK, 2 * E), lambda i: (i, 0)),
            pl.BlockSpec((2, CHUNK), lambda i: (0, i)),
        ],
        out_specs=pl.BlockSpec((UNIQUE_CAP, E), lambda i: (0, 0)),
        out_shape=jax.ShapeDtypeStruct((UNIQUE_CAP, E), F32),
        scratch_shapes=[pltpu.VMEM((UNIQUE_CAP, 256), F32)] * 2,
        compiler_params=pltpu.CompilerParams(vmem_limit_bytes=VMEM_LIMIT),
        cost_estimate=pl.CostEstimate(
            flops=4 * UNIQUE_CAP * count * 256, bytes_accessed=14_000_000, transcendentals=0
        ),
        name="row_sums",
    )(data, seg)


def turn_features(a):
    rest = a.shape[1:]
    return a.reshape((-1, 8, 2) + rest).swapaxes(1, 2).reshape(a.shape)


def unturn_features(a):
    rest = a.shape[1:]
    return a.reshape((-1, 2, 8) + rest).swapaxes(1, 2).reshape(a.shape)


def on_device(pooled, projection, out_weight, cotangent, segments):
    batch = pooled.shape[0]
    own = turn_features(out_weight.reshape(-1, K, H)).swapaxes(0, 1)
    weight = lax.all_gather(own, "fsdp", axis=0)
    projt = turn_features(projection).T
    xs, mixed, gram = front(pooled, projt)
    wgrad, gg = middle(gram, weight, cotangent)
    fg, pg = back(xs, mixed, gg, projt)
    received = lax.all_to_all(fg, ("fsdp", "emb"), split_axis=0, concat_axis=0, tiled=True)
    proj_grad = lax.psum(unturn_features(pg.T), ("fsdp", "emb"))
    weight_grad = lax.psum_scatter(wgrad, ("fsdp", "emb"), scatter_dimension=0, tiled=True)
    row_grad = row_sums(received.reshape(-1, 2 * E), segments.T)
    return (weight_grad, proj_grad, row_grad)


def solution(mesh):
    placed = (
        P(("fsdp", "emb"), None),
        P(),
        P("fsdp", None),
        P(("fsdp", "emb"), None),
        P(None, ("fsdp", "emb")),
    )
    return jax.shard_map(
        on_device,
        mesh=mesh,
        in_specs=placed,
        out_specs=(P(("fsdp", "emb"), None), P(), P(("fsdp", "emb"), None)),
        check_vma=False,
    )
```

time: 757 us -> 668 us (0.88); the launches traced: 744 us -> 668 us
  local copies, waits for them, and re-layouts: 187 us -> 9.43 us
  matrix products: 173 us -> 0 us
  waiting for transfers between devices: 351 us -> 499 us
  Pallas kernels: 0 us -> 137 us
    psum x1, waiting for transfers between devices: 0.02 us -> 267 us  [on_device(): proj_grad = lax.psum(unturn_features(pg.T), ('fsdp', 'emb'))]
    dot_general x25 -> x0, matrix products: 173 us -> none  [the longest x16 72.1 us: add_block(): jnp.dot(onehot, data_piece, preferred_element_type=jnp.float32)]
    pallas_call x0 -> x4, Pallas kernels: none -> 137 us  [the longest x1 44.9 us: middle(): pl.pallas_call(middle_kernel, in_specs=[whole] * 3, out_specs=[whole] * 2...]
    all_to_all x1, waiting for transfers between devices: 131 us -> 0.01 us  [on_device(): lax.all_to_all(fg, ('fsdp', 'emb'), split_axis=0, concat_axis=0, tiled=True)]
    convert_element_type x5 -> x0, local copies, waits for them, and re-layouts: 54.2 us -> none  [the longest x1 18.1 us: on_device(): feat_grad = feat_grad.astype(jnp.bfloat16).reshape(batch, F * E)]
    reshape x3 -> x1, local copies, waits for them, and re-layouts: 45.4 us -> 0.73 us  [turn_features(): return a.reshape((-1, 8, 2) + rest).swapaxes(1, 2).reshape(a.shape)]
    another operation x2 -> x1, local copies, waits for them, and re-layouts: 35.3 us -> 2 us  [turn_features(): return a.reshape((-1, 8, 2) + rest).swapaxes(1, 2).reshape(a.shape)]
    all_gather x1, waiting for transfers between devices: 0.01 us -> 31.5 us  [on_device(): weight = lax.all_gather(own, 'fsdp', axis=0)]
  transfers between devices with their start and end apart: 4 -> 4, of which waited for: 2 -> 3; matrix products, arithmetic and copies ran while one was open for 32% -> 1% of each run, Pallas kernels for 0% -> 8%
where the time goes in v1:
time: 668 us
  waiting for transfers between devices  499 us (75%)
  Pallas kernels  137 us (21%)
  between operations  13.8 us (2%)
  local copies, waits for them, and re-layouts  9.43 us (1%)
  starting transfers between devices  8.98 us (1%)
    psum x1, waiting for transfers between devices, on_device(): proj_grad = lax.psum(unturn_features(pg.T), ('fsdp', 'emb'))  267 us
    reduce_scatter x1, waiting for transfers between devices, on_device(): lax.psum_scatter(wgrad, ('fsdp', 'emb'), scatter_dimension=0, tiled=True)  200 us
    pallas_call x1, Pallas kernels, middle(): pl.pallas_call(middle_kernel, in_specs=[whole] * 3, out_specs=[whole] * 2...  44.9 us
    pallas_call x1, Pallas kernels, back(): pl.pallas_call(back_kernel, grid=(batch // ROWS,), in_specs=[pl.BlockSpec...  38 us
    pallas_call x1, Pallas kernels, front(): pl.pallas_call(front_kernel, grid=(batch // ROWS,), in_specs=[pl.BlockSpe...  31.9 us
    all_gather x1, waiting for transfers between devices, on_device(): weight = lax.all_gather(own, 'fsdp', axis=0)  31.5 us
    pallas_call x1, Pallas kernels, row_sums(): pl.pallas_call(rows_kernel, grid=(count // CHUNK,), in_specs=[pl.BlockSpe...  21.7 us
  transfers between devices with their start and end apart: 4, of which 3 were waited for; matrix products, arithmetic and copies ran while one was open for 1% of the time, Pallas kernels for 8%

profile of v1, /device:TPU:0, one launch (start us, length us, event | category | flops | bytes accessed | tf_op | source)
XLA Modules:
  0.0 667.6 jit_solution(8471180758340675292)
XLA Ops:
  7.2 0.0 all-gather.3.cloned.1.call-start
  7.2 2.0 copy.29
  9.2 0.0 all-gather.3.cloned.1.call-update
  9.2 0.0 all-reduce.2.cloned.1.call-start
  9.3 0.9 copy.20
  10.2 0.7 copy.22
  10.9 31.9 %front.1 = (bf16[128,256,256]{2,1,0:T(8,128)(2,1)}, bf16[128,96,256]{2,1,0:T(8,128)(2,1)}, bf16[96,128,256]{2,1,0:T(8,128)(2,1)}) custom-call(bf16[128,49152]{1,0:T(8,128)(2,1)} %x_ref.1, bf16[96,256]{1,0:T(8,128)(2,1)} %bitcast.25), custom_call_target="tpu_custom_call" | custom-call | flops 2415919104 | bytes 42000000 | tf_op jit(solution)/shard_map/front/pallas_call | solution.py:77
  42.9 31.5 %all-gather.3.cloned.1.call-done = bf16[1536,16,128]{2,1,0:T(8,128)(2,1)} async-done(((bf16[96,16,128]{2,1,0:T(8,128)(2,1)}), bf16[1536,16,128]{2,1,0:T(8,128)(2,1)}) %all-gather.3.cloned.1.call-update) | async-done | bytes 6291472 | tf_op jit(solution)/shard_map/all_gather | solution.py:300
  74.4 44.9 %middle.1 = (f32[24576,128]{1,0:T(8,128)}, bf16[128,96,256]{2,1,0:T(8,128)(2,1)}) custom-call(bf16[96,128,256]{2,1,0:T(8,128)(2,1)} %get-tuple-element.10.gram_ref, bf16[16,96,16,128]{3,2,1,0:T(8,128)(2,1)} %bitcast.21, bf16[128,128]{1,0:T(8,128)(2,1)} %cot_ref.1), custom_call_target="tpu_custom_call" | custom-call | flops 2415919104 | bytes 33000000 | tf_op jit(solution)/shard_map/middle/pallas_call | solution.py:150
  119.3 38.0 %back.1 = (bf16[128,128,384]{2,1,0:T(8,128)(2,1)}, f32[96,256]{1,0:T(8,128)}) custom-call(bf16[128,256,256]{2,1,0:T(8,128)(2,1)} %get-tuple-element.12.xs_ref, bf16[128,96,256]{2,1,0:T(8,128)(2,1)} %get-tuple-element.13.mixed_ref, bf16[128,96,256]{2,1,0:T(8,128)(2,1)} %get-tuple-element.14.gg_ref, bf16[96,256]{1,0:T(8,128)(2,1)} %bitcast.26), custom_call_target="tpu_custom_call" | custom-call | flops 4831838208 | bytes 42000000 | tf_op jit(solution)/shard_map/back/pallas_call | solution.py:210
  157.3 1.0 copy.24
  158.3 0.7 copy.25
  159.0 0.0 all-reduce.2.cloned.1.call-update
  159.0 0.0 reduce-scatter.2.cloned.1.call-start
  159.1 0.7 reduce-scatter.2.cloned.1.call-update
  159.8 8.9 %all-to-all-start = ((bf16[128,128,384]{2,1,0:T(8,128)(2,1)}), bf16[128,128,384]{2,1,0:T(8,128)(2,1)}, u32[]{:S(2)}, u32[]{:S(2)}) async-start(bf16[128,128,384]{2,1,0:T(8,128)(2,1)} %get-tuple-element.16), calls=%async_computation.1 | async-start | bytes 25165824 | tf_op jit(solution)/shard_map/all_to_all | solution.py:305
  168.7 267.0 %all-reduce.2.cloned.1.call-done = f32[256,96]{1,0:T(8,128)} async-done(((f32[256,96]{1,0:T(8,128)}), f32[256,96]{1,0:T(8,128)}) %all-reduce.2.cloned.1.call-update) | async-done | bytes 98320 | tf_op jit(solution)/shard_map/psum | solution.py:306
  435.6 1.6 copy.26
  437.2 0.0 all-to-all-done
  437.2 21.7 %row_sums.1 = f32[1024,192]{1,0:T(8,128)} custom-call(bf16[16384,384]{1,0:T(8,128)(2,1)} %bitcast.13.data_ref, s32[2,16384]{1,0:T(2,128)} %bitcast.31), custom_call_target="tpu_custom_call" | custom-call | flops 17179869184 | bytes 14000000 | tf_op jit(solution)/shard_map/row_sums/pallas_call | solution.py:269
  459.0 2.4 copy.27
  461.4 199.6 %reduce-scatter.2.cloned.1.call-done = f32[192,128]{1,0:T(8,128)} async-done(((f32[24576,128]{1,0:T(8,128)}), f32[192,128]{1,0:T(8,128)}) %reduce-scatter.2.cloned.1.call-update) | async-done | bytes 98320 | tf_op jit(solution)/shard_map/reduce_scatter | solution.py:307
  (1 shorter events, 0.0 us)
Async XLA Ops:
  7.2 67.2 %all-gather.3.cloned.1.call-start = ((), (), s32[]{:S(2)}) async-start(), calls=%async_computation.4 | async-start | bytes 6684672 | tf_op jit(solution)/shard_map/all_gather | solution.py:300
  9.2 426.4 %all-reduce.2.cloned.1.call-start = ((), (), s32[]{:S(2)}) async-start(), calls=%async_computation.3 | async-start | bytes 262144 | tf_op jit(solution)/shard_map/psum | solution.py:306
  159.0 502.0 %reduce-scatter.2.cloned.1.call-start = ((), (), s32[]{:S(2)}) async-start(), calls=%async_computation.2 | async-start | bytes 12681216 | tf_op jit(solution)/shard_map/reduce_scatter | solution.py:307
  159.8 277.5 %all-to-all-start = ((bf16[128,128,384]{2,1,0:T(8,128)(2,1)}), bf16[128,128,384]{2,1,0:T(8,128)(2,1)}, u32[]{:S(2)}, u32[]{:S(2)}) async-start(bf16[128,128,384]{2,1,0:T(8,128)(2,1)} %get-tuple-element.16), calls=%async_computation.1 | async-start | bytes 25165824 | tf_op jit(solution)/shard_map/all_to_all | solution.py:305
Sparse Core Ops, SparseCore 0:
  10.8 63.5 all-gather.2
  159.2 276.3 all-reduce.1
  442.0 219.0 reduce-scatter.1

commit v2 on v1

--- a/solution.py
+++ b/solution.py
@@ -164,12 +164,98 @@
     )(gram, w, cot)
 
 
-def back_kernel(xs_ref, mixed_ref, gg_ref, projt_ref, fg_ref, pg_ref, wide):
+MESH = pl.DeviceIdType.MESH
+
+
+def place():
+    fsdp = lax.axis_index("fsdp")
+    emb = lax.axis_index("emb")
+    return fsdp // 4, fsdp % 4, emb // 2, emb % 2
+
+
+def device(x, y, z, core):
+    return (x * 4 + y, z * 2 + core)
+
+
+def back_kernel(
+    xs_ref, mixed_ref, gg_ref, projt_ref, wgrad_ref,
+    pg_ref, rows_ref, other_ref,
+    wide, stage, send_sem, recv_sem, own_sem, pair_sem,
+):
     low = lower_half(PAIRS)
-
-    @pl.when(pl.program_id(0) == 0)
+    step = pl.program_id(0)
+    steps = pl.num_programs(0)
+    x, y, z, core = place()
+    line = jnp.where(core == 0, x, y)
+    slot = lax.rem(step, 2)
+    sibling = device(x, y, z, 1 - core)
+
+    def weight_copy():
+        return pltpu.make_async_remote_copy(
+            src_ref=wgrad_ref.at[:, 1 - core],
+            dst_ref=other_ref,
+            send_sem=pair_sem.at[0],
+            recv_sem=pair_sem.at[1],
+            device_id=sibling,
+            device_id_type=MESH,
+        )
+
+    def copies(block, where):
+        at_x = pl.ds((x * 2 + core) * 128 + block * ROWS, ROWS)
+        at_y = pl.ds((y * 2 + core) * 128 + block * ROWS, ROWS)
+        found = []
+        for d in range(1, 4):
+            tx = lax.rem(x + d, 4)
+            ty = lax.rem(y + d, 4)
+            for kind, group, rows, target in (
+                (0, tx, at_x, device(tx, y, z, 0)),
+                (1, 4 + ty, at_y, device(x, ty, z, 1)),
+            ):
+                found.append(
+                    pltpu.make_async_remote_copy(
+                        src_ref=stage.at[where, pl.ds(group * 16, 16)],
+                        dst_ref=rows_ref.at[:, rows],
+                        send_sem=send_sem.at[where, kind * 3 + d - 1],
+                        recv_sem=recv_sem.at[block, d * 2 + core],
+                        device_id=target,
+                        device_id_type=MESH,
+                    )
+                )
+        group = jnp.where(core == 0, 4 + y, x)
+        there = pl.ds((jnp.where(core == 0, y, x) * 2 + core) * 128 + block * ROWS, ROWS)
+        found.append(
+            pltpu.make_async_remote_copy(
+                src_ref=stage.at[where, pl.ds(group * 16, 16)],
+                dst_ref=rows_ref.at[:, there],
+                send_sem=send_sem.at[where, 6],
+                recv_sem=recv_sem.at[block, 0],
+                device_id=sibling,
+                device_id_type=MESH,
+            )
+        )
+        return found
+
+    def own_copy(block, where):
+        group = jnp.where(core == 0, x, 4 + y)
+        here = pl.ds((line * 2 + core) * 128 + block * ROWS, ROWS)
+        return pltpu.make_async_copy(
+            stage.at[where, pl.ds(group * 16, 16)], rows_ref.at[:, here], own_sem.at[where]
+        )
+
+    @pl.when(step == 0)
     def _():
         pg_ref[...] = jnp.zeros_like(pg_ref)
+        barrier = pltpu.get_barrier_semaphore()
+        pl.semaphore_signal(barrier, inc=1, device_id=sibling, device_id_type=MESH)
+        for d in range(1, 4):
+            from_x = jnp.where(core == 0, lax.rem(x + d, 4), x)
+            from_y = jnp.where(core == 0, y, lax.rem(y + d, 4))
+            for other in range(2):
+                pl.semaphore_signal(
+                    barrier, inc=1, device_id=device(from_x, from_y, z, other), device_id_type=MESH
+                )
+        pl.semaphore_wait(barrier, 7)
+        weight_copy().start()
 
     def sample(b):
         xb = xs_ref[b]
@@ -189,24 +275,73 @@
         wide[pl.ds(b + 2 * ROWS, PAIRS, stride=3 * ROWS), :] = jnp.where(low, r0, r1)
         return pg
 
-    def samples(step, total):
+    def samples(turn, total):
         for inner in range(4):
-            total = total + sample(step * 4 + inner)
+            total = total + sample(turn * 4 + inner)
         return total
 
     pg_ref[...] += lax.fori_loop(0, ROWS // 4, samples, jnp.zeros((K, F), F32)) * SCALE
 
-    def pack(p, carry):
-        for tile in range(3):
-            at = pl.ds(pl.multiple_of(p * 3 * ROWS + tile * ROWS, ROWS), ROWS)
-            fg_ref[p, :, tile * 128 : tile * 128 + 128] = wide[at, :].astype(BF)
+    @pl.when(step >= 2)
+    def _():
+        for copy in copies(step - 2, slot):
+            copy.wait_send()
+        own_copy(step - 2, slot).wait()
+
+    def pack(q, carry):
+        for kind in range(2):
+            for last in range(4):
+                first, second = q // 4, q % 4
+                if kind == 0:
+                    owner = ((first * 4 + second) * 4 + last) * 2
+                else:
+                    owner = ((second * 4 + first) * 4 + last) * 2 + 1
+                for tile in range(3):
+                    at = pl.ds(pl.multiple_of(owner * 3 * ROWS + tile * ROWS, ROWS), ROWS)
+                    stage[slot, kind * 64 + q * 4 + last, :, tile * 128 : tile * 128 + 128] = wide[
+                        at, :
+                    ].astype(BF)
         return carry
 
-    lax.fori_loop(0, PAIRS, pack, 0, unroll=4)
-
-
-def back(xs, mixed, gg, projt):
+    lax.fori_loop(0, 16, pack, 0)
+    for copy in copies(step, slot):
+        copy.start()
+    own_copy(step, slot).start()
+
+    @pl.when(step == steps - 1)
+    def _():
+        for block, where in ((step - 1, 1 - slot), (step, slot)):
+            for copy in copies(block, where):
+                copy.wait_send()
+            own_copy(block, where).wait()
+        copy = weight_copy()
+        copy.wait_send()
+        copy.wait_recv()
+
+        def arrived(block, carry):
+            def wait(sender, sem):
+                at = pl.ds(sender * 128 + block * ROWS, ROWS)
+                pltpu.make_async_remote_copy(
+                    src_ref=stage.at[0, pl.ds(0, 16)],
+                    dst_ref=rows_ref.at[:, at],
+                    send_sem=send_sem.at[0, 0],
+                    recv_sem=recv_sem.at[block, sem],
+                    device_id=sibling,
+                    device_id_type=MESH,
+                ).wait_recv()
+
+            wait(line * 2 + 1 - core, 0)
+            for d in range(1, 4):
+                for other in range(2):
+                    wait(lax.rem(line + 4 - d, 4) * 2 + other, d * 2 + other)
+            return carry
+
+        lax.fori_loop(0, steps, arrived, 0)
+
+
+def back(xs, mixed, gg, projt, wgrad):
     batch = xs.shape[0]
+    any_space = pl.BlockSpec(memory_space=pl.ANY)
     return pl.pallas_call(
         back_kernel,
         grid=(batch // ROWS,),
@@ -215,73 +350,313 @@
             pl.BlockSpec((ROWS, K, 256), lambda i: (i, 0, 0)),
             pl.BlockSpec((ROWS, K, F), lambda i: (i, 0, 0)),
             pl.BlockSpec((K, F), lambda i: (0, 0)),
-        ],
-        out_specs=[
-            pl.BlockSpec((PAIRS, ROWS, 2 * E), lambda i: (0, i, 0)),
-            pl.BlockSpec((K, F), lambda i: (0, 0)),
-        ],
+            any_space,
+        ],
+        out_specs=[pl.BlockSpec((K, F), lambda i: (0, 0)), any_space, any_space],
         out_shape=[
-            jax.ShapeDtypeStruct((PAIRS, batch, 2 * E), BF),
             jax.ShapeDtypeStruct((K, F), F32),
-        ],
-        scratch_shapes=[pltpu.VMEM((F * E // 128 * ROWS, 128), F32)],
-        compiler_params=pltpu.CompilerParams(vmem_limit_bytes=VMEM_LIMIT),
+            jax.ShapeDtypeStruct((16, 8 * batch, 2 * E), BF),
+            jax.ShapeDtypeStruct((64, 2 * K, H), F32),
+        ],
+        scratch_shapes=[
+            pltpu.VMEM((F * E // 128 * ROWS, 128), F32),
+            pltpu.VMEM((2, PAIRS, ROWS, 2 * E), BF),
+            pltpu.SemaphoreType.DMA((2, 7)),
+            pltpu.SemaphoreType.DMA((batch // ROWS, 8)),
+            pltpu.SemaphoreType.DMA((2,)),
+            pltpu.SemaphoreType.DMA((2,)),
+        ],
+        compiler_params=pltpu.CompilerParams(
+            vmem_limit_bytes=VMEM_LIMIT, collective_id=1, has_side_effects=True
+        ),
         cost_estimate=pl.CostEstimate(
             flops=8 * batch * F * E * K, bytes_accessed=42_000_000, transcendentals=0
         ),
         name="back",
-    )(xs, mixed, gg, projt)
-
-
-CHUNK = 2048
+    )(xs, mixed, gg, projt, wgrad)
+
+
 SLOT_BLOCK = 256
-
-
-def rows_kernel(data_ref, seg_ref, out_ref, even, odd):
-    step = pl.program_id(0)
-
-    @pl.when(step == 0)
-    def _():
-        even[...] = jnp.zeros_like(even)
-        odd[...] = jnp.zeros_like(odd)
-
-    slot = lax.broadcasted_iota(jnp.int32, (SLOT_BLOCK, CHUNK), 0)
-    for block in range(UNIQUE_CAP // SLOT_BLOCK):
-        at = pl.ds(block * SLOT_BLOCK, SLOT_BLOCK)
-        for parity, total in ((0, even), (1, odd)):
-            seg = seg_ref[parity : parity + 1, :] - block * SLOT_BLOCK
-            hot = jnp.where(slot == seg, 1.0, 0.0).astype(BF)
-            total[at, :] += jnp.dot(
-                hot, data_ref[:, parity * 128 : parity * 128 + 256], preferred_element_type=F32
+HALF = UNIQUE_CAP // 2
+
+
+def sums_kernel(
+    rows_ref, seg_ref, wgrad_ref, other_ref, pg_ref,
+    wout_ref, pout_ref, out_ref,
+    data, table, table_z, sum_v, table_v,
+    own, other, w2, w2_in, w3, w3_in, w4, w4_in, pu, pv, pz, pc,
+    load_sem, own_sem, z_send, z_recv, v_send, v_recv, w_send, w_recv, p_send, p_recv,
+):
+    x, y, z, core = place()
+    u = jnp.where(core == 0, x, y)
+    v = jnp.where(core == 0, y, x)
+    low = lower_half(SLOT_BLOCK)
+
+    def at_u(d):
+        moved = lax.rem(u + d, 4)
+        return device(jnp.where(core == 0, moved, x), jnp.where(core == 0, y, moved), z, core)
+
+    def at_v(d):
+        moved = lax.rem(v + d, 4)
+        return device(jnp.where(core == 0, x, moved), jnp.where(core == 0, moved, y), z, core)
+
+    def at_z(d):
+        return device(x, y, lax.rem(z + d, 4), core)
+
+    sibling = device(x, y, z, 1 - core)
+
+    def remote(source, target, send, recv, to):
+        return pltpu.make_async_remote_copy(
+            src_ref=source,
+            dst_ref=target,
+            send_sem=send,
+            recv_sem=recv,
+            device_id=to,
+            device_id_type=MESH,
+        )
+
+    def load(j):
+        return pltpu.make_async_copy(rows_ref.at[j], data.at[j], load_sem.at[j])
+
+    own_copy = pltpu.make_async_copy(wgrad_ref.at[:, core], own, own_sem.at[0])
+    other_copy = pltpu.make_async_copy(other_ref, other, own_sem.at[1])
+    order = [1, 2, 3, 0]
+
+    def group_of(g):
+        return lax.rem(z + g, 4)
+
+    for g in order:
+        for n in range(4):
+            load(n * 4 + group_of(g)).start()
+        if g == 1:
+            own_copy.start()
+            other_copy.start()
+
+    barrier = pltpu.get_barrier_semaphore()
+    for d in range(1, 4):
+        for to in (at_u(d), at_v(d), at_z(d)):
+            pl.semaphore_signal(barrier, inc=1, device_id=to, device_id_type=MESH)
+    pl.semaphore_signal(barrier, inc=1, device_id=sibling, device_id_type=MESH)
+    pl.semaphore_wait(barrier, 10)
+
+    def spread(buffer, mine, stage, to):
+        return [
+            remote(buffer.at[mine], buffer.at[mine], p_send.at[stage, d - 1], p_recv.at[stage, d - 1], to(d))
+            for d in range(1, 4)
+        ]
+
+    def gathered(buffer, mine, stage, to):
+        for d in range(1, 4):
+            sender = lax.rem(mine + 4 - d, 4)
+            remote(
+                buffer.at[sender], buffer.at[sender], p_send.at[stage, d - 1], p_recv.at[stage, d - 1], to(d)
+            ).wait_recv()
+        return (buffer[0] + buffer[1]) + (buffer[2] + buffer[3])
+
+    def start(copies):
+        for copy in copies:
+            copy.start()
+        return copies
+
+    pending = []
+
+    def send_table(g, n):
+        return remote(
+            table.at[g, n],
+            table_z.at[g - 1, n],
+            z_send.at[g - 1, n],
+            z_recv.at[g - 1, n],
+            at_z(g),
+        )
+
+    def presum(g):
+        def one(n, carry):
+            j = n * 4 + group_of(g)
+            load(j).wait()
+            slot = lax.broadcasted_iota(jnp.int32, (SLOT_BLOCK, 8 * 128), 0)
+
+            def part(block, parity):
+                seg = seg_ref[j, parity : parity + 1, :] - block * SLOT_BLOCK
+                hot = jnp.where(slot == seg, 1.0, 0.0).astype(BF)
+                found = jnp.dot(
+                    hot, data[j, :, parity * 128 : parity * 128 + 256], preferred_element_type=F32
+                )
+                return found[:, :128], found[:, 128:]
+
+            for block in range(HALF // SLOT_BLOCK):
+                at = pl.ds(block * SLOT_BLOCK, SLOT_BLOCK)
+                even0, even1 = part(block, 0)
+                odd0, odd1 = part(block, 1)
+                r0 = pltpu.roll(odd0, 64, 1)
+                r1 = pltpu.roll(odd1, 64, 1)
+                table[g, n, at, 0:128] = (even0 + jnp.where(low, r0, r1)).astype(BF)
+                first = even1 + r1
+                even0, even1 = part(block + HALF // SLOT_BLOCK, 0)
+                odd0, odd1 = part(block + HALF // SLOT_BLOCK, 1)
+                r0 = pltpu.roll(even0, 64, 1)
+                r1 = pltpu.roll(even1, 64, 1)
+                table[g, n, at, 128:256] = jnp.where(low, first, r0 + odd0).astype(BF)
+                table[g, n, at, 256:384] = (jnp.where(low, r0, r1) + odd1).astype(BF)
+            if g > 0:
+                send_table(g, n).start()
+            return carry
+
+        lax.fori_loop(0, 4, one, 0)
+
+    def add_four(first, rest, target, parts):
+        def one(n, carry):
+            total = first[n].astype(F32) + rest[0, n].astype(F32)
+            total = total + (rest[1, n].astype(F32) + rest[2, n].astype(F32))
+            target[n] = total.astype(target.dtype)
+            return carry
+
+        lax.fori_loop(0, parts, one, 0)
+
+    def w_copies(source, arrive, stage, to, line, size):
+        return [
+            remote(
+                source.at[pl.ds(lax.rem(line + d, 4) * size, size)],
+                arrive.at[d - 1],
+                w_send.at[stage, d - 1],
+                w_recv.at[stage, d - 1],
+                to(d),
             )
-
-    @pl.when(step == pl.num_programs(0) - 1)
-    def _():
-        low = lower_half(UNIQUE_CAP)
-        r0 = pltpu.roll(odd[:, :128], 64, 1)
-        r1 = pltpu.roll(odd[:, 128:], 64, 1)
-        out_ref[:, :128] = even[:, :128] + jnp.where(low, r0, r1)
-        out_ref[:, 128:] = (even[:, 128:] + r1)[:, :64]
-
-
-def row_sums(data, seg):
-    count = data.shape[0]
+            for d in range(1, 4)
+        ]
+
+    pu[u] = pg_ref[...]
+    p0 = start(spread(pu, u, 0, at_u))
+    presum(1)
+
+    own_copy.wait()
+    other_copy.wait()
+
+    def pair_sum(n, carry):
+        first, second, last = n // 16, (n // 4) % 4, n % 4
+        source = jnp.where(core == 0, first * 16 + second * 4, second * 16 + first * 4) + last
+        w2[n] = (own[source] + other[source]).astype(BF)
+        return carry
+
+    lax.fori_loop(0, 64, pair_sum, 0)
+    s2 = start(w_copies(w2, w2_in, 0, at_u, u, 16))
+    pv[v] = gathered(pu, u, 0, at_u)
+    p1 = start(spread(pv, v, 1, at_v))
+    presum(2)
+    for copy in s2:
+        copy.wait_recv()
+    add_four(w2.at[pl.ds(u * 16, 16)], w2_in, w3, 16)
+    s3 = start(w_copies(w3, w3_in, 1, at_v, v, 4))
+    pz[z] = gathered(pv, v, 1, at_v)
+    p2 = start(spread(pz, z, 2, at_z))
+    presum(3)
+    for copy in s3:
+        copy.wait_recv()
+    add_four(w3.at[pl.ds(v * 4, 4)], w3_in, w4, 4)
+    s4 = start(w_copies(w4, w4_in, 2, at_z, z, 1))
+    pc[core] = gathered(pz, z, 2, at_z)
+    p3 = remote(pc.at[core], pc.at[core], p_send.at[3, 0], p_recv.at[3, 0], sibling)
+    p3.start()
+    presum(0)
+    for copy in s4:
+        copy.wait_recv()
+    total = w4[z].astype(F32) + w4_in[0, 0].astype(F32)
+    wout_ref[...] = total + (w4_in[1, 0].astype(F32) + w4_in[2, 0].astype(F32))
+    remote(pc.at[1 - core], pc.at[1 - core], p_send.at[3, 0], p_recv.at[3, 0], sibling).wait_recv()
+    pout_ref[...] = pc[0] + pc[1]
+
+    def v_copy(d):
+        return remote(sum_v.at[d], table_v.at[d - 1], v_send.at[d - 1], v_recv.at[d - 1], at_v(d))
+
+    for d in order:
+        n = lax.rem(v + d, 4)
+        for g in range(1, 4):
+            send_table(g, n).wait_recv()
+
+        def add(part, carry):
+            at = pl.ds(pl.multiple_of(part * 64, 64), 64)
+            total = table[0, n, at].astype(F32) + table_z[0, n, at].astype(F32)
+            total = total + (table_z[1, n, at].astype(F32) + table_z[2, n, at].astype(F32))
+            sum_v[d, at] = total.astype(BF)
+            return carry
+
+        lax.fori_loop(0, HALF // 64, add, 0)
+        if d > 0:
+            v_copy(d).start()
+    for d in range(1, 4):
+        v_copy(d).wait_recv()
+
+    def finish(part, carry):
+        at = pl.ds(pl.multiple_of(part * 64, 64), 64)
+        after = pl.ds(pl.multiple_of(part * 64 + HALF, 64), 64)
+        total = sum_v[0, at].astype(F32) + table_v[0, at].astype(F32)
+        total = total + (table_v[1, at].astype(F32) + table_v[2, at].astype(F32))
+        out_ref[at, :] = total[:, :E]
+        r1 = pltpu.roll(total[:, 128:256], 64, 1)
+        r2 = pltpu.roll(total[:, 256:], 64, 1)
+        out_ref[after, :128] = jnp.where(lower_half(64), r1, r2)
+        out_ref[after, 128:] = r2[:, :64]
+        return carry
+
+    lax.fori_loop(0, HALF // 64, finish, 0)
+
+    for copy in p0 + p1 + p2 + [p3] + s2 + s3 + s4:
+        copy.wait_send()
+    for d in range(1, 4):
+        v_copy(d).wait_send()
+        for n in range(4):
+            send_table(d, n).wait_send()
+
+
+def sums(rows, seg, wgrad, other, pg):
+    any_space = pl.BlockSpec(memory_space=pl.ANY)
+    whole = pl.BlockSpec(memory_space=pltpu.VMEM)
+    dma = pltpu.SemaphoreType.DMA
     return pl.pallas_call(
-        rows_kernel,
-        grid=(count // CHUNK,),
-        in_specs=[
-            pl.BlockSpec((CHUNK, 2 * E), lambda i: (i, 0)),
-            pl.BlockSpec((2, CHUNK), lambda i: (0, i)),
-        ],
-        out_specs=pl.BlockSpec((UNIQUE_CAP, E), lambda i: (0, 0)),
-        out_shape=jax.ShapeDtypeStruct((UNIQUE_CAP, E), F32),
-        scratch_shapes=[pltpu.VMEM((UNIQUE_CAP, 256), F32)] * 2,
-        compiler_params=pltpu.CompilerParams(vmem_limit_bytes=VMEM_LIMIT),
+        sums_kernel,
+        in_specs=[any_space, whole, any_space, any_space, whole],
+        out_specs=[whole] * 3,
+        out_shape=[
+            jax.ShapeDtypeStruct((2 * K, H), F32),
+            jax.ShapeDtypeStruct((K, F), F32),
+            jax.ShapeDtypeStruct((UNIQUE_CAP, E), F32),
+        ],
+        scratch_shapes=[
+            pltpu.VMEM(rows.shape, BF),
+            pltpu.VMEM((4, 4, HALF, 2 * E), BF),
+            pltpu.VMEM((3, 4, HALF, 2 * E), BF),
+            pltpu.VMEM((4, HALF, 2 * E), BF),
+            pltpu.VMEM((3, HALF, 2 * E), BF),
+            pltpu.VMEM((64, 2 * K, H), F32),
+            pltpu.VMEM((64, 2 * K, H), F32),
+            pltpu.VMEM((64, 2 * K, H), BF),
+            pltpu.VMEM((3, 16, 2 * K, H), BF),
+            pltpu.VMEM((16, 2 * K, H), BF),
+            pltpu.VMEM((3, 4, 2 * K, H), BF),
+            pltpu.VMEM((4, 2 * K, H), BF),
+            pltpu.VMEM((3, 1, 2 * K, H), BF),
+            pltpu.VMEM((4, K, F), F32),
+            pltpu.VMEM((4, K, F), F32),
+            pltpu.VMEM((4, K, F), F32),
+            pltpu.VMEM((2, K, F), F32),
+            dma((16,)),
+            dma((2,)),
+            dma((3, 4)),
+            dma((3, 4)),
+            dma((3,)),
+            dma((3,)),
+            dma((3, 3)),
+            dma((3, 3)),
+            dma((4, 3)),
+            dma((4, 3)),
+        ],
+        compiler_params=pltpu.CompilerParams(
+            vmem_limit_bytes=VMEM_LIMIT, collective_id=2, has_side_effects=True
+        ),
         cost_estimate=pl.CostEstimate(
-            flops=4 * UNIQUE_CAP * count * 256, bytes_accessed=14_000_000, transcendentals=0
+            flops=16 * 4 * UNIQUE_CAP * 1024 * 256, bytes_accessed=30_000_000, transcendentals=0
         ),
-        name="row_sums",
-    )(data, seg)
+        name="sums",
+    )(rows, seg, wgrad, other, pg)
 
 
 def turn_features(a):
@@ -294,19 +669,41 @@
     return a.reshape((-1, 2, 8) + rest).swapaxes(1, 2).reshape(a.shape)
 
 
+def seg_groups():
+    groups = []
+    for x in range(4):
+        groups.append([(x * 4 + y) * 8 + z * 2 for y in range(4) for z in range(4)])
+    for y in range(4):
+        groups.append([(x * 4 + y) * 8 + z * 2 + 1 for x in range(4) for z in range(4)])
+    return groups
+
+
+def spread_segments(segments):
+    core = lax.axis_index("emb") % 2
+    seg = segments.T.reshape(2, 4, 4, 4, 2, 128)
+    along_x = seg.transpose(2, 3, 0, 1, 4, 5).reshape(16, 2, 1024)
+    along_y = seg.transpose(1, 3, 0, 2, 4, 5).reshape(16, 2, 1024)
+    return lax.all_to_all(
+        jnp.where(core == 0, along_x, along_y),
+        ("fsdp", "emb"),
+        split_axis=0,
+        concat_axis=0,
+        axis_index_groups=seg_groups(),
+        tiled=True,
+    )
+
+
 def on_device(pooled, projection, out_weight, cotangent, segments):
-    batch = pooled.shape[0]
     own = turn_features(out_weight.reshape(-1, K, H)).swapaxes(0, 1)
     weight = lax.all_gather(own, "fsdp", axis=0)
+    seg = spread_segments(segments)
     projt = turn_features(projection).T
     xs, mixed, gram = front(pooled, projt)
     wgrad, gg = middle(gram, weight, cotangent)
-    fg, pg = back(xs, mixed, gg, projt)
-    received = lax.all_to_all(fg, ("fsdp", "emb"), split_axis=0, concat_axis=0, tiled=True)
-    proj_grad = lax.psum(unturn_features(pg.T), ("fsdp", "emb"))
-    weight_grad = lax.psum_scatter(wgrad, ("fsdp", "emb"), scatter_dimension=0, tiled=True)
-    row_grad = row_sums(received.reshape(-1, 2 * E), segments.T)
-    return (weight_grad, proj_grad, row_grad)
+    wgrad = wgrad.reshape(64, 2, 2 * K, H)
+    pg, rows, other = back(xs, mixed, gg, projt, wgrad)
+    weight_grad, pg, row_grad = sums(rows, seg, wgrad, other, pg)
+    return (weight_grad, unturn_features(pg.T), row_grad)
 
 
 def solution(mesh):

time: 668 us -> 319 us (0.48)
  waiting for transfers between devices: 499 us -> 21.6 us
  Pallas kernels: 137 us -> 262 us
    psum x1 -> x0, waiting for transfers between devices: 267 us -> none  [on_device(): proj_grad = lax.psum(unturn_features(pg.T), ('fsdp', 'emb'))]
    reduce_scatter x1 -> x0, waiting for transfers between devices: 200 us -> none  [on_device(): lax.psum_scatter(wgrad, ('fsdp', 'emb'), scatter_dimension=0, tiled=True)]
    pallas_call x1, Pallas kernels: 21.7 us -> 104 us  [sums(): pl.pallas_call(sums_kernel, in_specs=[any_space, whole, any_space, any_sp...]
    pallas_call x1, Pallas kernels: 38 us -> 81.4 us  [back(): pl.pallas_call(back_kernel, grid=(batch // ROWS,), in_specs=[pl.BlockSpec...]
    all_gather x1, waiting for transfers between devices: 31.5 us -> 21.6 us  [on_device(): weight = lax.all_gather(own, 'fsdp', axis=0)]
  transfers between devices with their start and end apart: 4 -> 2, of which waited for: 3 -> 1; matrix products, arithmetic and copies ran while one was open for 1% -> 1% of each run, Pallas kernels for 8% -> 50%
where the time goes in v2:
time: 319 us; the launch traced here: 318 us
  Pallas kernels  262 us (82%)
  waiting for transfers between devices  21.6 us (7%)
  between operations  14.1 us (4%)
  local copies, waits for them, and re-layouts  11.9 us (4%)
  starting transfers between devices  8.17 us (3%)
    pallas_call x1, Pallas kernels, sums(): pl.pallas_call(sums_kernel, in_specs=[any_space, whole, any_space, any_sp...  104 us
    pallas_call x1, Pallas kernels, back(): pl.pallas_call(back_kernel, grid=(batch // ROWS,), in_specs=[pl.BlockSpec...  81.4 us
    pallas_call x1, Pallas kernels, middle(): pl.pallas_call(middle_kernel, in_specs=[whole] * 3, out_specs=[whole] * 2...  44.9 us
    pallas_call x1, Pallas kernels, front(): pl.pallas_call(front_kernel, grid=(batch // ROWS,), in_specs=[pl.BlockSpe...  32 us
    all_gather x1, waiting for transfers between devices, on_device(): weight = lax.all_gather(own, 'fsdp', axis=0)  21.6 us
    all_to_all x1, starting transfers between devices, spread_segments(): lax.all_to_all(jnp.where(core == 0, along_x, along_y), ('fsdp', 'emb'), s...  8.13 us
  transfers between devices with their start and end apart: 2, of which 1 were waited for; matrix products, arithmetic and copies ran while one was open for 1% of the time, Pallas kernels for 50%

profile of v2, /device:TPU:0, one launch (start us, length us, event | category | flops | bytes accessed | tf_op | source)
XLA Modules:
  0.0 317.9 jit_solution(4080240113742791292)
XLA Ops:
  7.2 0.0 all-gather.3.cloned.1.call-start
  7.2 2.0 copy.37
  9.2 0.0 all-gather.3.cloned.1.call-update
  9.2 1.1 reshape.37
  10.4 0.8 select_n.21
  11.2 8.1 %all-to-all-start = ((s32[16,2,1024]{2,1,0:T(2,128)}), s32[16,2,1024]{2,1,0:T(2,128)S(1)}, u32[]{:S(2)}, u32[]{:S(2)}) async-start(s32[16,2,1024]{2,1,0:T(2,128)} %select_n.21), calls=%async_computation | async-start | bytes 262144 | tf_op jit(solution)/shard_map/all_to_all | solution.py:686
  19.3 0.9 copy.24
  20.3 0.7 copy.26
  21.0 32.0 %front.1 = (bf16[128,256,256]{2,1,0:T(8,128)(2,1)}, bf16[128,96,256]{2,1,0:T(8,128)(2,1)}, bf16[96,128,256]{2,1,0:T(8,128)(2,1)}) custom-call(bf16[128,49152]{1,0:T(8,128)(2,1)} %x_ref.1, bf16[96,256]{1,0:T(8,128)(2,1)} %bitcast.31), custom_call_target="tpu_custom_call" | custom-call | flops 2415919104 | bytes 42000000 | tf_op jit(solution)/shard_map/front/pallas_call | solution.py:77
  52.9 21.6 %all-gather.3.cloned.1.call-done = bf16[1536,16,128]{2,1,0:T(8,128)(2,1)} async-done(((bf16[96,16,128]{2,1,0:T(8,128)(2,1)}), bf16[1536,16,128]{2,1,0:T(8,128)(2,1)}) %all-gather.3.cloned.1.call-update) | async-done | bytes 6291472 | tf_op jit(solution)/shard_map/all_gather | solution.py:698
  74.6 44.9 %middle.1 = (f32[24576,128]{1,0:T(8,128)}, bf16[128,96,256]{2,1,0:T(8,128)(2,1)}) custom-call(bf16[96,128,256]{2,1,0:T(8,128)(2,1)} %get-tuple-element.16.gram_ref, bf16[16,96,16,128]{3,2,1,0:T(8,128)(2,1)} %bitcast.27, bf16[128,128]{1,0:T(8,128)(2,1)} %cot_ref.1), custom_call_target="tpu_custom_call" | custom-call | flops 2415919104 | bytes 33000000 | tf_op jit(solution)/shard_map/middle/pallas_call | solution.py:150
  119.5 81.4 %back.1 = (f32[96,256]{1,0:T(8,128)}, bf16[16,1024,384]{2,1,0:T(8,128)(2,1)}, f32[64,192,128]{2,1,0:T(8,128)}) custom-call(bf16[128,256,256]{2,1,0:T(8,128)(2,1)} %get-tuple-element.14.xs_ref, bf16[128,96,256]{2,1,0:T(8,128)(2,1)} %get-tuple-element.15.mixed_ref, bf16[128,96,256]{2,1,0:T(8,128)(2,1)} %get-tuple-element.17.gg_ref, bf16[96,256]{1,0:T(8,128)(2,1)} %bitcast.32, ...), custom_call_target="tpu_custom_call" | custom-call | flops 4831838208 | bytes 42000000 | tf_op jit(solution)/shard_map/back/pallas_call | solution.py:345
  200.9 0.0 all-to-all-done.seg_ref
  200.9 0.0 copy-start
  200.9 0.6 copy-done
  201.6 103.7 %sums.1 = (f32[192,128]{1,0:T(8,128)}, f32[96,256]{1,0:T(8,128)}, f32[1024,192]{1,0:T(8,128)}) custom-call(bf16[16,1024,384]{2,1,0:T(8,128)(2,1)} %get-tuple-element.19.rows_ref, s32[16,2,1024]{2,1,0:T(2,128)} %copy-done, f32[64,2,192,128]{3,2,1,0:T(8,128)} %bitcast.26, f32[64,192,128]{2,1,0:T(8,128)} %get-tuple-element.20.other_ref, ...), custom_call_target="tpu_custom_call" | custom-call | flops 17179869184 | bytes 30000000 | tf_op jit(solution)/shard_map/sums/pallas_call | solution.py:614
  305.3 1.0 copy.30
  306.3 0.1 copy.31
  306.4 0.7 copy.32
  307.1 2.4 copy.33
  309.5 1.5 copy.39
  (2 shorter events, 0.1 us)
Async XLA Ops:
  7.2 67.4 %all-gather.3.cloned.1.call-start = ((), (), s32[]{:S(2)}) async-start(), calls=%async_computation.1 | async-start | bytes 6684672 | tf_op jit(solution)/shard_map/all_gather | solution.py:698
  11.2 189.7 %all-to-all-start = ((s32[16,2,1024]{2,1,0:T(2,128)}), s32[16,2,1024]{2,1,0:T(2,128)S(1)}, u32[]{:S(2)}, u32[]{:S(2)}) async-start(s32[16,2,1024]{2,1,0:T(2,128)} %select_n.21), calls=%async_computation | async-start | bytes 262144 | tf_op jit(solution)/shard_map/all_to_all | solution.py:686
  200.9 0.7 copy-start
Sparse Core Ops, SparseCore 0:
  10.8 63.7 all-gather.2

commit v3 on v2

--- a/solution.py
+++ b/solution.py
@@ -32,7 +32,137 @@
     return lax.broadcasted_iota(jnp.int32, (rows, 128), 1) < 64
 
 
-def front_kernel(x_ref, projt_ref, xs_ref, mixed_ref, gram_ref, wide, turned):
+MESH = pl.DeviceIdType.MESH
+
+
+def place():
+    fsdp = lax.axis_index("fsdp")
+    emb = lax.axis_index("emb")
+    return fsdp // 4, fsdp % 4, emb // 2, emb % 2
+
+
+def device(x, y, z, core):
+    return (x * 4 + y, z * 2 + core)
+
+
+def turn(at, d):
+    return lax.rem(at + 4 + d, 4)
+
+
+def greet(devices):
+    barrier = pltpu.get_barrier_semaphore()
+    for to in devices:
+        pl.semaphore_signal(barrier, inc=1, device_id=to, device_id_type=MESH)
+    pl.semaphore_wait(barrier, len(devices))
+
+
+def remote(source, target, send, recv, to):
+    return pltpu.make_async_remote_copy(
+        src_ref=source,
+        dst_ref=target,
+        send_sem=send,
+        recv_sem=recv,
+        device_id=to,
+        device_id_type=MESH,
+    )
+
+
+def front_kernel(
+    x_ref, projt_ref, own_ref, cut_ref,
+    xs_ref, mixed_ref, gram_ref, weight_ref, seg_ref,
+    wide, turned, u_send, u_recv, v_send, v_recv, s_send, s_recv, g_send, g_recv, own_sem,
+):
+    step = pl.program_id(0)
+    x, y, z, core = place()
+    u = jnp.where(core == 0, x, y)
+    v = jnp.where(core == 0, y, x)
+    half = pl.ds(pl.multiple_of(core * (K // 2), K // 2), K // 2)
+    other_half = pl.ds(pl.multiple_of((1 - core) * (K // 2), K // 2), K // 2)
+    sibling = device(x, y, z, 1 - core)
+
+    def at(du, dv, dz):
+        moved_u, moved_v = turn(u, du), turn(v, dv)
+        return device(
+            jnp.where(core == 0, moved_u, moved_v),
+            jnp.where(core == 0, moved_v, moved_u),
+            turn(z, dz),
+            core,
+        )
+
+    def block(du, dv):
+        moved_u, moved_v = turn(u, du), turn(v, dv)
+        return jnp.where(core == 0, moved_u * 4 + moved_v, moved_v * 4 + moved_u)
+
+    def along_u(d):
+        return remote(
+            own_ref.at[half], weight_ref.at[block(0, 0), half], u_send.at[d - 1], u_recv.at[d - 1], at(d, 0, 0)
+        )
+
+    def from_u(d):
+        there = weight_ref.at[block(-d, 0), half]
+        return remote(there, there, u_send.at[d - 1], u_recv.at[d - 1], at(d, 0, 0))
+
+    def along_v(d, du):
+        there = weight_ref.at[block(du, 0), half]
+        source = own_ref.at[half] if du == 0 else there
+        return remote(source, there, v_send.at[d - 1, du], v_recv.at[d - 1, du], at(0, d, 0))
+
+    def from_v(d, du):
+        there = weight_ref.at[block(du, -d), half]
+        return remote(there, there, v_send.at[d - 1, du], v_recv.at[d - 1, du], at(0, d, 0))
+
+    def to_sibling(du, dv):
+        there = weight_ref.at[block(du, dv), half]
+        return remote(there, there, s_send.at[du, dv % 4], s_recv.at[du, dv % 4], sibling)
+
+    def from_sibling(du, dv):
+        first = jnp.where(core == 0, turn(x, dv), turn(x, du))
+        second = jnp.where(core == 0, turn(y, du), turn(y, dv))
+        there = weight_ref.at[first * 4 + second, other_half]
+        return remote(there, there, s_send.at[du, dv % 4], s_recv.at[du, dv % 4], sibling)
+
+    def segments_to(dv, dz):
+        there = turn(v, dv) * 4 + turn(z, dz)
+        return remote(
+            cut_ref.at[there], seg_ref.at[v * 4 + z], g_send.at[dv, dz], g_recv.at[dv, dz], at(0, dv, dz)
+        )
+
+    def segments_from(dv, dz):
+        there = seg_ref.at[turn(v, -dv) * 4 + turn(z, -dz)]
+        return remote(there, there, g_send.at[dv, dz], g_recv.at[dv, dz], at(0, dv, dz))
+
+    plane = [(dv, dz) for dv in range(4) for dz in range(4) if dv or dz]
+    blocks = [(du, dv) for du in range(4) for dv in range(4) if du or dv]
+    weight_copy = pltpu.make_async_copy(own_ref, weight_ref.at[block(0, 0)], own_sem.at[0])
+    seg_copy = pltpu.make_async_copy(cut_ref.at[v * 4 + z], seg_ref.at[v * 4 + z], own_sem.at[1])
+
+    @pl.when(step == 0)
+    def _():
+        greet([at(d, 0, 0) for d in range(1, 4)] + [at(0, dv, dz) for dv, dz in plane] + [sibling])
+        for d in range(1, 4):
+            along_u(d).start()
+        for d in range(1, 4):
+            along_v(d, 0).start()
+        weight_copy.start()
+        seg_copy.start()
+        for dv, dz in plane:
+            segments_to(dv, dz).start()
+
+    @pl.when(step == 2)
+    def _():
+        for d in range(1, 4):
+            from_u(d).wait_recv()
+            for dv in range(1, 4):
+                along_v(dv, 4 - d).start()
+            to_sibling(4 - d, 0).start()
+
+    @pl.when(step == pl.num_programs(0) - 1)
+    def _():
+        for du in range(4):
+            for d in range(1, 4):
+                from_v(d, du).wait_recv()
+                to_sibling(du, 4 - d).start()
+
     def spread(step, carry):
         for inner in range(8):
             tile = step * 8 + inner
@@ -66,41 +196,75 @@
         return carry
 
     lax.fori_loop(0, ROWS // 4, samples, 0)
-    for half in range(2):
-        gram_ref[:, :, half * 128 : half * 128 + 128] = (
-            turned[half].reshape(K, ROWS, 128).astype(BF)
+    for part in range(2):
+        gram_ref[:, :, part * 128 : part * 128 + 128] = (
+            turned[part].reshape(K, ROWS, 128).astype(BF)
         )
 
-
-def front(x, projt):
+    @pl.when(step == pl.num_programs(0) - 1)
+    def _():
+        for du, dv in blocks:
+            from_sibling(du, dv).wait_recv()
+            to_sibling(du, dv).wait_send()
+        for dv, dz in plane:
+            segments_from(dv, dz).wait_recv()
+            segments_to(dv, dz).wait_send()
+        for d in range(1, 4):
+            along_u(d).wait_send()
+            for du in range(4):
+                along_v(d, du).wait_send()
+        weight_copy.wait()
+        seg_copy.wait()
+
+
+def front(x, projt, own, cut):
     batch = x.shape[0]
+    any_space = pl.BlockSpec(memory_space=pl.ANY)
+    dma = pltpu.SemaphoreType.DMA
     return pl.pallas_call(
         front_kernel,
         grid=(batch // ROWS,),
         in_specs=[
             pl.BlockSpec((ROWS, F * E), lambda i: (i, 0)),
             pl.BlockSpec((K, F), lambda i: (0, 0)),
+            any_space,
+            any_space,
         ],
         out_specs=[
             pl.BlockSpec((ROWS, F, 256), lambda i: (i, 0, 0)),
             pl.BlockSpec((ROWS, K, 256), lambda i: (i, 0, 0)),
             pl.BlockSpec((K, ROWS, F), lambda i: (0, i, 0)),
+            any_space,
+            any_space,
         ],
         out_shape=[
             jax.ShapeDtypeStruct((batch, F, 256), BF),
             jax.ShapeDtypeStruct((batch, K, 256), BF),
             jax.ShapeDtypeStruct((K, batch, F), BF),
+            jax.ShapeDtypeStruct((16,) + own.shape, BF),
+            jax.ShapeDtypeStruct(cut.shape, jnp.int32),
         ],
         scratch_shapes=[
             pltpu.VMEM((F * E // 128 * ROWS, 128), F32),
             pltpu.VMEM((2, K * ROWS, 128), F32),
-        ],
-        compiler_params=pltpu.CompilerParams(vmem_limit_bytes=VMEM_LIMIT),
+            dma((3,)),
+            dma((3,)),
+            dma((3, 4)),
+            dma((3, 4)),
+            dma((4, 4)),
+            dma((4, 4)),
+            dma((4, 4)),
+            dma((4, 4)),
+            dma((2,)),
+        ],
+        compiler_params=pltpu.CompilerParams(
+            vmem_limit_bytes=VMEM_LIMIT, collective_id=3, has_side_effects=True
+        ),
         cost_estimate=pl.CostEstimate(
             flops=4 * batch * F * E * K, bytes_accessed=42_000_000, transcendentals=0
         ),
         name="front",
-    )(x, projt)
+    )(x, projt, own, cut)
 
 
 def middle_kernel(gram_ref, w_ref, cot_ref, wgrad_ref, gg_ref, turned):
@@ -164,23 +328,10 @@
     )(gram, w, cot)
 
 
-MESH = pl.DeviceIdType.MESH
-
-
-def place():
-    fsdp = lax.axis_index("fsdp")
-    emb = lax.axis_index("emb")
-    return fsdp // 4, fsdp % 4, emb // 2, emb % 2
-
-
-def device(x, y, z, core):
-    return (x * 4 + y, z * 2 + core)
-
-
 def back_kernel(
     xs_ref, mixed_ref, gg_ref, projt_ref, wgrad_ref,
-    pg_ref, rows_ref, other_ref,
-    wide, stage, send_sem, recv_sem, own_sem, pair_sem,
+    pg_ref, rows_ref, wz_ref,
+    wide, stage, own, other, w2, w2_in, send_sem, recv_sem, own_sem, pair_sem, z_send, z_recv,
 ):
     low = lower_half(PAIRS)
     step = pl.program_id(0)
@@ -191,14 +342,15 @@
     sibling = device(x, y, z, 1 - core)
 
     def weight_copy():
-        return pltpu.make_async_remote_copy(
-            src_ref=wgrad_ref.at[:, 1 - core],
-            dst_ref=other_ref,
-            send_sem=pair_sem.at[0],
-            recv_sem=pair_sem.at[1],
-            device_id=sibling,
-            device_id_type=MESH,
-        )
+        return remote(wgrad_ref.at[:, 1 - core], other, pair_sem.at[0], pair_sem.at[1], sibling)
+
+    def weight_own():
+        return pltpu.make_async_copy(wgrad_ref.at[:, core], own, pair_sem.at[2])
+
+    def weight_z(d):
+        there = turn(z, d)
+        to = device(x, y, there, core)
+        return remote(w2.at[there], w2_in.at[d - 1], z_send.at[d - 1], z_recv.at[d - 1], to)
 
     def copies(block, where):
         at_x = pl.ds((x * 2 + core) * 128 + block * ROWS, ROWS)
@@ -245,17 +397,31 @@
     @pl.when(step == 0)
     def _():
         pg_ref[...] = jnp.zeros_like(pg_ref)
-        barrier = pltpu.get_barrier_semaphore()
-        pl.semaphore_signal(barrier, inc=1, device_id=sibling, device_id_type=MESH)
+        senders = [sibling]
         for d in range(1, 4):
             from_x = jnp.where(core == 0, lax.rem(x + d, 4), x)
             from_y = jnp.where(core == 0, y, lax.rem(y + d, 4))
-            for other in range(2):
-                pl.semaphore_signal(
-                    barrier, inc=1, device_id=device(from_x, from_y, z, other), device_id_type=MESH
-                )
-        pl.semaphore_wait(barrier, 7)
+            senders += [device(from_x, from_y, z, other_core) for other_core in range(2)]
+            senders.append(device(x, y, turn(z, d), core))
+        greet(senders)
         weight_copy().start()
+        weight_own().start()
+
+    @pl.when(step == 2)
+    def _():
+        weight_own().wait()
+        weight_copy().wait_send()
+        weight_copy().wait_recv()
+
+        def pair_sum(n, carry):
+            to_z, first, second = n // 16, (n // 4) % 4, n % 4
+            source = jnp.where(core == 0, first * 4 + second, second * 4 + first) * 4 + to_z
+            w2[to_z, n % 16] = (own[source] + other[source]).astype(BF)
+            return carry
+
+        lax.fori_loop(0, 64, pair_sum, 0)
+        for d in range(1, 4):
+            weight_z(d).start()
 
     def sample(b):
         xb = xs_ref[b]
@@ -314,9 +480,18 @@
             for copy in copies(block, where):
                 copy.wait_send()
             own_copy(block, where).wait()
-        copy = weight_copy()
-        copy.wait_send()
-        copy.wait_recv()
+        for d in range(1, 4):
+            weight_z(d).wait_recv()
+
+        def sum_z(n, carry):
+            total = w2[z, n].astype(F32) + w2_in[0, n].astype(F32)
+            total = total + (w2_in[1, n].astype(F32) + w2_in[2, n].astype(F32))
+            wz_ref[n] = total.astype(BF)
+            return carry
+
+        lax.fori_loop(0, 16, sum_z, 0)
+        for d in range(1, 4):
+            weight_z(d).wait_send()
 
         def arrived(block, carry):
             def wait(sender, sem):
@@ -352,19 +527,29 @@
             pl.BlockSpec((K, F), lambda i: (0, 0)),
             any_space,
         ],
-        out_specs=[pl.BlockSpec((K, F), lambda i: (0, 0)), any_space, any_space],
+        out_specs=[
+            pl.BlockSpec((K, F), lambda i: (0, 0)),
+            any_space,
+            pl.BlockSpec((16, 2 * K, H), lambda i: (0, 0, 0)),
+        ],
         out_shape=[
             jax.ShapeDtypeStruct((K, F), F32),
             jax.ShapeDtypeStruct((16, 8 * batch, 2 * E), BF),
-            jax.ShapeDtypeStruct((64, 2 * K, H), F32),
+            jax.ShapeDtypeStruct((16, 2 * K, H), BF),
         ],
         scratch_shapes=[
             pltpu.VMEM((F * E // 128 * ROWS, 128), F32),
             pltpu.VMEM((2, PAIRS, ROWS, 2 * E), BF),
+            pltpu.VMEM((64, 2 * K, H), F32),
+            pltpu.VMEM((64, 2 * K, H), F32),
+            pltpu.VMEM((4, 16, 2 * K, H), BF),
+            pltpu.VMEM((3, 16, 2 * K, H), BF),
             pltpu.SemaphoreType.DMA((2, 7)),
             pltpu.SemaphoreType.DMA((batch // ROWS, 8)),
             pltpu.SemaphoreType.DMA((2,)),
-            pltpu.SemaphoreType.DMA((2,)),
+            pltpu.SemaphoreType.DMA((3,)),
+            pltpu.SemaphoreType.DMA((3,)),
+            pltpu.SemaphoreType.DMA((3,)),
         ],
         compiler_params=pltpu.CompilerParams(
             vmem_limit_bytes=VMEM_LIMIT, collective_id=1, has_side_effects=True
@@ -378,14 +563,16 @@
 
 SLOT_BLOCK = 256
 HALF = UNIQUE_CAP // 2
+FIRST = 128
+ORDER = (1, 2, 3, 0)
 
 
 def sums_kernel(
-    rows_ref, seg_ref, wgrad_ref, other_ref, pg_ref,
+    rows_ref, seg_ref, wz_ref, pg_ref,
     wout_ref, pout_ref, out_ref,
-    data, table, table_z, sum_v, table_v,
-    own, other, w2, w2_in, w3, w3_in, w4, w4_in, pu, pv, pz, pc,
-    load_sem, own_sem, z_send, z_recv, v_send, v_recv, w_send, w_recv, p_send, p_recv,
+    data, table, az, bv, sum_a, sum_b, va, zb, w3_in, w4, w4_in, pu, pv, pz, pc,
+    load_sem, az_send, az_recv, bv_send, bv_recv, va_send, va_recv, zb_send, zb_recv,
+    w_send, w_recv, p_send, p_recv,
 ):
     x, y, z, core = place()
     u = jnp.where(core == 0, x, y)
@@ -393,51 +580,27 @@
     low = lower_half(SLOT_BLOCK)
 
     def at_u(d):
-        moved = lax.rem(u + d, 4)
+        moved = turn(u, d)
         return device(jnp.where(core == 0, moved, x), jnp.where(core == 0, y, moved), z, core)
 
     def at_v(d):
-        moved = lax.rem(v + d, 4)
+        moved = turn(v, d)
         return device(jnp.where(core == 0, x, moved), jnp.where(core == 0, moved, y), z, core)
 
     def at_z(d):
-        return device(x, y, lax.rem(z + d, 4), core)
+        return device(x, y, turn(z, d), core)
 
     sibling = device(x, y, z, 1 - core)
 
-    def remote(source, target, send, recv, to):
-        return pltpu.make_async_remote_copy(
-            src_ref=source,
-            dst_ref=target,
-            send_sem=send,
-            recv_sem=recv,
-            device_id=to,
-            device_id_type=MESH,
-        )
-
-    def load(j):
-        return pltpu.make_async_copy(rows_ref.at[j], data.at[j], load_sem.at[j])
-
-    own_copy = pltpu.make_async_copy(wgrad_ref.at[:, core], own, own_sem.at[0])
-    other_copy = pltpu.make_async_copy(other_ref, other, own_sem.at[1])
-    order = [1, 2, 3, 0]
-
-    def group_of(g):
-        return lax.rem(z + g, 4)
-
-    for g in order:
-        for n in range(4):
-            load(n * 4 + group_of(g)).start()
-        if g == 1:
-            own_copy.start()
-            other_copy.start()
-
-    barrier = pltpu.get_barrier_semaphore()
-    for d in range(1, 4):
-        for to in (at_u(d), at_v(d), at_z(d)):
-            pl.semaphore_signal(barrier, inc=1, device_id=to, device_id_type=MESH)
-    pl.semaphore_signal(barrier, inc=1, device_id=sibling, device_id_type=MESH)
-    pl.semaphore_wait(barrier, 10)
+    def load(dz, dv):
+        j = turn(v, dv) * 4 + turn(z, dz)
+        return pltpu.make_async_copy(rows_ref.at[j], data.at[dz, dv], load_sem.at[dz, dv])
+
+    for dz in ORDER:
+        for dv in ORDER:
+            load(dz, dv).start()
+
+    greet([to(d) for d in range(1, 4) for to in (at_u, at_v, at_z)] + [sibling])
 
     def spread(buffer, mine, stage, to):
         return [
@@ -447,10 +610,8 @@
 
     def gathered(buffer, mine, stage, to):
         for d in range(1, 4):
-            sender = lax.rem(mine + 4 - d, 4)
-            remote(
-                buffer.at[sender], buffer.at[sender], p_send.at[stage, d - 1], p_recv.at[stage, d - 1], to(d)
-            ).wait_recv()
+            there = buffer.at[turn(mine, -d)]
+            remote(there, there, p_send.at[stage, d - 1], p_recv.at[stage, d - 1], to(d)).wait_recv()
         return (buffer[0] + buffer[1]) + (buffer[2] + buffer[3])
 
     def start(copies):
@@ -458,64 +619,106 @@
             copy.start()
         return copies
 
-    pending = []
-
-    def send_table(g, n):
+    def send_a(dz, dv):
         return remote(
-            table.at[g, n],
-            table_z.at[g - 1, n],
-            z_send.at[g - 1, n],
-            z_recv.at[g - 1, n],
-            at_z(g),
+            table.at[dz, dv, pl.ds(0, FIRST)],
+            az.at[dz - 1, dv],
+            az_send.at[dz - 1, dv],
+            az_recv.at[dz - 1, dv],
+            at_z(dz),
         )
 
-    def presum(g):
+    def send_b(dv, dz):
+        return remote(
+            table.at[dz, dv, pl.ds(FIRST, HALF - FIRST)],
+            bv.at[dv - 1, dz],
+            bv_send.at[dv - 1, dz],
+            bv_recv.at[dv - 1, dz],
+            at_v(dv),
+        )
+
+    def second_a(dv):
+        return remote(sum_a.at[dv], va.at[dv - 1], va_send.at[dv - 1], va_recv.at[dv - 1], at_v(dv))
+
+    def second_b(dz):
+        return remote(sum_b.at[dz], zb.at[dz - 1], zb_send.at[dz - 1], zb_recv.at[dz - 1], at_z(dz))
+
+    def one_table(dz, dv):
+        load(dz, dv).wait()
+        j = turn(v, dv) * 4 + turn(z, dz)
+        slot = lax.broadcasted_iota(jnp.int32, (SLOT_BLOCK, 8 * 128), 0)
+
+        def part(block, parity):
+            seg = seg_ref[j, parity : parity + 1, :] - block * SLOT_BLOCK
+            hot = jnp.where(slot == seg, 1.0, 0.0).astype(BF)
+            found = jnp.dot(
+                hot, data[dz, dv, :, parity * 128 : parity * 128 + 256], preferred_element_type=F32
+            )
+            return found[:, :128], found[:, 128:]
+
+        for block in range(HALF // SLOT_BLOCK):
+            at = pl.ds(block * SLOT_BLOCK, SLOT_BLOCK)
+            even0, even1 = part(block, 0)
+            odd0, odd1 = part(block, 1)
+            r0 = pltpu.roll(odd0, 64, 1)
+            r1 = pltpu.roll(odd1, 64, 1)
+            table[dz, dv, at, 0:128] = (even0 + jnp.where(low, r0, r1)).astype(BF)
+            first = even1 + r1
+            even0, even1 = part(block + HALF // SLOT_BLOCK, 0)
+            odd0, odd1 = part(block + HALF // SLOT_BLOCK, 1)
+            r0 = pltpu.roll(even0, 64, 1)
+            r1 = pltpu.roll(even1, 64, 1)
+            table[dz, dv, at, 128:256] = jnp.where(low, first, r0 + odd0).astype(BF)
+            table[dz, dv, at, 256:384] = (jnp.where(low, r0, r1) + odd1).astype(BF)
+
+    def tables(dz):
+        def one(turns, carry):
+            dv = lax.rem(turns + 1, 4)
+            one_table(dz, dv)
+            if dz > 0:
+                send_a(dz, dv).start()
+
+            @pl.when(dv > 0)
+            def _():
+                send_b(dv, dz).start()
+
+            return carry
+
+        lax.fori_loop(0, 4, one, 0)
+
+    def add_four(first, second, third, fourth, target, size):
+        rows = first.shape[0]
+
         def one(n, carry):
-            j = n * 4 + group_of(g)
-            load(j).wait()
-            slot = lax.broadcasted_iota(jnp.int32, (SLOT_BLOCK, 8 * 128), 0)
-
-            def part(block, parity):
-                seg = seg_ref[j, parity : parity + 1, :] - block * SLOT_BLOCK
-                hot = jnp.where(slot == seg, 1.0, 0.0).astype(BF)
-                found = jnp.dot(
-                    hot, data[j, :, parity * 128 : parity * 128 + 256], preferred_element_type=F32
-                )
-                return found[:, :128], found[:, 128:]
-
-            for block in range(HALF // SLOT_BLOCK):
-                at = pl.ds(block * SLOT_BLOCK, SLOT_BLOCK)
-                even0, even1 = part(block, 0)
-                odd0, odd1 = part(block, 1)
-                r0 = pltpu.roll(odd0, 64, 1)
-                r1 = pltpu.roll(odd1, 64, 1)
-                table[g, n, at, 0:128] = (even0 + jnp.where(low, r0, r1)).astype(BF)
-                first = even1 + r1
-                even0, even1 = part(block + HALF // SLOT_BLOCK, 0)
-                odd0, odd1 = part(block + HALF // SLOT_BLOCK, 1)
-                r0 = pltpu.roll(even0, 64, 1)
-                r1 = pltpu.roll(even1, 64, 1)
-                table[g, n, at, 128:256] = jnp.where(low, first, r0 + odd0).astype(BF)
-                table[g, n, at, 256:384] = (jnp.where(low, r0, r1) + odd1).astype(BF)
-            if g > 0:
-                send_table(g, n).start()
+            at = pl.ds(pl.multiple_of(n * size, size), size)
+            total = (first[at].astype(F32) + second[at].astype(F32)) + (
+                third[at].astype(F32) + fourth[at].astype(F32)
+            )
+            target[at] = total.astype(target.dtype)
             return carry
 
-        lax.fori_loop(0, 4, one, 0)
-
-    def add_four(first, rest, target, parts):
-        def one(n, carry):
-            total = first[n].astype(F32) + rest[0, n].astype(F32)
-            total = total + (rest[1, n].astype(F32) + rest[2, n].astype(F32))
-            target[n] = total.astype(target.dtype)
-            return carry
-
-        lax.fori_loop(0, parts, one, 0)
+        lax.fori_loop(0, rows // size, one, 0)
+
+    def total_b(dz):
+        for dv in range(1, 4):
+            send_b(dv, dz).wait_recv()
+        mine = table.at[dz, 0, pl.ds(FIRST, HALF - FIRST)]
+        add_four(mine, bv.at[0, dz], bv.at[1, dz], bv.at[2, dz], sum_b.at[dz], 64)
+        if dz > 0:
+            second_b(dz).start()
+
+    def total_a(dv):
+        for dz in range(1, 4):
+            send_a(dz, dv).wait_recv()
+        mine = table.at[0, dv, pl.ds(0, FIRST)]
+        add_four(mine, az.at[0, dv], az.at[1, dv], az.at[2, dv], sum_a.at[dv], 64)
+        if dv > 0:
+            second_a(dv).start()
 
     def w_copies(source, arrive, stage, to, line, size):
         return [
             remote(
-                source.at[pl.ds(lax.rem(line + d, 4) * size, size)],
+                source.at[pl.ds(turn(line, d) * size, size)],
                 arrive.at[d - 1],
                 w_send.at[stage, d - 1],
                 w_recv.at[stage, d - 1],
@@ -526,94 +729,76 @@
 
     pu[u] = pg_ref[...]
     p0 = start(spread(pu, u, 0, at_u))
-    presum(1)
-
-    own_copy.wait()
-    other_copy.wait()
-
-    def pair_sum(n, carry):
-        first, second, last = n // 16, (n // 4) % 4, n % 4
-        source = jnp.where(core == 0, first * 16 + second * 4, second * 16 + first * 4) + last
-        w2[n] = (own[source] + other[source]).astype(BF)
-        return carry
-
-    lax.fori_loop(0, 64, pair_sum, 0)
-    s2 = start(w_copies(w2, w2_in, 0, at_u, u, 16))
+    s3 = start(w_copies(wz_ref, w3_in, 0, at_u, u, 4))
+    tables(1)
     pv[v] = gathered(pu, u, 0, at_u)
     p1 = start(spread(pv, v, 1, at_v))
-    presum(2)
-    for copy in s2:
+    for copy in s3:
         copy.wait_recv()
-    add_four(w2.at[pl.ds(u * 16, 16)], w2_in, w3, 16)
-    s3 = start(w_copies(w3, w3_in, 1, at_v, v, 4))
+    add_four(wz_ref.at[pl.ds(u * 4, 4)], w3_in.at[0], w3_in.at[1], w3_in.at[2], w4, 1)
+    s4 = start(w_copies(w4, w4_in, 1, at_v, v, 1))
+    tables(2)
+    total_b(1)
     pz[z] = gathered(pv, v, 1, at_v)
     p2 = start(spread(pz, z, 2, at_z))
-    presum(3)
-    for copy in s3:
-        copy.wait_recv()
-    add_four(w3.at[pl.ds(v * 4, 4)], w3_in, w4, 4)
-    s4 = start(w_copies(w4, w4_in, 2, at_z, z, 1))
+    tables(3)
+    total_b(2)
     pc[core] = gathered(pz, z, 2, at_z)
     p3 = remote(pc.at[core], pc.at[core], p_send.at[3, 0], p_recv.at[3, 0], sibling)
     p3.start()
-    presum(0)
     for copy in s4:
         copy.wait_recv()
-    total = w4[z].astype(F32) + w4_in[0, 0].astype(F32)
+    total = w4[v].astype(F32) + w4_in[0, 0].astype(F32)
     wout_ref[...] = total + (w4_in[1, 0].astype(F32) + w4_in[2, 0].astype(F32))
+    tables(0)
+    total_b(3)
+    for dv in ORDER:
+        total_a(dv)
+    total_b(0)
     remote(pc.at[1 - core], pc.at[1 - core], p_send.at[3, 0], p_recv.at[3, 0], sibling).wait_recv()
     pout_ref[...] = pc[0] + pc[1]
 
-    def v_copy(d):
-        return remote(sum_v.at[d], table_v.at[d - 1], v_send.at[d - 1], v_recv.at[d - 1], at_v(d))
-
-    for d in order:
-        n = lax.rem(v + d, 4)
-        for g in range(1, 4):
-            send_table(g, n).wait_recv()
-
-        def add(part, carry):
+    def finish(mine, others, start_row, rows):
+        def one(part, carry):
             at = pl.ds(pl.multiple_of(part * 64, 64), 64)
-            total = table[0, n, at].astype(F32) + table_z[0, n, at].astype(F32)
-            total = total + (table_z[1, n, at].astype(F32) + table_z[2, n, at].astype(F32))
-            sum_v[d, at] = total.astype(BF)
+            before = pl.ds(pl.multiple_of(part * 64 + start_row, 64), 64)
+            after = pl.ds(pl.multiple_of(part * 64 + start_row + HALF, 64), 64)
+            total = mine[at, :].astype(F32) + others[0, at].astype(F32)
+            total = total + (others[1, at].astype(F32) + others[2, at].astype(F32))
+            out_ref[before, :] = total[:, :E]
+            r1 = pltpu.roll(total[:, 128:256], 64, 1)
+            r2 = pltpu.roll(total[:, 256:], 64, 1)
+            out_ref[after, :128] = jnp.where(lower_half(64), r1, r2)
+            out_ref[after, 128:] = r2[:, :64]
             return carry
 
-        lax.fori_loop(0, HALF // 64, add, 0)
-        if d > 0:
-            v_copy(d).start()
+        lax.fori_loop(0, rows // 64, one, 0)
+
     for d in range(1, 4):
-        v_copy(d).wait_recv()
-
-    def finish(part, carry):
-        at = pl.ds(pl.multiple_of(part * 64, 64), 64)
-        after = pl.ds(pl.multiple_of(part * 64 + HALF, 64), 64)
-        total = sum_v[0, at].astype(F32) + table_v[0, at].astype(F32)
-        total = total + (table_v[1, at].astype(F32) + table_v[2, at].astype(F32))
-        out_ref[at, :] = total[:, :E]
-        r1 = pltpu.roll(total[:, 128:256], 64, 1)
-        r2 = pltpu.roll(total[:, 256:], 64, 1)
-        out_ref[after, :128] = jnp.where(lower_half(64), r1, r2)
-        out_ref[after, 128:] = r2[:, :64]
-        return carry
-
-    lax.fori_loop(0, HALF // 64, finish, 0)
-
-    for copy in p0 + p1 + p2 + [p3] + s2 + s3 + s4:
+        second_a(d).wait_recv()
+    finish(sum_a.at[0], va, 0, FIRST)
+    for d in range(1, 4):
+        second_b(d).wait_recv()
+    finish(sum_b.at[0], zb, FIRST, HALF - FIRST)
+
+    for copy in p0 + p1 + p2 + [p3] + s3 + s4:
         copy.wait_send()
     for d in range(1, 4):
-        v_copy(d).wait_send()
+        second_a(d).wait_send()
+        second_b(d).wait_send()
         for n in range(4):
-            send_table(d, n).wait_send()
-
-
-def sums(rows, seg, wgrad, other, pg):
+            send_a(d, n).wait_send()
+            send_b(d, n).wait_send()
+
+
+def sums(rows, seg, wz, pg):
     any_space = pl.BlockSpec(memory_space=pl.ANY)
     whole = pl.BlockSpec(memory_space=pltpu.VMEM)
     dma = pltpu.SemaphoreType.DMA
+    rest = HALF - FIRST
     return pl.pallas_call(
         sums_kernel,
-        in_specs=[any_space, whole, any_space, any_space, whole],
+        in_specs=[any_space, whole, whole, whole],
         out_specs=[whole] * 3,
         out_shape=[
             jax.ShapeDtypeStruct((2 * K, H), F32),
@@ -621,16 +806,14 @@
             jax.ShapeDtypeStruct((UNIQUE_CAP, E), F32),
         ],
         scratch_shapes=[
-            pltpu.VMEM(rows.shape, BF),
+            pltpu.VMEM((4, 4) + rows.shape[1:], BF),
             pltpu.VMEM((4, 4, HALF, 2 * E), BF),
-            pltpu.VMEM((3, 4, HALF, 2 * E), BF),
-            pltpu.VMEM((4, HALF, 2 * E), BF),
-            pltpu.VMEM((3, HALF, 2 * E), BF),
-            pltpu.VMEM((64, 2 * K, H), F32),
-            pltpu.VMEM((64, 2 * K, H), F32),
-            pltpu.VMEM((64, 2 * K, H), BF),
-            pltpu.VMEM((3, 16, 2 * K, H), BF),
-            pltpu.VMEM((16, 2 * K, H), BF),
+            pltpu.VMEM((3, 4, FIRST, 2 * E), BF),
+            pltpu.VMEM((3, 4, rest, 2 * E), BF),
+            pltpu.VMEM((4, FIRST, 2 * E), BF),
+            pltpu.VMEM((4, rest, 2 * E), BF),
+            pltpu.VMEM((3, FIRST, 2 * E), BF),
+            pltpu.VMEM((3, rest, 2 * E), BF),
             pltpu.VMEM((3, 4, 2 * K, H), BF),
             pltpu.VMEM((4, 2 * K, H), BF),
             pltpu.VMEM((3, 1, 2 * K, H), BF),
@@ -638,14 +821,17 @@
             pltpu.VMEM((4, K, F), F32),
             pltpu.VMEM((4, K, F), F32),
             pltpu.VMEM((2, K, F), F32),
-            dma((16,)),
-            dma((2,)),
+            dma((4, 4)),
+            dma((3, 4)),
+            dma((3, 4)),
             dma((3, 4)),
             dma((3, 4)),
             dma((3,)),
             dma((3,)),
-            dma((3, 3)),
-            dma((3, 3)),
+            dma((3,)),
+            dma((3,)),
+            dma((2, 3)),
+            dma((2, 3)),
             dma((4, 3)),
             dma((4, 3)),
         ],
@@ -656,7 +842,7 @@
             flops=16 * 4 * UNIQUE_CAP * 1024 * 256, bytes_accessed=30_000_000, transcendentals=0
         ),
         name="sums",
-    )(rows, seg, wgrad, other, pg)
+    )(rows, seg, wz, pg)
 
 
 def turn_features(a):
@@ -669,40 +855,22 @@
     return a.reshape((-1, 2, 8) + rest).swapaxes(1, 2).reshape(a.shape)
 
 
-def seg_groups():
-    groups = []
-    for x in range(4):
-        groups.append([(x * 4 + y) * 8 + z * 2 for y in range(4) for z in range(4)])
-    for y in range(4):
-        groups.append([(x * 4 + y) * 8 + z * 2 + 1 for x in range(4) for z in range(4)])
-    return groups
-
-
-def spread_segments(segments):
+def cut_segments(segments):
     core = lax.axis_index("emb") % 2
     seg = segments.T.reshape(2, 4, 4, 4, 2, 128)
     along_x = seg.transpose(2, 3, 0, 1, 4, 5).reshape(16, 2, 1024)
     along_y = seg.transpose(1, 3, 0, 2, 4, 5).reshape(16, 2, 1024)
-    return lax.all_to_all(
-        jnp.where(core == 0, along_x, along_y),
-        ("fsdp", "emb"),
-        split_axis=0,
-        concat_axis=0,
-        axis_index_groups=seg_groups(),
-        tiled=True,
-    )
+    return jnp.where(core == 0, along_x, along_y)
 
 
 def on_device(pooled, projection, out_weight, cotangent, segments):
     own = turn_features(out_weight.reshape(-1, K, H)).swapaxes(0, 1)
-    weight = lax.all_gather(own, "fsdp", axis=0)
-    seg = spread_segments(segments)
     projt = turn_features(projection).T
-    xs, mixed, gram = front(pooled, projt)
+    xs, mixed, gram, weight, seg = front(pooled, projt, own, cut_segments(segments))
     wgrad, gg = middle(gram, weight, cotangent)
     wgrad = wgrad.reshape(64, 2, 2 * K, H)
-    pg, rows, other = back(xs, mixed, gg, projt, wgrad)
-    weight_grad, pg, row_grad = sums(rows, seg, wgrad, other, pg)
+    pg, rows, wz = back(xs, mixed, gg, projt, wgrad)
+    weight_grad, pg, row_grad = sums(rows, seg, wz, pg)
     return (weight_grad, unturn_features(pg.T), row_grad)
 
 

time: 319 us -> 245 us (0.77)
  Pallas kernels: 262 us -> 233 us
  waiting for transfers between devices: 21.6 us -> 0 us
  between operations: 14.1 us -> 0.71 us
  starting transfers between devices: 8.17 us -> 0 us
    pallas_call x1, Pallas kernels: 104 us -> 59.5 us  [sums(): pl.pallas_call(sums_kernel, in_specs=[any_space, whole, whole, whole], ou...]
    all_gather x1 -> x0, waiting for transfers between devices: 21.6 us -> none  [on_device(): weight = lax.all_gather(own, 'fsdp', axis=0)]
    pallas_call x1, Pallas kernels: 32 us -> 47 us  [front(): pl.pallas_call(front_kernel, grid=(batch // ROWS,), in_specs=[pl.BlockSpe...]
    all_to_all x1 -> x0, starting transfers between devices: 8.13 us -> none  [spread_segments(): lax.all_to_all(jnp.where(core == 0, along_x, along_y), ('fsdp', 'emb'), s...]
  transfers between devices with their start and end apart: 2 -> 0, of which waited for: 1 -> 0; matrix products, arithmetic and copies ran while one was open for 1% -> 0% of each run, Pallas kernels for 50% -> 0%
where the time goes in v3:
time: 245 us
  Pallas kernels  233 us (95%)
  local copies, waits for them, and re-layouts  11.2 us (5%)
    pallas_call x1, Pallas kernels, back(): pl.pallas_call(back_kernel, grid=(batch // ROWS,), in_specs=[pl.BlockSpec...  81.2 us
    pallas_call x1, Pallas kernels, sums(): pl.pallas_call(sums_kernel, in_specs=[any_space, whole, whole, whole], ou...  59.5 us
    pallas_call x1, Pallas kernels, front(): pl.pallas_call(front_kernel, grid=(batch // ROWS,), in_specs=[pl.BlockSpe...  47 us
    pallas_call x1, Pallas kernels, middle(): pl.pallas_call(middle_kernel, in_specs=[whole] * 3, out_specs=[whole] * 2...  44.8 us
    unnamed x4, local copies, waits for them, and re-layouts  5.6 us

profile of v3, /device:TPU:0, one launch (start us, length us, event | category | flops | bytes accessed | tf_op | source)
XLA Modules:
  0.0 244.6 jit_solution(8316789544079763149)
XLA Ops:
  0.6 0.9 copy.14
  1.6 0.7 copy.16
  2.3 1.1 reshape.36
  3.4 0.8 select_n.20.cut_ref
  4.2 2.0 copy.27
  6.2 47.0 %front.1 = (bf16[128,256,256]{2,1,0:T(8,128)(2,1)}, bf16[128,96,256]{2,1,0:T(8,128)(2,1)}, bf16[96,128,256]{2,1,0:T(8,128)(2,1)}, bf16[16,96,16,128]{3,2,1,0:T(8,128)(2,1)}, s32[16,2,1024]{2,1,0:T(2,128)}) custom-call(bf16[128,49152]{1,0:T(8,128)(2,1)} %x_ref.1, bf16[96,256]{1,0:T(8,128)(2,1)} %bitcast.28, bf16[96,16,128]{2,1,0:T(8,128)(2,1)} %bitcast.25, ...), custom_call_target="tpu_custom_call" | custom-call | flops 2415919104 | bytes 42000000 | tf_op jit(solution)/shard_map/front/pallas_call | solution.py:224
  53.3 44.8 %middle.1 = (f32[24576,128]{1,0:T(8,128)}, bf16[128,96,256]{2,1,0:T(8,128)(2,1)}) custom-call(bf16[96,128,256]{2,1,0:T(8,128)(2,1)} %get-tuple-element.18.gram_ref, bf16[16,96,16,128]{3,2,1,0:T(8,128)(2,1)} %get-tuple-element.19.w_ref, bf16[128,128]{1,0:T(8,128)(2,1)} %cot_ref.1), custom_call_target="tpu_custom_call" | custom-call | flops 2415919104 | bytes 33000000 | tf_op jit(solution)/shard_map/middle/pallas_call | solution.py:314
  98.1 81.2 %back.1 = (f32[96,256]{1,0:T(8,128)}, bf16[16,1024,384]{2,1,0:T(8,128)(2,1)}, bf16[16,192,128]{2,1,0:T(8,128)(2,1)}) custom-call(bf16[128,256,256]{2,1,0:T(8,128)(2,1)} %get-tuple-element.16.xs_ref, bf16[128,96,256]{2,1,0:T(8,128)(2,1)} %get-tuple-element.17.mixed_ref, bf16[128,96,256]{2,1,0:T(8,128)(2,1)} %get-tuple-element.20.gg_ref, ...), custom_call_target="tpu_custom_call" | custom-call | flops 4831838208 | bytes 42000000 | tf_op jit(solution)/shard_map/back/pallas_call | solution.py:520
  179.3 59.5 %sums.1 = (f32[192,128]{1,0:T(8,128)}, f32[96,256]{1,0:T(8,128)}, f32[1024,192]{1,0:T(8,128)}) custom-call(bf16[16,1024,384]{2,1,0:T(8,128)(2,1)} %get-tuple-element.22.rows_ref, s32[16,2,1024]{2,1,0:T(2,128)} %get-tuple-element.23.seg_ref, bf16[16,192,128]{2,1,0:T(8,128)(2,1)} %get-tuple-element.24.wz_ref, f32[96,256]{1,0:T(8,128)} %get-tuple-element.25.pg_ref), custom_call_target="tpu_custom_call" | custom-call | flops 17179869184 | bytes 30000000 | tf_op jit(solution)/shard_map/sums/pallas_call | solution.py:799
  238.8 1.0 copy.20
  239.8 0.1 copy.21
  239.9 0.7 copy.22
  240.6 2.4 copy.23
  243.1 1.5 copy.29
  (2 shorter events, 0.1 us)

commit v4 on v3

--- a/solution.py
+++ b/solution.py
@@ -148,20 +148,22 @@
         for dv, dz in plane:
             segments_to(dv, dz).start()
 
-    @pl.when(step == 2)
+    @pl.when(step == 1)
     def _():
-        for d in range(1, 4):
+        for d in (1, 3, 2):
             from_u(d).wait_recv()
             for dv in range(1, 4):
                 along_v(dv, 4 - d).start()
             to_sibling(4 - d, 0).start()
 
-    @pl.when(step == pl.num_programs(0) - 1)
-    def _():
-        for du in range(4):
-            for d in range(1, 4):
-                from_v(d, du).wait_recv()
-                to_sibling(du, 4 - d).start()
+    for when, arrived in ((3, (0,)), (6, (1, 3)), (7, (2,))):
+
+        @pl.when(step == when)
+        def _(arrived=arrived):
+            for du in arrived:
+                for d in range(1, 4):
+                    from_v(d, du).wait_recv()
+                    to_sibling(du, 4 - d).start()
 
     def spread(step, carry):
         for inner in range(8):
@@ -267,71 +269,15 @@
     )(x, projt, own, cut)
 
 
-def middle_kernel(gram_ref, w_ref, cot_ref, wgrad_ref, gg_ref, turned):
-    batch = gram_ref.shape[1]
-
-    def weight(k):
-        return w_ref[:, k].reshape(F, H)
-
-    def product(step, total):
-        for inner in range(8):
-            k = step * 8 + inner
-            total = total + jnp.dot(gram_ref[k], weight(k), preferred_element_type=F32)
-        return total
-
-    preact = lax.fori_loop(0, K // 8, product, jnp.zeros((batch, H), F32))
-    sig = jax.nn.sigmoid(preact)
-    slope = (cot_ref[...].astype(F32) * sig * (1.0 + preact * (1.0 - sig))).astype(BF)
-
-    def gradients(step, carry):
-        for inner in range(4):
-            k = step * 4 + inner
-            wgrad = lax.dot_general(gram_ref[k], slope, TN, preferred_element_type=F32)
-            for block in range(16):
-                for parity in range(2):
-                    at = block * 16 + parity * 8
-                    wgrad_ref[pl.ds(block * 8 * 2 * K + parity * K + k, 8, stride=2 * K), :] = wgrad[
-                        at : at + 8
-                    ]
-            gg = lax.dot_general(slope, weight(k), NT, preferred_element_type=F32)
-            turned[0, pl.ds(k, batch, stride=K), :] = gg[:, :128]
-            turned[1, pl.ds(k, batch, stride=K), :] = gg[:, 128:]
-        return carry
-
-    lax.fori_loop(0, K // 4, gradients, 0)
-
-    def pack(b, carry):
-        at = pl.ds(pl.multiple_of(b * K, K), K)
-        gg_ref[b] = jnp.concatenate([turned[0, at, :], turned[1, at, :]], axis=1).astype(BF)
-        return carry
-
-    lax.fori_loop(0, batch, pack, 0)
-
-
-def middle(gram, w, cot):
-    batch = gram.shape[1]
-    whole = pl.BlockSpec(memory_space=pltpu.VMEM)
-    return pl.pallas_call(
-        middle_kernel,
-        in_specs=[whole] * 3,
-        out_specs=[whole] * 2,
-        out_shape=[
-            jax.ShapeDtypeStruct((F * K, H), F32),
-            jax.ShapeDtypeStruct((batch, K, F), BF),
-        ],
-        scratch_shapes=[pltpu.VMEM((2, batch * K, 128), F32)],
-        compiler_params=pltpu.CompilerParams(vmem_limit_bytes=VMEM_LIMIT),
-        cost_estimate=pl.CostEstimate(
-            flops=6 * batch * F * K * H, bytes_accessed=33_000_000, transcendentals=batch * H
-        ),
-        name="middle",
-    )(gram, w, cot)
+CHUNKS = 8
+DEPTH = K // CHUNKS
 
 
 def back_kernel(
-    xs_ref, mixed_ref, gg_ref, projt_ref, wgrad_ref,
+    xs_ref, mixed_ref, projt_ref, gram_any, w_any, cot_ref,
     pg_ref, rows_ref, wz_ref,
-    wide, stage, own, other, w2, w2_in, send_sem, recv_sem, own_sem, pair_sem, z_send, z_recv,
+    wide, stage, gram, w, slope_ref, gg_all, turned, give, other, w2, w2_in,
+    send_sem, recv_sem, own_sem, pair_sem, z_send, z_recv, gram_sem, w_sem,
 ):
     low = lower_half(PAIRS)
     step = pl.program_id(0)
@@ -341,11 +287,17 @@
     slot = lax.rem(step, 2)
     sibling = device(x, y, z, 1 - core)
 
+    batch = gram.shape[1]
+
+    def loads(n):
+        at = pl.ds(n * DEPTH, DEPTH)
+        return (
+            pltpu.make_async_copy(gram_any.at[at], gram.at[at], gram_sem.at[n]),
+            pltpu.make_async_copy(w_any.at[:, at], w.at[:, at], w_sem.at[n]),
+        )
+
     def weight_copy():
-        return remote(wgrad_ref.at[:, 1 - core], other, pair_sem.at[0], pair_sem.at[1], sibling)
-
-    def weight_own():
-        return pltpu.make_async_copy(wgrad_ref.at[:, core], own, pair_sem.at[2])
+        return remote(give, other, pair_sem.at[0], pair_sem.at[1], sibling)
 
     def weight_z(d):
         there = turn(z, d)
@@ -403,20 +355,78 @@
             from_y = jnp.where(core == 0, y, lax.rem(y + d, 4))
             senders += [device(from_x, from_y, z, other_core) for other_core in range(2)]
             senders.append(device(x, y, turn(z, d), core))
+        for n in range(CHUNKS):
+            for copy in loads(n):
+                copy.start()
         greet(senders)
-        weight_copy().start()
-        weight_own().start()
+
+        def product(n, total):
+            for copy in loads(n):
+                copy.wait()
+            for inner in range(DEPTH):
+                k = n * DEPTH + inner
+                total = total + jnp.dot(
+                    gram[k], w[:, k].reshape(F, H), preferred_element_type=F32
+                )
+            return total
+
+        preact = lax.fori_loop(0, CHUNKS, product, jnp.zeros((batch, H), F32))
+        sig = jax.nn.sigmoid(preact)
+        slope_ref[...] = (
+            cot_ref[...].astype(F32) * sig * (1.0 + preact * (1.0 - sig))
+        ).astype(BF)
+
+        for part in range(2):
+
+            def gram_grad(turns, carry):
+                for inner in range(4):
+                    k = turns * 4 + inner
+                    gg = lax.dot_general(
+                        slope_ref[...],
+                        w[part * 8 : part * 8 + 8, k].reshape(128, H),
+                        NT,
+                        preferred_element_type=F32,
+                    )
+                    turned[pl.ds(k, batch, stride=K + 1), :] = gg
+                return carry
+
+            lax.fori_loop(0, K // 4, gram_grad, 0)
+
+            def pack_gg(turns, carry):
+                for inner in range(4):
+                    b = turns * 4 + inner
+                    gg_all[b, :, part * 128 : part * 128 + 128] = turned[
+                        pl.ds(b * (K + 1), K), :
+                    ].astype(BF)
+                return carry
+
+            lax.fori_loop(0, batch // 4, pack_gg, 0)
+
+    def weight_grads(first):
+        def one(turns, carry):
+            for inner in range(4):
+                k = first + turns * 4 + inner
+                wgrad = lax.dot_general(gram[k], slope_ref[...], TN, preferred_element_type=F32)
+                for block in range(16):
+                    for parity in range(2):
+                        at = block * 16 + parity * 8
+                        turned[
+                            pl.ds(block * 8 * (2 * K + 1) + parity * K + k, 8, stride=2 * K + 1), :
+                        ] = wgrad[at : at + 8]
+            return carry
+
+        lax.fori_loop(0, K // 8, one, 0)
 
     @pl.when(step == 2)
     def _():
-        weight_own().wait()
         weight_copy().wait_send()
         weight_copy().wait_recv()
 
         def pair_sum(n, carry):
             to_z, first, second = n // 16, (n // 4) % 4, n % 4
-            source = jnp.where(core == 0, first * 4 + second, second * 4 + first) * 4 + to_z
-            w2[to_z, n % 16] = (own[source] + other[source]).astype(BF)
+            chip = jnp.where(core == 0, first * 4 + second, second * 4 + first) * 4 + to_z
+            mine = turned[pl.ds((chip * 2 + core) * (2 * K + 1), 2 * K), :]
+            w2[to_z, n % 16] = (mine + other[chip].astype(F32)).astype(BF)
             return carry
 
         lax.fori_loop(0, 64, pair_sum, 0)
@@ -425,7 +435,7 @@
 
     def sample(b):
         xb = xs_ref[b]
-        gg = gg_ref[b]
+        gg = gg_all[step * ROWS + b]
         mg = jnp.dot(gg, xb, preferred_element_type=F32).astype(BF)
         pg = lax.dot_general(mg, xb, NT, preferred_element_type=F32)
         left = jnp.concatenate([gg, projt_ref[...]], axis=0)
@@ -474,6 +484,23 @@
         copy.start()
     own_copy(step, slot).start()
 
+    @pl.when(step == 0)
+    def _():
+        weight_grads(0)
+
+    @pl.when(step == 1)
+    def _():
+        weight_grads(K // 2)
+
+        def pack_wgrad(chip, carry):
+            give[chip] = turned[
+                pl.ds((chip * 2 + 1 - core) * (2 * K + 1), 2 * K), :
+            ].astype(BF)
+            return carry
+
+        lax.fori_loop(0, 64, pack_wgrad, 0)
+        weight_copy().start()
+
     @pl.when(step == steps - 1)
     def _():
         for block, where in ((step - 1, 1 - slot), (step, slot)):
@@ -514,7 +541,7 @@
         lax.fori_loop(0, steps, arrived, 0)
 
 
-def back(xs, mixed, gg, projt, wgrad):
+def back(xs, mixed, projt, gram, w, cot):
     batch = xs.shape[0]
     any_space = pl.BlockSpec(memory_space=pl.ANY)
     return pl.pallas_call(
@@ -523,9 +550,10 @@
         in_specs=[
             pl.BlockSpec((ROWS, F, 256), lambda i: (i, 0, 0)),
             pl.BlockSpec((ROWS, K, 256), lambda i: (i, 0, 0)),
-            pl.BlockSpec((ROWS, K, F), lambda i: (i, 0, 0)),
             pl.BlockSpec((K, F), lambda i: (0, 0)),
             any_space,
+            any_space,
+            pl.BlockSpec((batch, H), lambda i: (0, 0)),
         ],
         out_specs=[
             pl.BlockSpec((K, F), lambda i: (0, 0)),
@@ -540,25 +568,32 @@
         scratch_shapes=[
             pltpu.VMEM((F * E // 128 * ROWS, 128), F32),
             pltpu.VMEM((2, PAIRS, ROWS, 2 * E), BF),
-            pltpu.VMEM((64, 2 * K, H), F32),
-            pltpu.VMEM((64, 2 * K, H), F32),
+            pltpu.VMEM(gram.shape, BF),
+            pltpu.VMEM(w.shape, BF),
+            pltpu.VMEM((batch, H), BF),
+            pltpu.VMEM((batch, K, F), BF),
+            pltpu.VMEM((PAIRS * (2 * K + 1), H), F32),
+            pltpu.VMEM((64, 2 * K, H), BF),
+            pltpu.VMEM((64, 2 * K, H), BF),
             pltpu.VMEM((4, 16, 2 * K, H), BF),
             pltpu.VMEM((3, 16, 2 * K, H), BF),
             pltpu.SemaphoreType.DMA((2, 7)),
             pltpu.SemaphoreType.DMA((batch // ROWS, 8)),
             pltpu.SemaphoreType.DMA((2,)),
+            pltpu.SemaphoreType.DMA((2,)),
             pltpu.SemaphoreType.DMA((3,)),
             pltpu.SemaphoreType.DMA((3,)),
-            pltpu.SemaphoreType.DMA((3,)),
+            pltpu.SemaphoreType.DMA((CHUNKS,)),
+            pltpu.SemaphoreType.DMA((CHUNKS,)),
         ],
         compiler_params=pltpu.CompilerParams(
             vmem_limit_bytes=VMEM_LIMIT, collective_id=1, has_side_effects=True
         ),
         cost_estimate=pl.CostEstimate(
-            flops=8 * batch * F * E * K, bytes_accessed=42_000_000, transcendentals=0
+            flops=14 * batch * F * E * K, bytes_accessed=60_000_000, transcendentals=0
         ),
         name="back",
-    )(xs, mixed, gg, projt, wgrad)
+    )(xs, mixed, projt, gram, w, cot)
 
 
 SLOT_BLOCK = 256
@@ -867,9 +902,7 @@
     own = turn_features(out_weight.reshape(-1, K, H)).swapaxes(0, 1)
     projt = turn_features(projection).T
     xs, mixed, gram, weight, seg = front(pooled, projt, own, cut_segments(segments))
-    wgrad, gg = middle(gram, weight, cotangent)
-    wgrad = wgrad.reshape(64, 2, 2 * K, H)
-    pg, rows, wz = back(xs, mixed, gg, projt, wgrad)
+    pg, rows, wz = back(xs, mixed, projt, gram, weight, cotangent)
     weight_grad, pg, row_grad = sums(rows, seg, wz, pg)
     return (weight_grad, unturn_features(pg.T), row_grad)
 

time: 245 us -> 224 us (0.914)
  Pallas kernels: 233 us -> 211 us
    pallas_call x1 -> x0, Pallas kernels: 44.8 us -> none  [middle(): pl.pallas_call(middle_kernel, in_specs=[whole] * 3, out_specs=[whole] * 2...]
    pallas_call x1, Pallas kernels: 81.2 us -> 101 us  [back(): pl.pallas_call(back_kernel, grid=(batch // ROWS,), in_specs=[pl.BlockSpec...]
    pallas_call x1, Pallas kernels: 47 us -> 50.8 us  [front(): pl.pallas_call(front_kernel, grid=(batch // ROWS,), in_specs=[pl.BlockSpe...]
where the time goes in v4:
time: 224 us; the launch traced here: 223 us
  Pallas kernels  211 us (94%)
  local copies, waits for them, and re-layouts  11.3 us (5%)
    pallas_call x1, Pallas kernels, back(): pl.pallas_call(back_kernel, grid=(batch // ROWS,), in_specs=[pl.BlockSpec...  101 us
    pallas_call x1, Pallas kernels, sums(): pl.pallas_call(sums_kernel, in_specs=[any_space, whole, whole, whole], ou...  59.4 us
    pallas_call x1, Pallas kernels, front(): pl.pallas_call(front_kernel, grid=(batch // ROWS,), in_specs=[pl.BlockSpe...  50.8 us
    unnamed x4, local copies, waits for them, and re-layouts  5.6 us

profile of v4, /device:TPU:0, one launch (start us, length us, event | category | flops | bytes accessed | tf_op | source)
XLA Modules:
  0.0 223.2 jit_solution(15718245282257163296)
XLA Ops:
  0.6 0.9 copy.14
  1.6 0.7 copy.16
  2.3 1.1 reshape.33
  3.4 0.8 select_n.20.cut_ref
  4.2 2.0 copy.27
  6.2 50.8 %front.1 = (bf16[128,256,256]{2,1,0:T(8,128)(2,1)}, bf16[128,96,256]{2,1,0:T(8,128)(2,1)}, bf16[96,128,256]{2,1,0:T(8,128)(2,1)}, bf16[16,96,16,128]{3,2,1,0:T(8,128)(2,1)}, s32[16,2,1024]{2,1,0:T(2,128)}) custom-call(bf16[128,49152]{1,0:T(8,128)(2,1)} %x_ref.1, bf16[96,256]{1,0:T(8,128)(2,1)} %bitcast.26, bf16[96,16,128]{2,1,0:T(8,128)(2,1)} %bitcast.23, ...), custom_call_target="tpu_custom_call" | custom-call | flops 2415919104 | bytes 42000000 | tf_op jit(solution)/shard_map/front/pallas_call | solution.py:226
  57.1 100.9 %back.1 = (f32[96,256]{1,0:T(8,128)}, bf16[16,1024,384]{2,1,0:T(8,128)(2,1)}, bf16[16,192,128]{2,1,0:T(8,128)(2,1)}) custom-call(bf16[128,256,256]{2,1,0:T(8,128)(2,1)} %get-tuple-element.14.xs_ref, bf16[128,96,256]{2,1,0:T(8,128)(2,1)} %get-tuple-element.15.mixed_ref, bf16[96,256]{1,0:T(8,128)(2,1)} %bitcast.27, ...), custom_call_target="tpu_custom_call" | custom-call | flops 8455716864 | bytes 60000000 | tf_op jit(solution)/shard_map/back/pallas_call | solution.py:547
  158.0 59.4 %sums.1 = (f32[192,128]{1,0:T(8,128)}, f32[96,256]{1,0:T(8,128)}, f32[1024,192]{1,0:T(8,128)}) custom-call(bf16[16,1024,384]{2,1,0:T(8,128)(2,1)} %get-tuple-element.18.rows_ref, s32[16,2,1024]{2,1,0:T(2,128)} %get-tuple-element.19.seg_ref, bf16[16,192,128]{2,1,0:T(8,128)(2,1)} %get-tuple-element.20.wz_ref, f32[96,256]{1,0:T(8,128)} %get-tuple-element.21.pg_ref), custom_call_target="tpu_custom_call" | custom-call | flops 17179869184 | bytes 30000000 | tf_op jit(solution)/shard_map/sums/pallas_call | solution.py:834
  217.4 1.0 copy.20
  218.4 0.1 copy.21
  218.5 0.7 copy.22
  219.2 2.4 %copy.23 = f32[1024,192]{0,1:T(8,128)} copy(f32[1024,192]{1,0:T(8,128)} %get-tuple-element.30) | data formatting | bytes 1572864
  221.7 1.5 copy.29
  (2 shorter events, 0.1 us)

commit v5 on v4

--- a/solution.py
+++ b/solution.py
@@ -67,18 +67,29 @@
     )
 
 
-def front_kernel(
-    x_ref, projt_ref, own_ref, cut_ref,
-    xs_ref, mixed_ref, gram_ref, weight_ref, seg_ref,
-    wide, turned, u_send, u_recv, v_send, v_recv, s_send, s_recv, g_send, g_recv, own_sem,
+SLOTS = 3
+STEPS = 8
+
+
+def main_kernel(
+    x_ref, projt_ref, own_ref, cut_ref, cot_ref,
+    pg_ref, rows_ref, wz_ref, seg_ref,
+    wide, flat, mixed_all, gram, weight_ref, slope_ref, gg_all, turned, stage, give, other, w2_in,
+    u_send, u_recv, v_send, v_recv, s_send, s_recv, g_send, g_recv, first_sem,
+    send_sem, recv_sem, own_sem, pair_sem, z_send, z_recv,
 ):
     step = pl.program_id(0)
+    batch = gram.shape[1]
+    low = lower_half(PAIRS)
     x, y, z, core = place()
     u = jnp.where(core == 0, x, y)
     v = jnp.where(core == 0, y, x)
+    line = u
     half = pl.ds(pl.multiple_of(core * (K // 2), K // 2), K // 2)
     other_half = pl.ds(pl.multiple_of((1 - core) * (K // 2), K // 2), K // 2)
     sibling = device(x, y, z, 1 - core)
+    back = step - STEPS
+    slot = lax.rem(step + SLOTS - STEPS % SLOTS, SLOTS)
 
     def at(du, dv, dz):
         moved_u, moved_v = turn(u, du), turn(v, dv)
@@ -131,178 +142,13 @@
         there = seg_ref.at[turn(v, -dv) * 4 + turn(z, -dz)]
         return remote(there, there, g_send.at[dv, dz], g_recv.at[dv, dz], at(0, dv, dz))
 
-    plane = [(dv, dz) for dv in range(4) for dz in range(4) if dv or dz]
-    blocks = [(du, dv) for du in range(4) for dv in range(4) if du or dv]
-    weight_copy = pltpu.make_async_copy(own_ref, weight_ref.at[block(0, 0)], own_sem.at[0])
-    seg_copy = pltpu.make_async_copy(cut_ref.at[v * 4 + z], seg_ref.at[v * 4 + z], own_sem.at[1])
-
-    @pl.when(step == 0)
-    def _():
-        greet([at(d, 0, 0) for d in range(1, 4)] + [at(0, dv, dz) for dv, dz in plane] + [sibling])
-        for d in range(1, 4):
-            along_u(d).start()
-        for d in range(1, 4):
-            along_v(d, 0).start()
-        weight_copy.start()
-        seg_copy.start()
-        for dv, dz in plane:
-            segments_to(dv, dz).start()
-
-    @pl.when(step == 1)
-    def _():
-        for d in (1, 3, 2):
-            from_u(d).wait_recv()
-            for dv in range(1, 4):
-                along_v(dv, 4 - d).start()
-            to_sibling(4 - d, 0).start()
-
-    for when, arrived in ((3, (0,)), (6, (1, 3)), (7, (2,))):
-
-        @pl.when(step == when)
-        def _(arrived=arrived):
-            for du in arrived:
-                for d in range(1, 4):
-                    from_v(d, du).wait_recv()
-                    to_sibling(du, 4 - d).start()
-
-    def spread(step, carry):
-        for inner in range(8):
-            tile = step * 8 + inner
-            wide[pl.ds(pl.multiple_of(tile * ROWS, ROWS), ROWS), :] = x_ref[
-                :, pl.ds(pl.multiple_of(tile * 128, 128), 128)
-            ].astype(F32)
-        return carry
-
-    lax.fori_loop(0, F * E // 1024, spread, 0)
-    low = lower_half(PAIRS)
-
-    def sample(b):
-        a0 = wide[pl.ds(b, PAIRS, stride=3 * ROWS), :]
-        a1 = wide[pl.ds(b + ROWS, PAIRS, stride=3 * ROWS), :]
-        a2 = wide[pl.ds(b + 2 * ROWS, PAIRS, stride=3 * ROWS), :]
-        r1 = pltpu.roll(a1, 64, 1)
-        r2 = pltpu.roll(a2, 64, 1)
-        even = jnp.concatenate([a0, jnp.where(low, a1, 0.0)], axis=1)
-        odd = jnp.concatenate([jnp.where(low, r1, r2), jnp.where(low, r2, 0.0)], axis=1)
-        xb = interleave(even, odd).astype(BF)
-        xs_ref[b] = xb
-        mixed = jnp.dot(projt_ref[...], xb, preferred_element_type=F32).astype(BF)
-        mixed_ref[b] = mixed
-        gram = lax.dot_general(mixed, xb, NT, preferred_element_type=F32) * SCALE
-        turned[0, pl.ds(b, K, stride=ROWS), :] = gram[:, :128]
-        turned[1, pl.ds(b, K, stride=ROWS), :] = gram[:, 128:]
-
-    def samples(step, carry):
-        for inner in range(4):
-            sample(step * 4 + inner)
-        return carry
-
-    lax.fori_loop(0, ROWS // 4, samples, 0)
-    for part in range(2):
-        gram_ref[:, :, part * 128 : part * 128 + 128] = (
-            turned[part].reshape(K, ROWS, 128).astype(BF)
-        )
-
-    @pl.when(step == pl.num_programs(0) - 1)
-    def _():
-        for du, dv in blocks:
-            from_sibling(du, dv).wait_recv()
-            to_sibling(du, dv).wait_send()
-        for dv, dz in plane:
-            segments_from(dv, dz).wait_recv()
-            segments_to(dv, dz).wait_send()
-        for d in range(1, 4):
-            along_u(d).wait_send()
-            for du in range(4):
-                along_v(d, du).wait_send()
-        weight_copy.wait()
-        seg_copy.wait()
-
-
-def front(x, projt, own, cut):
-    batch = x.shape[0]
-    any_space = pl.BlockSpec(memory_space=pl.ANY)
-    dma = pltpu.SemaphoreType.DMA
-    return pl.pallas_call(
-        front_kernel,
-        grid=(batch // ROWS,),
-        in_specs=[
-            pl.BlockSpec((ROWS, F * E), lambda i: (i, 0)),
-            pl.BlockSpec((K, F), lambda i: (0, 0)),
-            any_space,
-            any_space,
-        ],
-        out_specs=[
-            pl.BlockSpec((ROWS, F, 256), lambda i: (i, 0, 0)),
-            pl.BlockSpec((ROWS, K, 256), lambda i: (i, 0, 0)),
-            pl.BlockSpec((K, ROWS, F), lambda i: (0, i, 0)),
-            any_space,
-            any_space,
-        ],
-        out_shape=[
-            jax.ShapeDtypeStruct((batch, F, 256), BF),
-            jax.ShapeDtypeStruct((batch, K, 256), BF),
-            jax.ShapeDtypeStruct((K, batch, F), BF),
-            jax.ShapeDtypeStruct((16,) + own.shape, BF),
-            jax.ShapeDtypeStruct(cut.shape, jnp.int32),
-        ],
-        scratch_shapes=[
-            pltpu.VMEM((F * E // 128 * ROWS, 128), F32),
-            pltpu.VMEM((2, K * ROWS, 128), F32),
-            dma((3,)),
-            dma((3,)),
-            dma((3, 4)),
-            dma((3, 4)),
-            dma((4, 4)),
-            dma((4, 4)),
-            dma((4, 4)),
-            dma((4, 4)),
-            dma((2,)),
-        ],
-        compiler_params=pltpu.CompilerParams(
-            vmem_limit_bytes=VMEM_LIMIT, collective_id=3, has_side_effects=True
-        ),
-        cost_estimate=pl.CostEstimate(
-            flops=4 * batch * F * E * K, bytes_accessed=42_000_000, transcendentals=0
-        ),
-        name="front",
-    )(x, projt, own, cut)
-
-
-CHUNKS = 8
-DEPTH = K // CHUNKS
-
-
-def back_kernel(
-    xs_ref, mixed_ref, projt_ref, gram_any, w_any, cot_ref,
-    pg_ref, rows_ref, wz_ref,
-    wide, stage, gram, w, slope_ref, gg_all, turned, give, other, w2, w2_in,
-    send_sem, recv_sem, own_sem, pair_sem, z_send, z_recv, gram_sem, w_sem,
-):
-    low = lower_half(PAIRS)
-    step = pl.program_id(0)
-    steps = pl.num_programs(0)
-    x, y, z, core = place()
-    line = jnp.where(core == 0, x, y)
-    slot = lax.rem(step, 2)
-    sibling = device(x, y, z, 1 - core)
-
-    batch = gram.shape[1]
-
-    def loads(n):
-        at = pl.ds(n * DEPTH, DEPTH)
-        return (
-            pltpu.make_async_copy(gram_any.at[at], gram.at[at], gram_sem.at[n]),
-            pltpu.make_async_copy(w_any.at[:, at], w.at[:, at], w_sem.at[n]),
-        )
-
     def weight_copy():
         return remote(give, other, pair_sem.at[0], pair_sem.at[1], sibling)
 
     def weight_z(d):
         there = turn(z, d)
         to = device(x, y, there, core)
-        return remote(w2.at[there], w2_in.at[d - 1], z_send.at[d - 1], z_recv.at[d - 1], to)
+        return remote(give.at[pl.ds(there * 16, 16)], w2_in.at[d - 1], z_send.at[d - 1], z_recv.at[d - 1], to)
 
     def copies(block, where):
         at_x = pl.ds((x * 2 + core) * 128 + block * ROWS, ROWS)
@@ -346,48 +192,112 @@
             stage.at[where, pl.ds(group * 16, 16)], rows_ref.at[:, here], own_sem.at[where]
         )
 
+    plane = [(dv, dz) for dv in range(4) for dz in range(4) if dv or dz]
+    blocks = [(du, dv) for du in range(4) for dv in range(4) if du or dv]
+    weight_copy_own = pltpu.make_async_copy(own_ref, weight_ref.at[block(0, 0)], first_sem.at[0])
+    seg_copy = pltpu.make_async_copy(cut_ref.at[v * 4 + z], seg_ref.at[v * 4 + z], first_sem.at[1])
+
+    def pass_on(arrived):
+        for du in arrived:
+            for d in range(1, 4):
+                from_v(d, du).wait_recv()
+                to_sibling(du, 4 - d).start()
+
     @pl.when(step == 0)
     def _():
         pg_ref[...] = jnp.zeros_like(pg_ref)
-        senders = [sibling]
+        senders = [at(d, 0, 0) for d in range(1, 4)] + [at(0, dv, dz) for dv, dz in plane] + [sibling]
         for d in range(1, 4):
-            from_x = jnp.where(core == 0, lax.rem(x + d, 4), x)
-            from_y = jnp.where(core == 0, y, lax.rem(y + d, 4))
-            senders += [device(from_x, from_y, z, other_core) for other_core in range(2)]
-            senders.append(device(x, y, turn(z, d), core))
-        for n in range(CHUNKS):
-            for copy in loads(n):
-                copy.start()
+            moved = turn(u, d)
+            senders.append(
+                device(jnp.where(core == 0, moved, x), jnp.where(core == 0, y, moved), z, 1 - core)
+            )
         greet(senders)
-
-        def product(n, total):
-            for copy in loads(n):
-                copy.wait()
-            for inner in range(DEPTH):
-                k = n * DEPTH + inner
-                total = total + jnp.dot(
-                    gram[k], w[:, k].reshape(F, H), preferred_element_type=F32
-                )
-            return total
-
-        preact = lax.fori_loop(0, CHUNKS, product, jnp.zeros((batch, H), F32))
-        sig = jax.nn.sigmoid(preact)
-        slope_ref[...] = (
-            cot_ref[...].astype(F32) * sig * (1.0 + preact * (1.0 - sig))
-        ).astype(BF)
-
+        for d in range(1, 4):
+            along_u(d).start()
+        for d in range(1, 4):
+            along_v(d, 0).start()
+        weight_copy_own.start()
+        seg_copy.start()
+        for dv, dz in plane:
+            segments_to(dv, dz).start()
+
+    @pl.when(step == 1)
+    def _():
+        for d in (1, 3, 2):
+            from_u(d).wait_recv()
+            for dv in range(1, 4):
+                along_v(dv, 4 - d).start()
+            to_sibling(4 - d, 0).start()
+
+    @pl.when(step == 3)
+    def _():
+        pass_on((0,))
+
+    @pl.when(step == 6)
+    def _():
+        pass_on((1, 3))
+
+    def spread(turns, carry):
+        for inner in range(8):
+            tile = turns * 8 + inner
+            wide[pl.ds(pl.multiple_of(tile * ROWS, ROWS), ROWS), :] = x_ref[
+                :, pl.ds(pl.multiple_of(tile * 128, 128), 128)
+            ].astype(F32)
+        return carry
+
+    lax.fori_loop(0, F * E // 1024, spread, 0)
+
+    def matrix(b):
+        a0 = wide[pl.ds(b, PAIRS, stride=3 * ROWS), :]
+        a1 = wide[pl.ds(b + ROWS, PAIRS, stride=3 * ROWS), :]
+        a2 = wide[pl.ds(b + 2 * ROWS, PAIRS, stride=3 * ROWS), :]
+        r1 = pltpu.roll(a1, 64, 1)
+        r2 = pltpu.roll(a2, 64, 1)
+        even = jnp.concatenate([a0, jnp.where(low, a1, 0.0)], axis=1)
+        odd = jnp.concatenate([jnp.where(low, r1, r2), jnp.where(low, r2, 0.0)], axis=1)
+        return interleave(even, odd).astype(BF)
+
+    @pl.when(step < STEPS)
+    def _():
+        def sample(b):
+            xb = matrix(b)
+            mixed = jnp.dot(projt_ref[...], xb, preferred_element_type=F32).astype(BF)
+            mixed_all[step * ROWS + b] = mixed
+            gram_b = lax.dot_general(mixed, xb, NT, preferred_element_type=F32) * SCALE
+            flat[0, pl.ds(b, K, stride=ROWS), :] = gram_b[:, :128]
+            flat[1, pl.ds(b, K, stride=ROWS), :] = gram_b[:, 128:]
+
+        def samples(turns, carry):
+            for inner in range(4):
+                sample(turns * 4 + inner)
+            return carry
+
+        lax.fori_loop(0, ROWS // 4, samples, 0)
+        rows = pl.ds(pl.multiple_of(step * ROWS, ROWS), ROWS)
         for part in range(2):
+            gram[:, rows, part * 128 : part * 128 + 128] = (
+                flat[part].reshape(K, ROWS, 128).astype(BF)
+            )
+
+    @pl.when(step == STEPS - 1)
+    def _():
+        pass_on((2,))
+
+    def gram_grads(part):
+        rows = pl.ds(part * (batch // 2), batch // 2)
+        for lanes in range(2):
 
             def gram_grad(turns, carry):
                 for inner in range(4):
                     k = turns * 4 + inner
                     gg = lax.dot_general(
-                        slope_ref[...],
-                        w[part * 8 : part * 8 + 8, k].reshape(128, H),
+                        slope_ref[rows, :],
+                        weight_ref[lanes * 8 : lanes * 8 + 8, k].reshape(128, H),
                         NT,
                         preferred_element_type=F32,
                     )
-                    turned[pl.ds(k, batch, stride=K + 1), :] = gg
+                    turned[pl.ds(k, batch // 2, stride=K + 1), :] = gg
                 return carry
 
             lax.fori_loop(0, K // 4, gram_grad, 0)
@@ -395,12 +305,12 @@
             def pack_gg(turns, carry):
                 for inner in range(4):
                     b = turns * 4 + inner
-                    gg_all[b, :, part * 128 : part * 128 + 128] = turned[
+                    gg_all[part * (batch // 2) + b, :, lanes * 128 : lanes * 128 + 128] = turned[
                         pl.ds(b * (K + 1), K), :
                     ].astype(BF)
                 return carry
 
-            lax.fori_loop(0, batch // 4, pack_gg, 0)
+            lax.fori_loop(0, batch // 8, pack_gg, 0)
 
     def weight_grads(first):
         def one(turns, carry):
@@ -417,7 +327,28 @@
 
         lax.fori_loop(0, K // 8, one, 0)
 
-    @pl.when(step == 2)
+    @pl.when(step == STEPS)
+    def _():
+        weight_copy_own.wait()
+        for du, dv in blocks:
+            from_sibling(du, dv).wait_recv()
+
+        def product(turns, total):
+            for inner in range(8):
+                k = turns * 8 + inner
+                total = total + jnp.dot(
+                    gram[k], weight_ref[:, k].reshape(F, H), preferred_element_type=F32
+                )
+            return total
+
+        preact = lax.fori_loop(0, K // 8, product, jnp.zeros((batch, H), F32))
+        sig = jax.nn.sigmoid(preact)
+        slope_ref[...] = (
+            cot_ref[...].astype(F32) * sig * (1.0 + preact * (1.0 - sig))
+        ).astype(BF)
+        gram_grads(0)
+
+    @pl.when(back == 5)
     def _():
         weight_copy().wait_send()
         weight_copy().wait_recv()
@@ -426,69 +357,75 @@
             to_z, first, second = n // 16, (n // 4) % 4, n % 4
             chip = jnp.where(core == 0, first * 4 + second, second * 4 + first) * 4 + to_z
             mine = turned[pl.ds((chip * 2 + core) * (2 * K + 1), 2 * K), :]
-            w2[to_z, n % 16] = (mine + other[chip].astype(F32)).astype(BF)
+            give[n] = (mine + other[chip].astype(F32)).astype(BF)
             return carry
 
         lax.fori_loop(0, 64, pair_sum, 0)
         for d in range(1, 4):
             weight_z(d).start()
 
-    def sample(b):
-        xb = xs_ref[b]
-        gg = gg_all[step * ROWS + b]
-        mg = jnp.dot(gg, xb, preferred_element_type=F32).astype(BF)
-        pg = lax.dot_general(mg, xb, NT, preferred_element_type=F32)
-        left = jnp.concatenate([gg, projt_ref[...]], axis=0)
-        right = jnp.concatenate([mixed_ref[b], mg], axis=0)
-        fg = lax.dot_general(left, right, TN, preferred_element_type=F32) * SCALE
-        fg = fg.reshape(16, 2, 8, 256)
-        even = fg[:, 0].reshape(PAIRS, 256)
-        odd = fg[:, 1].reshape(PAIRS, 256)
-        r0 = pltpu.roll(odd[:, :128], 64, 1)
-        r1 = pltpu.roll(odd[:, 128:], 64, 1)
-        wide[pl.ds(b, PAIRS, stride=3 * ROWS), :] = even[:, :128]
-        wide[pl.ds(b + ROWS, PAIRS, stride=3 * ROWS), :] = jnp.where(low, even[:, 128:], r0)
-        wide[pl.ds(b + 2 * ROWS, PAIRS, stride=3 * ROWS), :] = jnp.where(low, r0, r1)
-        return pg
-
-    def samples(turn, total):
-        for inner in range(4):
-            total = total + sample(turn * 4 + inner)
-        return total
-
-    pg_ref[...] += lax.fori_loop(0, ROWS // 4, samples, jnp.zeros((K, F), F32)) * SCALE
-
-    @pl.when(step >= 2)
-    def _():
-        for copy in copies(step - 2, slot):
-            copy.wait_send()
-        own_copy(step - 2, slot).wait()
-
-    def pack(q, carry):
-        for kind in range(2):
-            for last in range(4):
-                first, second = q // 4, q % 4
-                if kind == 0:
-                    owner = ((first * 4 + second) * 4 + last) * 2
-                else:
-                    owner = ((second * 4 + first) * 4 + last) * 2 + 1
-                for tile in range(3):
-                    at = pl.ds(pl.multiple_of(owner * 3 * ROWS + tile * ROWS, ROWS), ROWS)
-                    stage[slot, kind * 64 + q * 4 + last, :, tile * 128 : tile * 128 + 128] = wide[
-                        at, :
-                    ].astype(BF)
-        return carry
-
-    lax.fori_loop(0, 16, pack, 0)
-    for copy in copies(step, slot):
-        copy.start()
-    own_copy(step, slot).start()
-
-    @pl.when(step == 0)
+    @pl.when(step >= STEPS)
+    def _():
+        def sample(b):
+            xb = matrix(b)
+            gg = gg_all[back * ROWS + b]
+            mg = jnp.dot(gg, xb, preferred_element_type=F32).astype(BF)
+            pg = lax.dot_general(mg, xb, NT, preferred_element_type=F32)
+            left = jnp.concatenate([gg, projt_ref[...]], axis=0)
+            right = jnp.concatenate([mixed_all[back * ROWS + b], mg], axis=0)
+            fg = lax.dot_general(left, right, TN, preferred_element_type=F32) * SCALE
+            fg = fg.reshape(16, 2, 8, 256)
+            even = fg[:, 0].reshape(PAIRS, 256)
+            odd = fg[:, 1].reshape(PAIRS, 256)
+            r0 = pltpu.roll(odd[:, :128], 64, 1)
+            r1 = pltpu.roll(odd[:, 128:], 64, 1)
+            wide[pl.ds(b, PAIRS, stride=3 * ROWS), :] = even[:, :128]
+            wide[pl.ds(b + ROWS, PAIRS, stride=3 * ROWS), :] = jnp.where(low, even[:, 128:], r0)
+            wide[pl.ds(b + 2 * ROWS, PAIRS, stride=3 * ROWS), :] = jnp.where(low, r0, r1)
+            return pg
+
+        def samples(turns, total):
+            for inner in range(4):
+                total = total + sample(turns * 4 + inner)
+            return total
+
+        pg_ref[...] += lax.fori_loop(0, ROWS // 4, samples, jnp.zeros((K, F), F32)) * SCALE
+
+        @pl.when(back >= SLOTS)
+        def _():
+            for copy in copies(back - SLOTS, slot):
+                copy.wait_send()
+            own_copy(back - SLOTS, slot).wait()
+
+        def pack(q, carry):
+            for kind in range(2):
+                for last in range(4):
+                    first, second = q // 4, q % 4
+                    if kind == 0:
+                        owner = ((first * 4 + second) * 4 + last) * 2
+                    else:
+                        owner = ((second * 4 + first) * 4 + last) * 2 + 1
+                    for tile in range(3):
+                        at = pl.ds(pl.multiple_of(owner * 3 * ROWS + tile * ROWS, ROWS), ROWS)
+                        stage[slot, kind * 64 + q * 4 + last, :, tile * 128 : tile * 128 + 128] = wide[
+                            at, :
+                        ].astype(BF)
+            return carry
+
+        lax.fori_loop(0, 16, pack, 0)
+        for copy in copies(back, slot):
+            copy.start()
+        own_copy(back, slot).start()
+
+    @pl.when(back == 1)
+    def _():
+        gram_grads(1)
+
+    @pl.when(back == 2)
     def _():
         weight_grads(0)
 
-    @pl.when(step == 1)
+    @pl.when(back == 3)
     def _():
         weight_grads(K // 2)
 
@@ -501,17 +438,28 @@
         lax.fori_loop(0, 64, pack_wgrad, 0)
         weight_copy().start()
 
-    @pl.when(step == steps - 1)
-    def _():
-        for block, where in ((step - 1, 1 - slot), (step, slot)):
-            for copy in copies(block, where):
+    @pl.when(back == STEPS - 1)
+    def _():
+        for du, dv in blocks:
+            to_sibling(du, dv).wait_send()
+        for dv, dz in plane:
+            segments_from(dv, dz).wait_recv()
+            segments_to(dv, dz).wait_send()
+        for d in range(1, 4):
+            along_u(d).wait_send()
+            for du in range(4):
+                along_v(d, du).wait_send()
+        seg_copy.wait()
+        for ago in range(SLOTS):
+            sent, where = back - ago, lax.rem(slot + SLOTS - ago, SLOTS)
+            for copy in copies(sent, where):
                 copy.wait_send()
-            own_copy(block, where).wait()
+            own_copy(sent, where).wait()
         for d in range(1, 4):
             weight_z(d).wait_recv()
 
         def sum_z(n, carry):
-            total = w2[z, n].astype(F32) + w2_in[0, n].astype(F32)
+            total = give[z * 16 + n].astype(F32) + w2_in[0, n].astype(F32)
             total = total + (w2_in[1, n].astype(F32) + w2_in[2, n].astype(F32))
             wz_ref[n] = total.astype(BF)
             return carry
@@ -538,18 +486,18 @@
                     wait(lax.rem(line + 4 - d, 4) * 2 + other, d * 2 + other)
             return carry
 
-        lax.fori_loop(0, steps, arrived, 0)
-
-
-def back(xs, mixed, projt, gram, w, cot):
-    batch = xs.shape[0]
+        lax.fori_loop(0, STEPS, arrived, 0)
+
+
+def main(x, projt, own, cut, cot):
+    batch = x.shape[0]
     any_space = pl.BlockSpec(memory_space=pl.ANY)
+    dma = pltpu.SemaphoreType.DMA
     return pl.pallas_call(
-        back_kernel,
-        grid=(batch // ROWS,),
+        main_kernel,
+        grid=(2 * STEPS,),
         in_specs=[
-            pl.BlockSpec((ROWS, F, 256), lambda i: (i, 0, 0)),
-            pl.BlockSpec((ROWS, K, 256), lambda i: (i, 0, 0)),
+            pl.BlockSpec((ROWS, F * E), lambda i: (lax.rem(i, STEPS), 0)),
             pl.BlockSpec((K, F), lambda i: (0, 0)),
             any_space,
             any_space,
@@ -559,41 +507,51 @@
             pl.BlockSpec((K, F), lambda i: (0, 0)),
             any_space,
             pl.BlockSpec((16, 2 * K, H), lambda i: (0, 0, 0)),
+            any_space,
         ],
         out_shape=[
             jax.ShapeDtypeStruct((K, F), F32),
             jax.ShapeDtypeStruct((16, 8 * batch, 2 * E), BF),
             jax.ShapeDtypeStruct((16, 2 * K, H), BF),
+            jax.ShapeDtypeStruct(cut.shape, jnp.int32),
         ],
         scratch_shapes=[
             pltpu.VMEM((F * E // 128 * ROWS, 128), F32),
-            pltpu.VMEM((2, PAIRS, ROWS, 2 * E), BF),
-            pltpu.VMEM(gram.shape, BF),
-            pltpu.VMEM(w.shape, BF),
+            pltpu.VMEM((2, K * ROWS, 128), F32),
+            pltpu.VMEM((batch, K, 256), BF),
+            pltpu.VMEM((K, batch, F), BF),
+            pltpu.VMEM((16,) + own.shape, BF),
             pltpu.VMEM((batch, H), BF),
             pltpu.VMEM((batch, K, F), BF),
             pltpu.VMEM((PAIRS * (2 * K + 1), H), F32),
+            pltpu.VMEM((SLOTS, PAIRS, ROWS, 2 * E), BF),
             pltpu.VMEM((64, 2 * K, H), BF),
             pltpu.VMEM((64, 2 * K, H), BF),
-            pltpu.VMEM((4, 16, 2 * K, H), BF),
             pltpu.VMEM((3, 16, 2 * K, H), BF),
-            pltpu.SemaphoreType.DMA((2, 7)),
-            pltpu.SemaphoreType.DMA((batch // ROWS, 8)),
-            pltpu.SemaphoreType.DMA((2,)),
-            pltpu.SemaphoreType.DMA((2,)),
-            pltpu.SemaphoreType.DMA((3,)),
-            pltpu.SemaphoreType.DMA((3,)),
-            pltpu.SemaphoreType.DMA((CHUNKS,)),
-            pltpu.SemaphoreType.DMA((CHUNKS,)),
+            dma((3,)),
+            dma((3,)),
+            dma((3, 4)),
+            dma((3, 4)),
+            dma((4, 4)),
+            dma((4, 4)),
+            dma((4, 4)),
+            dma((4, 4)),
+            dma((2,)),
+            dma((SLOTS, 7)),
+            dma((STEPS, 8)),
+            dma((SLOTS,)),
+            dma((2,)),
+            dma((3,)),
+            dma((3,)),
         ],
         compiler_params=pltpu.CompilerParams(
             vmem_limit_bytes=VMEM_LIMIT, collective_id=1, has_side_effects=True
         ),
         cost_estimate=pl.CostEstimate(
-            flops=14 * batch * F * E * K, bytes_accessed=60_000_000, transcendentals=0
+            flops=18 * batch * F * E * K, bytes_accessed=60_000_000, transcendentals=batch * H
         ),
-        name="back",
-    )(xs, mixed, projt, gram, w, cot)
+        name="main",
+    )(x, projt, own, cut, cot)
 
 
 SLOT_BLOCK = 256
@@ -901,8 +859,7 @@
 def on_device(pooled, projection, out_weight, cotangent, segments):
     own = turn_features(out_weight.reshape(-1, K, H)).swapaxes(0, 1)
     projt = turn_features(projection).T
-    xs, mixed, gram, weight, seg = front(pooled, projt, own, cut_segments(segments))
-    pg, rows, wz = back(xs, mixed, projt, gram, weight, cotangent)
+    pg, rows, wz, seg = main(pooled, projt, own, cut_segments(segments), cotangent)
     weight_grad, pg, row_grad = sums(rows, seg, wz, pg)
     return (weight_grad, unturn_features(pg.T), row_grad)
 

time: 224 us -> 221 us (0.987)
    pallas_call x2 -> x1, Pallas kernels: 152 us -> 150 us  [main(): pl.pallas_call(main_kernel, grid=(2 * STEPS,), in_specs=[pl.BlockSpec((RO...]
where the time goes in v5:
time: 221 us
  Pallas kernels  209 us (95%)
  local copies, waits for them, and re-layouts  11.3 us (5%)
    pallas_call x1, Pallas kernels, main(): pl.pallas_call(main_kernel, grid=(2 * STEPS,), in_specs=[pl.BlockSpec((RO...  150 us
    pallas_call x1, Pallas kernels, sums(): pl.pallas_call(sums_kernel, in_specs=[any_space, whole, whole, whole], ou...  59.1 us
    unnamed x4, local copies, waits for them, and re-layouts  5.6 us

profile of v5, /device:TPU:0, one launch (start us, length us, event | category | flops | bytes accessed | tf_op | source)
XLA Modules:
  0.0 221.0 jit_solution(17757718755817329227)
XLA Ops:
  0.6 0.9 copy.14
  1.6 0.7 copy.16
  2.3 1.1 reshape.33
  3.4 0.8 select_n.20.cut_ref
  4.2 2.0 copy.27
  6.2 149.9 %main.1 = (f32[96,256]{1,0:T(8,128)}, bf16[16,1024,384]{2,1,0:T(8,128)(2,1)}, bf16[16,192,128]{2,1,0:T(8,128)(2,1)}, s32[16,2,1024]{2,1,0:T(2,128)}) custom-call(bf16[128,49152]{1,0:T(8,128)(2,1)} %x_ref.1, bf16[96,256]{1,0:T(8,128)(2,1)} %bitcast.31, bf16[96,16,128]{2,1,0:T(8,128)(2,1)} %bitcast.26, s32[16,2,1024]{2,1,0:T(2,128)} %select_n.20.cut_ref, ...), custom_call_target="tpu_custom_call" | custom-call | flops 10871635968 | bytes 60000000 | tf_op jit(solution)/shard_map/main/pallas_call | solution.py:496
  156.2 59.1 %sums.1 = (f32[192,128]{1,0:T(8,128)}, f32[96,256]{1,0:T(8,128)}, f32[1024,192]{1,0:T(8,128)}) custom-call(bf16[16,1024,384]{2,1,0:T(8,128)(2,1)} %get-tuple-element.10.rows_ref, s32[16,2,1024]{2,1,0:T(2,128)} %get-tuple-element.11.seg_ref, bf16[16,192,128]{2,1,0:T(8,128)(2,1)} %get-tuple-element.12.wz_ref, f32[96,256]{1,0:T(8,128)} %get-tuple-element.13.pg_ref), custom_call_target="tpu_custom_call" | custom-call | flops 17179869184 | bytes 30000000 | tf_op jit(solution)/shard_map/sums/pallas_call | solution.py:792
  215.3 1.0 copy.20
  216.2 0.1 copy.21
  216.3 0.7 copy.22
  217.1 2.4 %copy.23 = f32[1024,192]{0,1:T(8,128)} copy(f32[1024,192]{1,0:T(8,128)} %get-tuple-element.22) | data formatting | bytes 1572864
  219.5 1.5 copy.29
  (2 shorter events, 0.1 us)

commit v6 on v5

--- a/solution.py
+++ b/solution.py
@@ -68,13 +68,14 @@
 
 
 SLOTS = 3
+PAD = ROWS + 1
 STEPS = 8
 
 
 def main_kernel(
     x_ref, projt_ref, own_ref, cut_ref, cot_ref,
     pg_ref, rows_ref, wz_ref, seg_ref,
-    wide, flat, mixed_all, gram, weight_ref, slope_ref, gg_all, turned, stage, give, other, w2_in,
+    wide, ready, mixed_all, gram, weight_ref, slope_ref, gg_all, turned, stage, give, other, w2_in,
     u_send, u_recv, v_send, v_recv, s_send, s_recv, g_send, g_recv, first_sem,
     send_sem, recv_sem, own_sem, pair_sem, z_send, z_recv,
 ):
@@ -260,57 +261,62 @@
 
     @pl.when(step < STEPS)
     def _():
-        def sample(b):
-            xb = matrix(b)
-            mixed = jnp.dot(projt_ref[...], xb, preferred_element_type=F32).astype(BF)
-            mixed_all[step * ROWS + b] = mixed
-            gram_b = lax.dot_general(mixed, xb, NT, preferred_element_type=F32) * SCALE
-            flat[0, pl.ds(b, K, stride=ROWS), :] = gram_b[:, :128]
-            flat[1, pl.ds(b, K, stride=ROWS), :] = gram_b[:, 128:]
-
         def samples(turns, carry):
-            for inner in range(4):
-                sample(turns * 4 + inner)
+            group = [turns * 4 + inner for inner in range(4)]
+            xs = [matrix(b) for b in group]
+            mixed = [
+                jnp.dot(projt_ref[...], xb, preferred_element_type=F32).astype(BF) for xb in xs
+            ]
+            grams = [
+                lax.dot_general(m, xb, NT, preferred_element_type=F32) * SCALE
+                for m, xb in zip(mixed, xs)
+            ]
+            for b, m, gram_b in zip(group, mixed, grams):
+                mixed_all[step * ROWS + b] = m
+                turned[pl.ds(b, K, stride=PAD), :] = gram_b[:, :128]
+                turned[pl.ds(K * PAD + b, K, stride=PAD), :] = gram_b[:, 128:]
             return carry
 
         lax.fori_loop(0, ROWS // 4, samples, 0)
         rows = pl.ds(pl.multiple_of(step * ROWS, ROWS), ROWS)
-        for part in range(2):
-            gram[:, rows, part * 128 : part * 128 + 128] = (
-                flat[part].reshape(K, ROWS, 128).astype(BF)
-            )
+
+        def pack_gram(turns, carry):
+            for inner in range(8):
+                k = turns * 8 + inner
+                for part in range(2):
+                    at = pl.ds((part * K + k) * PAD, ROWS)
+                    gram[k, rows, part * 128 : part * 128 + 128] = turned[at, :].astype(BF)
+            return carry
+
+        lax.fori_loop(0, K // 8, pack_gram, 0)
 
     @pl.when(step == STEPS - 1)
     def _():
         pass_on((2,))
 
-    def gram_grads(part):
-        rows = pl.ds(part * (batch // 2), batch // 2)
-        for lanes in range(2):
-
-            def gram_grad(turns, carry):
-                for inner in range(4):
-                    k = turns * 4 + inner
-                    gg = lax.dot_general(
-                        slope_ref[rows, :],
-                        weight_ref[lanes * 8 : lanes * 8 + 8, k].reshape(128, H),
-                        NT,
-                        preferred_element_type=F32,
-                    )
-                    turned[pl.ds(k, batch // 2, stride=K + 1), :] = gg
-                return carry
-
-            lax.fori_loop(0, K // 4, gram_grad, 0)
-
-            def pack_gg(turns, carry):
-                for inner in range(4):
-                    b = turns * 4 + inner
-                    gg_all[part * (batch // 2) + b, :, lanes * 128 : lanes * 128 + 128] = turned[
-                        pl.ds(b * (K + 1), K), :
+    def gram_grads():
+        def gram_grad(turns, carry):
+            for inner in range(4):
+                k = turns * 4 + inner
+                gg = lax.dot_general(
+                    slope_ref[...], weight_ref[:, k].reshape(F, H), NT, preferred_element_type=F32
+                )
+                turned[pl.ds(k, batch, stride=K + 1), :] = gg[:, :128]
+                turned[pl.ds(batch * (K + 1) + k, batch, stride=K + 1), :] = gg[:, 128:]
+            return carry
+
+        lax.fori_loop(0, K // 4, gram_grad, 0)
+
+        def pack_gg(turns, carry):
+            for inner in range(4):
+                b = turns * 4 + inner
+                for part in range(2):
+                    gg_all[b, :, part * 128 : part * 128 + 128] = turned[
+                        pl.ds((part * batch + b) * (K + 1), K), :
                     ].astype(BF)
-                return carry
-
-            lax.fori_loop(0, batch // 8, pack_gg, 0)
+            return carry
+
+        lax.fori_loop(0, batch // 4, pack_gg, 0)
 
     def weight_grads(first):
         def one(turns, carry):
@@ -346,9 +352,9 @@
         slope_ref[...] = (
             cot_ref[...].astype(F32) * sig * (1.0 + preact * (1.0 - sig))
         ).astype(BF)
-        gram_grads(0)
-
-    @pl.when(back == 5)
+        gram_grads()
+
+    @pl.when(back == 2)
     def _():
         weight_copy().wait_send()
         weight_copy().wait_recv()
@@ -366,27 +372,27 @@
 
     @pl.when(step >= STEPS)
     def _():
-        def sample(b):
-            xb = matrix(b)
-            gg = gg_all[back * ROWS + b]
-            mg = jnp.dot(gg, xb, preferred_element_type=F32).astype(BF)
-            pg = lax.dot_general(mg, xb, NT, preferred_element_type=F32)
-            left = jnp.concatenate([gg, projt_ref[...]], axis=0)
-            right = jnp.concatenate([mixed_all[back * ROWS + b], mg], axis=0)
-            fg = lax.dot_general(left, right, TN, preferred_element_type=F32) * SCALE
-            fg = fg.reshape(16, 2, 8, 256)
-            even = fg[:, 0].reshape(PAIRS, 256)
-            odd = fg[:, 1].reshape(PAIRS, 256)
-            r0 = pltpu.roll(odd[:, :128], 64, 1)
-            r1 = pltpu.roll(odd[:, 128:], 64, 1)
-            wide[pl.ds(b, PAIRS, stride=3 * ROWS), :] = even[:, :128]
-            wide[pl.ds(b + ROWS, PAIRS, stride=3 * ROWS), :] = jnp.where(low, even[:, 128:], r0)
-            wide[pl.ds(b + 2 * ROWS, PAIRS, stride=3 * ROWS), :] = jnp.where(low, r0, r1)
-            return pg
-
         def samples(turns, total):
-            for inner in range(4):
-                total = total + sample(turns * 4 + inner)
+            group = [turns * 4 + inner for inner in range(4)]
+            xs = [matrix(b) for b in group]
+            ggs = [gg_all[back * ROWS + b] for b in group]
+            mgs = [
+                jnp.dot(gg, xb, preferred_element_type=F32).astype(BF) for gg, xb in zip(ggs, xs)
+            ]
+            for mg, xb in zip(mgs, xs):
+                total = total + lax.dot_general(mg, xb, NT, preferred_element_type=F32)
+            for b, gg, mg in zip(group, ggs, mgs):
+                left = jnp.concatenate([gg, projt_ref[...]], axis=0)
+                right = jnp.concatenate([mixed_all[back * ROWS + b], mg], axis=0)
+                fg = lax.dot_general(left, right, TN, preferred_element_type=F32) * SCALE
+                fg = fg.reshape(16, 2, 8, 256)
+                even = fg[:, 0].reshape(PAIRS, 256)
+                odd = fg[:, 1].reshape(PAIRS, 256)
+                r0 = pltpu.roll(odd[:, :128], 64, 1)
+                r1 = pltpu.roll(odd[:, 128:], 64, 1)
+                ready[pl.ds(b, PAIRS, stride=3 * PAD), :] = even[:, :128]
+                ready[pl.ds(b + PAD, PAIRS, stride=3 * PAD), :] = jnp.where(low, even[:, 128:], r0)
+                ready[pl.ds(b + 2 * PAD, PAIRS, stride=3 * PAD), :] = jnp.where(low, r0, r1)
             return total
 
         pg_ref[...] += lax.fori_loop(0, ROWS // 4, samples, jnp.zeros((K, F), F32)) * SCALE
@@ -406,8 +412,8 @@
                     else:
                         owner = ((second * 4 + first) * 4 + last) * 2 + 1
                     for tile in range(3):
-                        at = pl.ds(pl.multiple_of(owner * 3 * ROWS + tile * ROWS, ROWS), ROWS)
-                        stage[slot, kind * 64 + q * 4 + last, :, tile * 128 : tile * 128 + 128] = wide[
+                        at = pl.ds((owner * 3 + tile) * PAD, ROWS)
+                        stage[slot, kind * 64 + q * 4 + last, :, tile * 128 : tile * 128 + 128] = ready[
                             at, :
                         ].astype(BF)
             return carry
@@ -417,15 +423,11 @@
             copy.start()
         own_copy(back, slot).start()
 
+    @pl.when(back == 0)
+    def _():
+        weight_grads(0)
+
     @pl.when(back == 1)
-    def _():
-        gram_grads(1)
-
-    @pl.when(back == 2)
-    def _():
-        weight_grads(0)
-
-    @pl.when(back == 3)
     def _():
         weight_grads(K // 2)
 
@@ -517,13 +519,13 @@
         ],
         scratch_shapes=[
             pltpu.VMEM((F * E // 128 * ROWS, 128), F32),
-            pltpu.VMEM((2, K * ROWS, 128), F32),
+            pltpu.VMEM((3 * PAIRS * PAD, 128), F32),
             pltpu.VMEM((batch, K, 256), BF),
             pltpu.VMEM((K, batch, F), BF),
             pltpu.VMEM((16,) + own.shape, BF),
             pltpu.VMEM((batch, H), BF),
             pltpu.VMEM((batch, K, F), BF),
-            pltpu.VMEM((PAIRS * (2 * K + 1), H), F32),
+            pltpu.VMEM((2 * batch * (K + 1), H), F32),
             pltpu.VMEM((SLOTS, PAIRS, ROWS, 2 * E), BF),
             pltpu.VMEM((64, 2 * K, H), BF),
             pltpu.VMEM((64, 2 * K, H), BF),

time: 221 us -> 211 us (0.955)
  Pallas kernels: 209 us -> 199 us
    pallas_call x1, Pallas kernels: 150 us -> 139 us  [main(): pl.pallas_call(main_kernel, grid=(2 * STEPS,), in_specs=[pl.BlockSpec((RO...]
where the time goes in v6:
time: 211 us
  Pallas kernels  199 us (94%)
  local copies, waits for them, and re-layouts  11.3 us (5%)
    pallas_call x1, Pallas kernels, main(): pl.pallas_call(main_kernel, grid=(2 * STEPS,), in_specs=[pl.BlockSpec((RO...  139 us
    pallas_call x1, Pallas kernels, sums(): pl.pallas_call(sums_kernel, in_specs=[any_space, whole, whole, whole], ou...  59.6 us
    unnamed x4, local copies, waits for them, and re-layouts  5.6 us

profile of v6, /device:TPU:0, one launch (start us, length us, event | category | flops | bytes accessed | tf_op | source)
XLA Modules:
  0.0 210.5 jit_solution(8313038366365019108)
XLA Ops:
  0.6 0.9 copy.14
  1.6 0.7 copy.16
  2.3 1.1 reshape.33
  3.4 0.8 select_n.20.cut_ref
  4.2 2.0 copy.27
  6.2 138.9 %main.1 = (f32[96,256]{1,0:T(8,128)}, bf16[16,1024,384]{2,1,0:T(8,128)(2,1)}, bf16[16,192,128]{2,1,0:T(8,128)(2,1)}, s32[16,2,1024]{2,1,0:T(2,128)}) custom-call(bf16[128,49152]{1,0:T(8,128)(2,1)} %x_ref.1, bf16[96,256]{1,0:T(8,128)(2,1)} %bitcast.31, bf16[96,16,128]{2,1,0:T(8,128)(2,1)} %bitcast.26, s32[16,2,1024]{2,1,0:T(2,128)} %select_n.20.cut_ref, ...), custom_call_target="tpu_custom_call" | custom-call | flops 10871635968 | bytes 60000000 | tf_op jit(solution)/shard_map/main/pallas_call | solution.py:498
  145.2 59.6 %sums.1 = (f32[192,128]{1,0:T(8,128)}, f32[96,256]{1,0:T(8,128)}, f32[1024,192]{1,0:T(8,128)}) custom-call(bf16[16,1024,384]{2,1,0:T(8,128)(2,1)} %get-tuple-element.10.rows_ref, s32[16,2,1024]{2,1,0:T(2,128)} %get-tuple-element.11.seg_ref, bf16[16,192,128]{2,1,0:T(8,128)(2,1)} %get-tuple-element.12.wz_ref, f32[96,256]{1,0:T(8,128)} %get-tuple-element.13.pg_ref), custom_call_target="tpu_custom_call" | custom-call | flops 17179869184 | bytes 30000000 | tf_op jit(solution)/shard_map/sums/pallas_call | solution.py:794
  204.8 1.0 copy.20
  205.7 0.1 copy.21
  205.8 0.7 copy.22
  206.6 2.4 %copy.23 = f32[1024,192]{0,1:T(8,128)} copy(f32[1024,192]{1,0:T(8,128)} %get-tuple-element.22) | data formatting | bytes 1572864
  209.0 1.5 copy.29
  (2 shorter events, 0.1 us)

commit v7 on v6

--- a/solution.py
+++ b/solution.py
@@ -28,6 +28,13 @@
     return both.reshape(F, width)
 
 
+def reorder(dtype):
+    column = lax.broadcasted_iota(jnp.int32, (F, F), 1)
+    within = column & 15
+    natural = (column - within) + (within & 7) * 2 + (within >> 3)
+    return jnp.where(lax.broadcasted_iota(jnp.int32, (F, F), 0) == natural, 1.0, 0.0).astype(dtype)
+
+
 def lower_half(rows):
     return lax.broadcasted_iota(jnp.int32, (rows, 128), 1) < 64
 
@@ -73,9 +80,9 @@
 
 
 def main_kernel(
-    x_ref, projt_ref, own_ref, cut_ref, cot_ref,
+    x_ref, natural_ref, own_ref, cut_ref, cot_ref,
     pg_ref, rows_ref, wz_ref, seg_ref,
-    wide, ready, mixed_all, gram, weight_ref, slope_ref, gg_all, turned, stage, give, other, w2_in,
+    projt_ref, wide, ready, mixed_all, gram, weight_ref, slope_ref, gg_all, turned, stage, give, other, w2_in,
     u_send, u_recv, v_send, v_recv, s_send, s_recv, g_send, g_recv, first_sem,
     send_sem, recv_sem, own_sem, pair_sem, z_send, z_recv,
 ):
@@ -133,15 +140,31 @@
         there = weight_ref.at[first * 4 + second, other_half]
         return remote(there, there, s_send.at[du, dv % 4], s_recv.at[du, dv % 4], sibling)
 
+    def segment_parts(dv, dz):
+        to_v, to_z = turn(v, dv), turn(z, dz)
+        for along in range(4):
+            chip = jnp.where(core == 0, along * 4 + to_v, to_v * 4 + along) * 4 + to_z
+            source = cut_ref.at[:, pl.ds(pl.multiple_of(chip * 256, 256), 256)]
+            yield along, source, seg_ref.at[v * 4 + z, :, pl.ds(along * 256, 256)]
+
     def segments_to(dv, dz):
-        there = turn(v, dv) * 4 + turn(z, dz)
-        return remote(
-            cut_ref.at[there], seg_ref.at[v * 4 + z], g_send.at[dv, dz], g_recv.at[dv, dz], at(0, dv, dz)
-        )
+        return [
+            remote(source, there, g_send.at[dv, dz, n], g_recv.at[dv, dz, n], at(0, dv, dz))
+            for n, source, there in segment_parts(dv, dz)
+        ]
 
     def segments_from(dv, dz):
-        there = seg_ref.at[turn(v, -dv) * 4 + turn(z, -dz)]
-        return remote(there, there, g_send.at[dv, dz], g_recv.at[dv, dz], at(0, dv, dz))
+        found = []
+        for n in range(4):
+            there = seg_ref.at[turn(v, -dv) * 4 + turn(z, -dz), :, pl.ds(n * 256, 256)]
+            found.append(remote(there, there, g_send.at[dv, dz, n], g_recv.at[dv, dz, n], at(0, dv, dz)))
+        return found
+
+    def segments_own():
+        return [
+            pltpu.make_async_copy(source, there, g_send.at[0, 0, n])
+            for n, source, there in segment_parts(0, 0)
+        ]
 
     def weight_copy():
         return remote(give, other, pair_sem.at[0], pair_sem.at[1], sibling)
@@ -196,7 +219,6 @@
     plane = [(dv, dz) for dv in range(4) for dz in range(4) if dv or dz]
     blocks = [(du, dv) for du in range(4) for dv in range(4) if du or dv]
     weight_copy_own = pltpu.make_async_copy(own_ref, weight_ref.at[block(0, 0)], first_sem.at[0])
-    seg_copy = pltpu.make_async_copy(cut_ref.at[v * 4 + z], seg_ref.at[v * 4 + z], first_sem.at[1])
 
     def pass_on(arrived):
         for du in arrived:
@@ -207,6 +229,9 @@
     @pl.when(step == 0)
     def _():
         pg_ref[...] = jnp.zeros_like(pg_ref)
+        projt_ref[...] = jnp.dot(
+            natural_ref[...], reorder(BF), preferred_element_type=F32
+        ).astype(BF)
         senders = [at(d, 0, 0) for d in range(1, 4)] + [at(0, dv, dz) for dv, dz in plane] + [sibling]
         for d in range(1, 4):
             moved = turn(u, d)
@@ -219,9 +244,6 @@
         for d in range(1, 4):
             along_v(d, 0).start()
         weight_copy_own.start()
-        seg_copy.start()
-        for dv, dz in plane:
-            segments_to(dv, dz).start()
 
     @pl.when(step == 1)
     def _():
@@ -230,6 +252,14 @@
             for dv in range(1, 4):
                 along_v(dv, 4 - d).start()
             to_sibling(4 - d, 0).start()
+
+    @pl.when(step == 2)
+    def _():
+        for copy in segments_own():
+            copy.start()
+        for dv, dz in plane:
+            for copy in segments_to(dv, dz):
+                copy.start()
 
     @pl.when(step == 3)
     def _():
@@ -445,13 +475,16 @@
         for du, dv in blocks:
             to_sibling(du, dv).wait_send()
         for dv, dz in plane:
-            segments_from(dv, dz).wait_recv()
-            segments_to(dv, dz).wait_send()
+            for copy in segments_from(dv, dz):
+                copy.wait_recv()
+            for copy in segments_to(dv, dz):
+                copy.wait_send()
         for d in range(1, 4):
             along_u(d).wait_send()
             for du in range(4):
                 along_v(d, du).wait_send()
-        seg_copy.wait()
+        for copy in segments_own():
+            copy.wait()
         for ago in range(SLOTS):
             sent, where = back - ago, lax.rem(slot + SLOTS - ago, SLOTS)
             for copy in copies(sent, where):
@@ -515,9 +548,10 @@
             jax.ShapeDtypeStruct((K, F), F32),
             jax.ShapeDtypeStruct((16, 8 * batch, 2 * E), BF),
             jax.ShapeDtypeStruct((16, 2 * K, H), BF),
-            jax.ShapeDtypeStruct(cut.shape, jnp.int32),
+            jax.ShapeDtypeStruct((16, 2, 8 * batch), jnp.int32),
         ],
         scratch_shapes=[
+            pltpu.VMEM((K, F), BF),
             pltpu.VMEM((F * E // 128 * ROWS, 128), F32),
             pltpu.VMEM((3 * PAIRS * PAD, 128), F32),
             pltpu.VMEM((batch, K, 256), BF),
@@ -536,9 +570,9 @@
             dma((3, 4)),
             dma((4, 4)),
             dma((4, 4)),
-            dma((4, 4)),
-            dma((4, 4)),
-            dma((2,)),
+            dma((4, 4, 4)),
+            dma((4, 4, 4)),
+            dma((1,)),
             dma((SLOTS, 7)),
             dma((STEPS, 8)),
             dma((SLOTS,)),
@@ -726,18 +760,20 @@
     p0 = start(spread(pu, u, 0, at_u))
     s3 = start(w_copies(wz_ref, w3_in, 0, at_u, u, 4))
     tables(1)
+    tables(2)
     pv[v] = gathered(pu, u, 0, at_u)
     p1 = start(spread(pv, v, 1, at_v))
     for copy in s3:
         copy.wait_recv()
     add_four(wz_ref.at[pl.ds(u * 4, 4)], w3_in.at[0], w3_in.at[1], w3_in.at[2], w4, 1)
     s4 = start(w_copies(w4, w4_in, 1, at_v, v, 1))
-    tables(2)
     total_b(1)
+    tables(3)
     pz[z] = gathered(pv, v, 1, at_v)
     p2 = start(spread(pz, z, 2, at_z))
-    tables(3)
     total_b(2)
+    tables(0)
+    total_b(3)
     pc[core] = gathered(pz, z, 2, at_z)
     p3 = remote(pc.at[core], pc.at[core], p_send.at[3, 0], p_recv.at[3, 0], sibling)
     p3.start()
@@ -745,29 +781,34 @@
         copy.wait_recv()
     total = w4[v].astype(F32) + w4_in[0, 0].astype(F32)
     wout_ref[...] = total + (w4_in[1, 0].astype(F32) + w4_in[2, 0].astype(F32))
-    tables(0)
-    total_b(3)
     for dv in ORDER:
         total_a(dv)
     total_b(0)
     remote(pc.at[1 - core], pc.at[1 - core], p_send.at[3, 0], p_recv.at[3, 0], sibling).wait_recv()
-    pout_ref[...] = pc[0] + pc[1]
+    pout_ref[...] = lax.dot_general(
+        pc[0] + pc[1],
+        reorder(F32),
+        NT,
+        precision=lax.Precision.HIGHEST,
+        preferred_element_type=F32,
+    )
 
     def finish(mine, others, start_row, rows):
         def one(part, carry):
-            at = pl.ds(pl.multiple_of(part * 64, 64), 64)
-            before = pl.ds(pl.multiple_of(part * 64 + start_row, 64), 64)
-            after = pl.ds(pl.multiple_of(part * 64 + start_row + HALF, 64), 64)
+            at = pl.ds(pl.multiple_of(part * 128, 128), 128)
+            before = pl.ds(pl.multiple_of(part * 128 + start_row, 128), 128)
+            after = pl.ds(pl.multiple_of(part * 128 + start_row + HALF, 128), 128)
             total = mine[at, :].astype(F32) + others[0, at].astype(F32)
             total = total + (others[1, at].astype(F32) + others[2, at].astype(F32))
-            out_ref[before, :] = total[:, :E]
             r1 = pltpu.roll(total[:, 128:256], 64, 1)
             r2 = pltpu.roll(total[:, 256:], 64, 1)
-            out_ref[after, :128] = jnp.where(lower_half(64), r1, r2)
-            out_ref[after, 128:] = r2[:, :64]
-            return carry
-
-        lax.fori_loop(0, rows // 64, one, 0)
+            out_ref[:128, before] = total[:, :128].T
+            out_ref[128:, before] = total[:, 128:256].T[:64]
+            out_ref[:128, after] = jnp.where(lower_half(128), r1, r2).T
+            out_ref[128:, after] = r2.T[:64]
+            return carry
+
+        lax.fori_loop(0, rows // 128, one, 0)
 
     for d in range(1, 4):
         second_a(d).wait_recv()
@@ -798,7 +839,7 @@
         out_shape=[
             jax.ShapeDtypeStruct((2 * K, H), F32),
             jax.ShapeDtypeStruct((K, F), F32),
-            jax.ShapeDtypeStruct((UNIQUE_CAP, E), F32),
+            jax.ShapeDtypeStruct((E, UNIQUE_CAP), F32),
         ],
         scratch_shapes=[
             pltpu.VMEM((4, 4) + rows.shape[1:], BF),
@@ -845,25 +886,11 @@
     return a.reshape((-1, 8, 2) + rest).swapaxes(1, 2).reshape(a.shape)
 
 
-def unturn_features(a):
-    rest = a.shape[1:]
-    return a.reshape((-1, 2, 8) + rest).swapaxes(1, 2).reshape(a.shape)
-
-
-def cut_segments(segments):
-    core = lax.axis_index("emb") % 2
-    seg = segments.T.reshape(2, 4, 4, 4, 2, 128)
-    along_x = seg.transpose(2, 3, 0, 1, 4, 5).reshape(16, 2, 1024)
-    along_y = seg.transpose(1, 3, 0, 2, 4, 5).reshape(16, 2, 1024)
-    return jnp.where(core == 0, along_x, along_y)
-
-
 def on_device(pooled, projection, out_weight, cotangent, segments):
     own = turn_features(out_weight.reshape(-1, K, H)).swapaxes(0, 1)
-    projt = turn_features(projection).T
-    pg, rows, wz, seg = main(pooled, projt, own, cut_segments(segments), cotangent)
+    pg, rows, wz, seg = main(pooled, projection.T, own, segments.T, cotangent)
     weight_grad, pg, row_grad = sums(rows, seg, wz, pg)
-    return (weight_grad, unturn_features(pg.T), row_grad)
+    return (weight_grad, pg.T, row_grad.T)
 
 
 def solution(mesh):

time: 211 us -> 199 us (0.943)
  Pallas kernels: 199 us -> 191 us
  local copies, waits for them, and re-layouts: 11.3 us -> 7.17 us
    pallas_call x1, Pallas kernels: 59.6 us -> 51.3 us  [sums(): pl.pallas_call(sums_kernel, in_specs=[any_space, whole, whole, whole], ou...]
    unnamed x4 -> x3, local copies, waits for them, and re-layouts: 5.6 us -> 5.17 us
where the time goes in v7:
time: 199 us; the launch traced here: 198 us
  Pallas kernels  191 us (96%)
  local copies, waits for them, and re-layouts  7.17 us (4%)
    pallas_call x1, Pallas kernels, main(): pl.pallas_call(main_kernel, grid=(2 * STEPS,), in_specs=[pl.BlockSpec((RO...  139 us
    pallas_call x1, Pallas kernels, sums(): pl.pallas_call(sums_kernel, in_specs=[any_space, whole, whole, whole], ou...  51.3 us
    unnamed x3, local copies, waits for them, and re-layouts  5.17 us

profile of v7, /device:TPU:0, one launch (start us, length us, event | category | flops | bytes accessed | tf_op | source)
XLA Modules:
  0.0 198.5 jit_solution(4152197638691289792)
XLA Ops:
  0.6 2.0 %copy.10 = bf16[1,8,2,96,128]{4,1,2,3,0:T(8,128)(2,1)} copy(bf16[1,8,2,96,128]{4,3,2,1,0:T(8,128)(2,1)} %bitcast.13) | data formatting | bytes 786432 | tf_op jit(solution)/shard_map/reshape;reshape | solution.py:886
  2.6 139.4 %main.1 = (f32[96,256]{1,0:T(8,128)}, bf16[16,1024,384]{2,1,0:T(8,128)(2,1)}, bf16[16,192,128]{2,1,0:T(8,128)(2,1)}, s32[16,2,1024]{2,1,0:T(2,128)}) custom-call(bf16[128,49152]{1,0:T(8,128)(2,1)} %x_ref.1, bf16[96,256]{1,0:T(8,128)(2,1)} %bitcast.17, bf16[96,16,128]{2,1,0:T(8,128)(2,1)} %bitcast.14, s32[2,16384]{1,0:T(2,128)} %bitcast.16, ...), custom_call_target="tpu_custom_call" | custom-call | flops 10871635968 | bytes 60000000 | tf_op jit(solution)/shard_map/main/pallas_call | solution.py:531
  142.1 51.3 %sums.1 = (f32[192,128]{1,0:T(8,128)}, f32[96,256]{1,0:T(8,128)}, f32[192,1024]{1,0:T(8,128)}) custom-call(bf16[16,1024,384]{2,1,0:T(8,128)(2,1)} %get-tuple-element.10.rows_ref, s32[16,2,1024]{2,1,0:T(2,128)} %get-tuple-element.11.seg_ref, bf16[16,192,128]{2,1,0:T(8,128)(2,1)} %get-tuple-element.12.wz_ref, f32[96,256]{1,0:T(8,128)} %get-tuple-element.13.pg_ref), custom_call_target="tpu_custom_call" | custom-call | flops 17179869184 | bytes 30000000 | tf_op jit(solution)/shard_map/sums/pallas_call | solution.py:835
  193.3 1.5 copy.14
  194.9 1.5 copy.15
  196.4 2.1 %copy.16 = f32[1024,192]{0,1:T(8,128)} copy(f32[1024,192]{0,1:T(8,128)} %bitcast.12) | data formatting | bytes 1572864

commit v8 on v7

--- a/solution.py
+++ b/solution.py
@@ -178,7 +178,7 @@
         at_x = pl.ds((x * 2 + core) * 128 + block * ROWS, ROWS)
         at_y = pl.ds((y * 2 + core) * 128 + block * ROWS, ROWS)
         found = []
-        for d in range(1, 4):
+        for d in (2, 1, 3):
             tx = lax.rem(x + d, 4)
             ty = lax.rem(y + d, 4)
             for kind, group, rows, target in (
@@ -384,22 +384,6 @@
         ).astype(BF)
         gram_grads()
 
-    @pl.when(back == 2)
-    def _():
-        weight_copy().wait_send()
-        weight_copy().wait_recv()
-
-        def pair_sum(n, carry):
-            to_z, first, second = n // 16, (n // 4) % 4, n % 4
-            chip = jnp.where(core == 0, first * 4 + second, second * 4 + first) * 4 + to_z
-            mine = turned[pl.ds((chip * 2 + core) * (2 * K + 1), 2 * K), :]
-            give[n] = (mine + other[chip].astype(F32)).astype(BF)
-            return carry
-
-        lax.fori_loop(0, 64, pair_sum, 0)
-        for d in range(1, 4):
-            weight_z(d).start()
-
     @pl.when(step >= STEPS)
     def _():
         def samples(turns, total):
@@ -469,6 +453,22 @@
 
         lax.fori_loop(0, 64, pack_wgrad, 0)
         weight_copy().start()
+
+    @pl.when(back == 2)
+    def _():
+        weight_copy().wait_send()
+        weight_copy().wait_recv()
+
+        def pair_sum(n, carry):
+            to_z, first, second = n // 16, (n // 4) % 4, n % 4
+            chip = jnp.where(core == 0, first * 4 + second, second * 4 + first) * 4 + to_z
+            mine = turned[pl.ds((chip * 2 + core) * (2 * K + 1), 2 * K), :]
+            give[n] = (mine + other[chip].astype(F32)).astype(BF)
+            return carry
+
+        lax.fori_loop(0, 64, pair_sum, 0)
+        for d in range(1, 4):
+            weight_z(d).start()
 
     @pl.when(back == STEPS - 1)
     def _():
@@ -881,6 +881,23 @@
     )(rows, seg, wz, pg)
 
 
+def finish_kernel(w_ref, p_ref, r_ref, wout_ref, pout_ref, rout_ref):
+    wout_ref[...] = w_ref[...]
+    pout_ref[...] = p_ref[...]
+    rout_ref[...] = r_ref[...]
+
+
+def finish(*results):
+    whole = pl.BlockSpec(memory_space=pltpu.VMEM)
+    return pl.pallas_call(
+        finish_kernel,
+        in_specs=[whole] * 3,
+        out_specs=[whole] * 3,
+        out_shape=[jax.ShapeDtypeStruct(a.shape, a.dtype) for a in results],
+        name="finish",
+    )(*results)
+
+
 def turn_features(a):
     rest = a.shape[1:]
     return a.reshape((-1, 8, 2) + rest).swapaxes(1, 2).reshape(a.shape)
@@ -889,7 +906,7 @@
 def on_device(pooled, projection, out_weight, cotangent, segments):
     own = turn_features(out_weight.reshape(-1, K, H)).swapaxes(0, 1)
     pg, rows, wz, seg = main(pooled, projection.T, own, segments.T, cotangent)
-    weight_grad, pg, row_grad = sums(rows, seg, wz, pg)
+    weight_grad, pg, row_grad = finish(*sums(rows, seg, wz, pg))
     return (weight_grad, pg.T, row_grad.T)
 
 

time: 199 us -> 190 us (0.955)
  local copies, waits for them, and re-layouts: 7.17 us -> 2 us
  Pallas kernels: 191 us -> 186 us
    pallas_call x1, Pallas kernels: 139 us -> 133 us  [main(): pl.pallas_call(main_kernel, grid=(2 * STEPS,), in_specs=[pl.BlockSpec((RO...]
    unnamed x3 -> x0, local copies, waits for them, and re-layouts: 5.17 us -> none
    pallas_call x0 -> x1, Pallas kernels: none -> 2.19 us  [finish(): pl.pallas_call(finish_kernel, in_specs=[whole] * 3, out_specs=[whole] * 3...]
where the time goes in v8:
time: 190 us; the launch traced here: 189 us
  Pallas kernels  186 us (98%)
  local copies, waits for them, and re-layouts  2 us (1%)
    pallas_call x1, Pallas kernels, main(): pl.pallas_call(main_kernel, grid=(2 * STEPS,), in_specs=[pl.BlockSpec((RO...  133 us
    pallas_call x1, Pallas kernels, sums(): pl.pallas_call(sums_kernel, in_specs=[any_space, whole, whole, whole], ou...  51.1 us

profile of v8, /device:TPU:0, one launch (start us, length us, event | category | flops | bytes accessed | tf_op | source)
XLA Modules:
  0.0 188.8 jit_solution(16951574460331045148)
XLA Ops:
  0.6 2.0 %copy.10 = bf16[1,8,2,96,128]{4,1,2,3,0:T(8,128)(2,1)} copy(bf16[1,8,2,96,128]{4,3,2,1,0:T(8,128)(2,1)} %bitcast.12) | data formatting | bytes 786432 | tf_op jit(solution)/shard_map/reshape;reshape | solution.py:903
  2.6 132.9 %main.1 = (f32[96,256]{1,0:T(8,128)}, bf16[16,1024,384]{2,1,0:T(8,128)(2,1)}, bf16[16,192,128]{2,1,0:T(8,128)(2,1)}, s32[16,2,1024]{2,1,0:T(2,128)}) custom-call(bf16[128,49152]{1,0:T(8,128)(2,1)} %x_ref.1, bf16[96,256]{1,0:T(8,128)(2,1)} %bitcast.17, bf16[96,16,128]{2,1,0:T(8,128)(2,1)} %bitcast.13, s32[2,16384]{1,0:T(2,128)} %bitcast.15, ...), custom_call_target="tpu_custom_call" | custom-call | flops 10871635968 | bytes 60000000 | tf_op jit(solution)/shard_map/main/pallas_call | solution.py:531
  135.5 51.1 %sums.1 = (f32[192,128]{1,0:T(8,128)}, f32[96,256]{1,0:T(8,128)}, f32[192,1024]{1,0:T(8,128)}) custom-call(bf16[16,1024,384]{2,1,0:T(8,128)(2,1)} %get-tuple-element.13.rows_ref, s32[16,2,1024]{2,1,0:T(2,128)} %get-tuple-element.14.seg_ref, bf16[16,192,128]{2,1,0:T(8,128)(2,1)} %get-tuple-element.15.wz_ref, f32[96,256]{1,0:T(8,128)} %get-tuple-element.16.pg_ref), custom_call_target="tpu_custom_call" | custom-call | flops 17179869184 | bytes 30000000 | tf_op jit(solution)/shard_map/sums/pallas_call | solution.py:835
  186.6 2.2 %finish.1 = (f32[192,128]{1,0:T(8,128)}, f32[96,256]{1,0:T(8,128)}, f32[192,1024]{1,0:T(8,128)}) custom-call(f32[192,128]{1,0:T(8,128)} %get-tuple-element.17.w_ref, f32[96,256]{1,0:T(8,128)} %get-tuple-element.18.p_ref, f32[192,1024]{1,0:T(8,128)} %get-tuple-element.19.r_ref), custom_call_target="tpu_custom_call" | custom-call | tf_op jit(solution)/shard_map/finish/pallas_call | solution.py:892

commit v9 on v8

--- a/solution.py
+++ b/solution.py
@@ -761,19 +761,21 @@
     s3 = start(w_copies(wz_ref, w3_in, 0, at_u, u, 4))
     tables(1)
     tables(2)
+    total_b(1)
     pv[v] = gathered(pu, u, 0, at_u)
     p1 = start(spread(pv, v, 1, at_v))
     for copy in s3:
         copy.wait_recv()
     add_four(wz_ref.at[pl.ds(u * 4, 4)], w3_in.at[0], w3_in.at[1], w3_in.at[2], w4, 1)
     s4 = start(w_copies(w4, w4_in, 1, at_v, v, 1))
-    total_b(1)
     tables(3)
+    total_b(2)
     pz[z] = gathered(pv, v, 1, at_v)
     p2 = start(spread(pz, z, 2, at_z))
-    total_b(2)
     tables(0)
     total_b(3)
+    for dv in ORDER:
+        total_a(dv)
     pc[core] = gathered(pz, z, 2, at_z)
     p3 = remote(pc.at[core], pc.at[core], p_send.at[3, 0], p_recv.at[3, 0], sibling)
     p3.start()
@@ -781,8 +783,6 @@
         copy.wait_recv()
     total = w4[v].astype(F32) + w4_in[0, 0].astype(F32)
     wout_ref[...] = total + (w4_in[1, 0].astype(F32) + w4_in[2, 0].astype(F32))
-    for dv in ORDER:
-        total_a(dv)
     total_b(0)
     remote(pc.at[1 - core], pc.at[1 - core], p_send.at[3, 0], p_recv.at[3, 0], sibling).wait_recv()
     pout_ref[...] = lax.dot_general(

time: 190 us -> 190 us (level)
  no operation moved by 1% of the time
where the time goes in v9:
time: 190 us; the launch traced here: 189 us
  Pallas kernels  186 us (98%)
  local copies, waits for them, and re-layouts  2 us (1%)
    pallas_call x1, Pallas kernels, main(): pl.pallas_call(main_kernel, grid=(2 * STEPS,), in_specs=[pl.BlockSpec((RO...  133 us
    pallas_call x1, Pallas kernels, sums(): pl.pallas_call(sums_kernel, in_specs=[any_space, whole, whole, whole], ou...  51.2 us

profile of v9, /device:TPU:0, one launch (start us, length us, event | category | flops | bytes accessed | tf_op | source)
XLA Modules:
  0.0 188.9 jit_solution(1410003952579107596)
XLA Ops:
  0.6 2.0 %copy.10 = bf16[1,8,2,96,128]{4,1,2,3,0:T(8,128)(2,1)} copy(bf16[1,8,2,96,128]{4,3,2,1,0:T(8,128)(2,1)} %bitcast.12) | data formatting | bytes 786432 | tf_op jit(solution)/shard_map/reshape;reshape | solution.py:903
  2.6 132.9 %main.1 = (f32[96,256]{1,0:T(8,128)}, bf16[16,1024,384]{2,1,0:T(8,128)(2,1)}, bf16[16,192,128]{2,1,0:T(8,128)(2,1)}, s32[16,2,1024]{2,1,0:T(2,128)}) custom-call(bf16[128,49152]{1,0:T(8,128)(2,1)} %x_ref.1, bf16[96,256]{1,0:T(8,128)(2,1)} %bitcast.17, bf16[96,16,128]{2,1,0:T(8,128)(2,1)} %bitcast.13, s32[2,16384]{1,0:T(2,128)} %bitcast.15, ...), custom_call_target="tpu_custom_call" | custom-call | flops 10871635968 | bytes 60000000 | tf_op jit(solution)/shard_map/main/pallas_call | solution.py:531
  135.5 51.2 %sums.1 = (f32[192,128]{1,0:T(8,128)}, f32[96,256]{1,0:T(8,128)}, f32[192,1024]{1,0:T(8,128)}) custom-call(bf16[16,1024,384]{2,1,0:T(8,128)(2,1)} %get-tuple-element.13.rows_ref, s32[16,2,1024]{2,1,0:T(2,128)} %get-tuple-element.14.seg_ref, bf16[16,192,128]{2,1,0:T(8,128)(2,1)} %get-tuple-element.15.wz_ref, f32[96,256]{1,0:T(8,128)} %get-tuple-element.16.pg_ref), custom_call_target="tpu_custom_call" | custom-call | flops 17179869184 | bytes 30000000 | tf_op jit(solution)/shard_map/sums/pallas_call | solution.py:835
  186.7 2.2 %finish.1 = (f32[192,128]{1,0:T(8,128)}, f32[96,256]{1,0:T(8,128)}, f32[192,1024]{1,0:T(8,128)}) custom-call(f32[192,128]{1,0:T(8,128)} %get-tuple-element.17.w_ref, f32[96,256]{1,0:T(8,128)} %get-tuple-element.18.p_ref, f32[192,1024]{1,0:T(8,128)} %get-tuple-element.19.r_ref), custom_call_target="tpu_custom_call" | custom-call | tf_op jit(solution)/shard_map/finish/pallas_call | solution.py:892
